TPU v7x, 1024 devices: a whole 4x4x32 slice. The times are simulated.
1024 devices in a mesh: slab: 32 (over z), chan: 16 (over x_hi, y, core), pipe: 2 (over x_lo).
Axes of the slice: x: 4 (x_hi: 2, x_lo: 2; x = x_hi * 2 + x_lo), y: 4, z: 32, core: 2. Of those that a mesh axis runs over, the one named last changes fastest.
Arguments:
- features: bfloat16 [2, 3, 64, 512, 128], P('pipe', None, 'slab', 'chan'), may hold values from -6 to 6
- taps: bfloat16 [2, 3, 512], P('pipe', None, 'chan'), may hold values from -3 to 3
- kern: bfloat16 [2, 512, 9, 512], P('pipe'), may hold values from -0.09375 to 0.09375
- proj: bfloat16 [2, 512, 16], P('pipe'), may hold values from -0.5 to 0.5
Outputs:
- section_out: bfloat16 [2, 3, 64, 512, 128], P('pipe', None, 'slab', 'chan')
- conv_grad: float32 [2, 512, 9, 512], P('pipe', 'slab', None, 'chan')
All inputs are finite; a program needn't handle non-finite values.
Results may differ from a plain program's by a relative error of at most 0.015.
Values may be sent and summed in bfloat16 or wider, within the bound.
No kernel may reach another device: no remote copies, remote signals or barrier semaphores. Data moves between devices by JAX's collectives and lax.ppermute only.
A program may use at most 32 MiB of HBM per device.

v0:
```python
import math

import jax
import jax.numpy as jnp
from jax import lax
from jax.sharding import PartitionSpec as P


def padded_2(block, sides, width):
    for axis, dim in sides:
        count = lax.axis_size(axis)
        forward = [(i, i + 1) for i in range(count - 1)]
        backward = [(target, source) for source, target in forward]
        low = lax.ppermute(
            lax.slice_in_dim(block, block.shape[dim] - width, None, axis=dim), axis, forward
        )
        high = lax.ppermute(lax.slice_in_dim(block, 0, width, axis=dim), axis, backward)
        block = jnp.concatenate([low, block, high], axis=dim)
    return block


def partner(value, axis, bit):
    mask = 2**bit
    pairs = [(source, source ^ mask) for source in range(lax.axis_size(axis))]
    return lax.ppermute(value, axis, pairs)


def squash(summed):
    sigma = jax.nn.sigmoid(summed)
    return sigma * (1.0 + summed * (1.0 - sigma))


def delayed(values, lag):
    padded = jnp.pad(values, ((lag, 0), (0, 0), (0, 0), (0, 0)))
    return padded[: values.shape[0]]


def advanced(values, lag):
    padded = jnp.pad(values, ((0, lag), (0, 0), (0, 0), (0, 0)))
    return padded[lag:]


def collect(values):
    return lax.all_gather(values, "chan", axis=2, tiled=True)


def spread(values):
    return collect(padded_2(values, (("slab", 1),), 1))


def handoff(values):
    return partner(values, "pipe", 0)


def convolve(gathered, out_cols):
    tile_rows = gathered.shape[1] - 2
    columns = gathered.shape[3]
    padded = jnp.pad(gathered, ((0, 0), (0, 0), (0, 0), (1, 1)))
    total = jnp.zeros((gathered.shape[0], tile_rows, out_cols.shape[2], columns), jnp.float32)
    for row_tap in range(3):
        for col_tap in range(3):
            window = padded[:, row_tap : row_tap + tile_rows, :, col_tap : col_tap + columns]
            total = total + jnp.einsum(
                "frcw,co->frow",
                window,
                out_cols[:, 3 * row_tap + col_tap, :],
                preferred_element_type=jnp.float32,
            )
    return total


def adjoint(gathered, in_rows):
    tile_rows = gathered.shape[1] - 2
    columns = gathered.shape[3]
    padded = jnp.pad(gathered, ((0, 0), (0, 0), (0, 0), (1, 1)))
    total = jnp.zeros((gathered.shape[0], tile_rows, in_rows.shape[0], columns), jnp.float32)
    for row_tap in range(3):
        for col_tap in range(3):
            window = padded[
                :, 2 - row_tap : 2 - row_tap + tile_rows, :, 2 - col_tap : 2 - col_tap + columns
            ]
            total = total + jnp.einsum(
                "frow,co->frcw",
                window,
                in_rows[:, 3 * row_tap + col_tap, :],
                preferred_element_type=jnp.float32,
            )
    return total


def latent(output, full_proj):
    summed = jnp.einsum(
        "frcw,cl->frlw", collect(output), full_proj, preferred_element_type=jnp.float32
    )
    return summed.astype(jnp.bfloat16)


def expand(latent_in, own_proj):
    return jnp.einsum(
        "frlw,cl->frcw", latent_in, own_proj, preferred_element_type=jnp.float32
    ).astype(jnp.bfloat16)


def mix_frames(inputs32, history_one, history_two, depth_taps):
    total = depth_taps[0][None, None, :, None] * inputs32
    total = total + depth_taps[1][None, None, :, None] * history_one
    total = total + depth_taps[2][None, None, :, None] * history_two
    return total.astype(jnp.bfloat16)


def finish(inputs32, gathered, out_cols):
    summed = convolve(gathered, out_cols)
    output = (inputs32 + jax.nn.silu(summed)).astype(jnp.bfloat16)
    return (gathered, summed, output)


def run_section(inputs, history_one, history_two, depth_taps, out_cols):
    inputs32 = inputs.astype(jnp.float32)
    mixed = mix_frames(inputs32, history_one, history_two, depth_taps)
    return finish(inputs32, spread(mixed), out_cols)


def on_device(features, taps, kern, proj):
    section_index = lax.axis_index("pipe")
    encoder_side = section_index == 0
    chan_part = features.shape[3]
    offset = lax.axis_index("chan") * chan_part
    weights = kern[0]
    out_cols = lax.dynamic_slice_in_dim(weights, offset, chan_part, 2)
    in_rows = lax.dynamic_slice_in_dim(weights, offset, chan_part, 0)
    full_proj = proj[0]
    own_proj = lax.dynamic_slice_in_dim(full_proj, offset, chan_part, 0)
    depth_taps = taps[0].astype(jnp.float32)
    source = features[0]
    frames = source.shape[0]
    tile_rows = source.shape[1]
    columns = source.shape[3]
    cot_scale = 1.0 / math.sqrt(frames * tile_rows * lax.axis_size("slab") * columns)
    source32 = source.astype(jnp.float32)
    gathered_a, summed_a, output_a = run_section(
        source, delayed(source32, 1), delayed(source32, 2), depth_taps, out_cols
    )
    latent_in = handoff(latent(output_a, full_proj))
    second = expand(latent_in, own_proj)
    second32 = second.astype(jnp.float32)
    gathered_b, summed_b, output_b = run_section(
        second, delayed(second32, 1), delayed(second32, 2), depth_taps, out_cols
    )
    gathered = jnp.where(encoder_side, gathered_a, gathered_b)
    summed = jnp.where(encoder_side, summed_a, summed_b)
    output = jnp.where(encoder_side, output_a, output_b)
    cotangent = source.astype(jnp.float32) * cot_scale
    slope = squash(summed)
    grad_b = (cotangent * slope).astype(jnp.bfloat16)
    back = adjoint(spread(grad_b), in_rows)
    spread_back = (
        depth_taps[0][None, None, :, None] * back
        + depth_taps[1][None, None, :, None] * advanced(back, 1)
        + depth_taps[2][None, None, :, None] * advanced(back, 2)
    )
    grad_in = (cotangent + spread_back).astype(jnp.bfloat16)
    latent_back = handoff(latent(grad_in, full_proj))
    grad_out_a = jnp.einsum(
        "frlw,cl->frcw", latent_back, own_proj, preferred_element_type=jnp.float32
    )
    grad_a = (grad_out_a * slope).astype(jnp.bfloat16)
    grad_sum = jnp.where(encoder_side, grad_a, grad_b)
    padded = jnp.pad(gathered, ((0, 0), (0, 0), (0, 0), (1, 1)))
    pieces = []
    for row_tap in range(3):
        for col_tap in range(3):
            window = padded[:, row_tap : row_tap + tile_rows, :, col_tap : col_tap + columns]
            pieces.append(
                jnp.einsum("frcw,frow->co", window, grad_sum, preferred_element_type=jnp.float32)
            )
    kernel_share = lax.psum_scatter(
        jnp.stack(pieces, axis=1), "slab", scatter_dimension=0, tiled=True
    )
    return (output[None], kernel_share[None])


def solution(mesh):
    placed = (
        P("pipe", None, "slab", "chan", None),
        P("pipe", None, "chan"),
        P("pipe", None, None, None),
        P("pipe", None, None),
    )
    return jax.shard_map(
        on_device,
        mesh=mesh,
        in_specs=placed,
        out_specs=(P("pipe", None, "slab", "chan", None), P("pipe", "slab", None, "chan")),
        check_vma=False,
    )
```

profile of v0, /device:TPU:2, one launch (start us, length us, event | category | flops | bytes accessed | tf_op | source)
XLA Modules:
  0.0 519.2 jit_solution(13160860603940867608)
XLA Ops:
  7.2 0.8 bitcast_convert_fusion
  8.0 0.7 convert_element_type.73
  8.8 1.3 collective-permute-start.1
  10.1 4.5 collective-permute-start
  14.7 1.5 collective-permute-done
  16.2 0.6 pad_maximum_fusion
  16.9 1.7 constant_dynamic-slice_fusion
  18.6 0.4 copy.8
  19.0 86.9 %all-gather.4.cloned.1.call-done = bf16[3,4,512,128]{3,2,1,0:T(8,128)(2,1)} async-done(((bf16[3,4,32,128]{3,2,1,0:T(8,128)(2,1)}), bf16[3,4,512,128]{3,2,1,0:T(8,128)(2,1)}) %all-gather.4.cloned.1.call-update) | async-done | bytes 1572880 | tf_op jit(solution)/shard_map/all_gather | solution.py:44
  105.9 1.5 fusion.29
  107.4 1.5 fusion.32
  108.9 0.4 convolution_add_fusion.20
  109.3 0.4 convolution_add_fusion.19
  109.7 0.2 convolution_add_fusion.18
  110.0 0.4 convolution_add_fusion.17
  110.4 0.4 convolution_add_fusion.16
  111.2 1.0 add_convert_fusion.1
  112.2 23.7 %all_gather.16 = bf16[3,2,512,128]{3,2,1,0:T(8,128)(2,1)S(1)} all-gather(bf16[3,2,32,128]{3,2,1,0:T(8,128)(2,1)S(1)} %get-tuple-element.15), channel_id=1, replica_groups=mesh['slab'=32,'chan'=16,'pipe'=2] {'chan'}, dimensions={2}, use_global_device_ids=true | all-gather | bytes 835584 | tf_op jit(solution)/shard_map/all_gather | solution.py:44
  136.1 3.4 collective-permute-start.2
  139.5 2.3 collective-permute-done.2
  141.8 0.3 fusion.6
  142.2 1.3 collective-permute-start.4
  143.5 4.5 collective-permute-start.3
  148.1 1.5 collective-permute-done.3
  149.6 0.6 pad_maximum_fusion.1
  150.3 80.0 %all-gather.6.cloned.1.call-done = bf16[3,4,512,128]{3,2,1,0:T(8,128)(2,1)} async-done(((bf16[3,4,32,128]{3,2,1,0:T(8,128)(2,1)}), bf16[3,4,512,128]{3,2,1,0:T(8,128)(2,1)}) %all-gather.6.cloned.1.call-update) | async-done | bytes 1572880 | tf_op jit(solution)/shard_map/all_gather | solution.py:44
  230.3 1.5 fusion.25
  231.8 1.5 fusion.34
  233.3 0.4 convolution_add_fusion.13
  233.7 0.4 convolution_add_fusion.12
  234.4 0.4 convolution_add_fusion.10
  234.8 0.4 convolution_add_fusion.9
  235.7 1.0 multiply_convert_fusion
  236.8 1.3 collective-permute-start.6
  238.1 4.5 collective-permute-start.5
  242.6 1.5 collective-permute-done.5
  244.1 0.6 pad_maximum_fusion.2
  244.8 1.0 dynamic-slice_bitcast_fusion
  245.8 81.0 %all-gather.8.cloned.1.call-done = bf16[3,4,512,128]{3,2,1,0:T(8,128)(2,1)} async-done(((bf16[3,4,32,128]{3,2,1,0:T(8,128)(2,1)}), bf16[3,4,512,128]{3,2,1,0:T(8,128)(2,1)}) %all-gather.8.cloned.1.call-update) | async-done | bytes 1572880 | tf_op jit(solution)/shard_map/all_gather | solution.py:44
  326.9 1.5 fusion.21
  328.4 1.5 fusion.36
  329.9 0.4 convolution_add_fusion.6
  330.3 0.4 convolution_add_fusion.5
  331.0 0.4 convolution_add_fusion.3
  331.4 0.4 convolution_add_fusion.2
  332.1 0.4 fusion.1
  332.7 23.7 %all_gather.19 = bf16[3,2,512,128]{3,2,1,0:T(8,128)(2,1)S(1)} all-gather(bf16[3,2,32,128]{3,2,1,0:T(8,128)(2,1)S(1)} %fusion.49), channel_id=1, replica_groups=mesh['slab'=32,'chan'=16,'pipe'=2] {'chan'}, dimensions={2}, use_global_device_ids=true | all-gather | bytes 835584 | tf_op jit(solution)/shard_map/all_gather | solution.py:44
  356.6 3.7 collective-permute-start.7
  360.5 2.0 collective-permute-done.7
  362.5 0.3 fusion.16
  362.8 0.4 fusion.15
  363.2 0.3 fusion.9
  363.5 0.4 fusion.14
  364.0 0.4 fusion.13
  364.4 0.3 fusion.8
  364.8 0.4 fusion.12
  365.2 0.4 fusion.11
  365.6 0.3 fusion.7
  366.0 0.4 fusion.10
  366.4 3.7 copy.9
  370.1 0.8 copy-done.8
  370.9 0.7 select_bitcast_fusion
  371.6 139.5 %reduce-scatter.2.cloned.1.call-done = f32[16,9,32]{2,1,0:T(8,128)} async-done(((f32[512,9,32]{2,1,0:T(8,128)}), f32[16,9,32]{2,1,0:T(8,128)}) %reduce-scatter.2.cloned.1.call-update) | async-done | bytes 18448 | tf_op jit(solution)/shard_map/reduce_scatter | solution.py:176
  511.1 1.6 copy.10
  (61 shorter events, 3.0 us)
Async XLA Ops:
  7.2 128.7 %copy-start = (bf16[1,512,16]{1,2,0:T(8,128)(2,1)S(1)}, bf16[1,512,16]{1,2,0:T(8,128)(2,1)}, u32[]{:S(2)}) copy-start(bf16[1,512,16]{1,2,0:T(8,128)(2,1)} %param.7) | copy-start | bytes 49156
  7.2 98.7 %all-gather.4.cloned.1.call-start = ((), (), s32[]{:S(2)}) async-start(), calls=%async_computation.1 | async-start | bytes 1671168 | tf_op jit(solution)/shard_map/all_gather | solution.py:44
  8.7 133.4 %copy-start.12 = (f32[32]{0:T(128)}, f32[32]{0:T(128)S(1)}, u32[]{:S(2)}) copy-start(f32[32]{0:T(128)S(1)} %get-tuple-element.12) | copy-start | bytes 388
  8.7 133.4 %copy-start.14 = (f32[32]{0:T(128)}, f32[32]{0:T(128)S(1)}, u32[]{:S(2)}) copy-start(f32[32]{0:T(128)S(1)} %get-tuple-element.13) | copy-start | bytes 388
  8.7 133.4 %copy-start.16 = (f32[32]{0:T(128)}, f32[32]{0:T(128)S(1)}, u32[]{:S(2)}) copy-start(f32[32]{0:T(128)S(1)} %get-tuple-element.14) | copy-start | bytes 388
  8.8 5.9 %collective-permute-start.1 = (bf16[3,1,32,128]{3,2,1,0:T(8,128)(2,1)S(1)}, bf16[3,1,32,128]{3,2,1,0:T(8,128)(2,1)S(1)}, u32[]{:S(2)}, u32[]{:S(2)}) collective-permute-start(bf16[3,1,32,128]{3,2,1,0:T(8,128)(2,1)S(1)} %get-tuple-element.11), channel_id=1, source_target_pairs={{32,0},{64,32},{96,64},{128,96},{160,128},{192,160},{224,192},{256... | collective-permute-start | bytes 73736 | tf_op jit(solution)/shard_map/ppermute | solution.py:17
  10.1 6.1 %collective-permute-start = (bf16[3,1,32,128]{3,2,1,0:T(8,128)(2,1)S(1)}, bf16[3,1,32,128]{3,2,1,0:T(8,128)(2,1)S(1)}, u32[]{:S(2)}, u32[]{:S(2)}) collective-permute-start(bf16[3,1,32,128]{3,2,1,0:T(8,128)(2,1)S(1)} %get-tuple-element.10), channel_id=1, source_target_pairs={{0,32},{32,64},{64,96},{96,128},{128,160},{160,192},{192,224},{224... | collective-permute-start | bytes 73736 | tf_op jit(solution)/shard_map/ppermute | solution.py:14
  16.9 213.4 %all-gather.6.cloned.1.call-start = ((), (), s32[]{:S(2)}) async-start(), calls=%async_computation.2 | async-start | bytes 1671168 | tf_op jit(solution)/shard_map/all_gather | solution.py:44
  105.9 3.0 copy-start.2
  110.4 0.8 copy-start.4
  112.2 27.3 %copy-start.7 = (bf16[3,2,32,128]{3,2,1,0:T(8,128)(2,1)}, bf16[3,2,32,128]{3,2,1,0:T(8,128)(2,1)S(1)}, u32[]{:S(2)}) copy-start(bf16[3,2,32,128]{3,2,1,0:T(8,128)(2,1)S(1)} %get-tuple-element.15) | copy-start | bytes 147460
  136.1 5.7 %collective-permute-start.2 = (bf16[3,2,16,128]{3,2,1,0:T(8,128)(2,1)S(1)}, bf16[3,2,16,128]{3,2,1,0:T(8,128)(2,1)S(1)}, u32[]{:S(2)}, u32[]{:S(2)}) collective-permute-start(bf16[3,2,16,128]{3,2,1,0:T(8,128)(2,1)S(1)} %fusion.17), channel_id=1, source_target_pairs={{0,1},{1,0},{2,3},{3,2},{4,5},{5,4},{6,7},{7,6},{8,9},{9,8},{10,11... | collective-permute-start | bytes 73736 | tf_op jit(solution)/shard_map/ppermute | solution.py:25
  142.2 5.9 %collective-permute-start.4 = (bf16[3,1,32,128]{3,2,1,0:T(8,128)(2,1)S(1)}, bf16[3,1,32,128]{3,2,1,0:T(8,128)(2,1)S(1)}, u32[]{:S(2)}, u32[]{:S(2)}) collective-permute-start(bf16[3,1,32,128]{3,2,1,0:T(8,128)(2,1)S(1)} %get-tuple-element.9), channel_id=1, source_target_pairs={{32,0},{64,32},{96,64},{128,96},{160,128},{192,160},{224,192},{256... | collective-permute-start | bytes 73736 | tf_op jit(solution)/shard_map/ppermute | solution.py:17
  143.5 6.1 %collective-permute-start.3 = (bf16[3,1,32,128]{3,2,1,0:T(8,128)(2,1)S(1)}, bf16[3,1,32,128]{3,2,1,0:T(8,128)(2,1)S(1)}, u32[]{:S(2)}, u32[]{:S(2)}) collective-permute-start(bf16[3,1,32,128]{3,2,1,0:T(8,128)(2,1)S(1)} %get-tuple-element.8), channel_id=1, source_target_pairs={{0,32},{32,64},{64,96},{96,128},{128,160},{160,192},{192,224},{224... | collective-permute-start | bytes 73736 | tf_op jit(solution)/shard_map/ppermute | solution.py:14
  150.3 176.6 %all-gather.8.cloned.1.call-start = ((), (), s32[]{:S(2)}) async-start(), calls=%async_computation.3 | async-start | bytes 1671168 | tf_op jit(solution)/shard_map/all_gather | solution.py:44
  230.3 3.0 copy-start.1
  234.8 0.8 copy-start.5
  234.8 0.9 copy-start.10
  236.8 5.8 %collective-permute-start.6 = (bf16[3,1,32,128]{3,2,1,0:T(8,128)(2,1)S(1)}, bf16[3,1,32,128]{3,2,1,0:T(8,128)(2,1)S(1)}, u32[]{:S(2)}, u32[]{:S(2)}) collective-permute-start(bf16[3,1,32,128]{3,2,1,0:T(8,128)(2,1)S(1)} %get-tuple-element.7), channel_id=1, source_target_pairs={{32,0},{64,32},{96,64},{128,96},{160,128},{192,160},{224,192},{256... | collective-permute-start | bytes 73736 | tf_op jit(solution)/shard_map/ppermute | solution.py:17
  238.1 6.1 %collective-permute-start.5 = (bf16[3,1,32,128]{3,2,1,0:T(8,128)(2,1)S(1)}, bf16[3,1,32,128]{3,2,1,0:T(8,128)(2,1)S(1)}, u32[]{:S(2)}, u32[]{:S(2)}) collective-permute-start(bf16[3,1,32,128]{3,2,1,0:T(8,128)(2,1)S(1)} %get-tuple-element.6), channel_id=1, source_target_pairs={{0,32},{32,64},{64,96},{96,128},{128,160},{160,192},{192,224},{224... | collective-permute-start | bytes 73736 | tf_op jit(solution)/shard_map/ppermute | solution.py:14
  244.8 266.3 %reduce-scatter.2.cloned.1.call-start = ((), (), s32[]{:S(2)}) async-start(), calls=%async_computation.4 | async-start | bytes 4325376 | tf_op jit(solution)/shard_map/reduce_scatter | solution.py:176
  326.9 3.0 copy-start.3
  331.8 0.8 copy-start.6
  331.8 0.8 copy-start.13
  331.8 0.8 copy-start.15
  331.8 0.8 copy-start.17
  356.6 5.9 %copy-start.9 = (f32[3,2,32,128]{3,2,1,0:T(8,128)S(1)}, f32[3,2,32,128]{3,2,1,0:T(8,128)}, u32[]{:S(2)}) copy-start(f32[3,2,32,128]{3,2,1,0:T(8,128)} %get-tuple-element.18) | copy-start | bytes 294916
  356.6 5.9 %copy-start.11 = (f32[3,2,32,128]{3,2,1,0:T(8,128)S(1)}, f32[3,2,32,128]{3,2,1,0:T(8,128)}, u32[]{:S(2)}) copy-start(f32[3,2,32,128]{3,2,1,0:T(8,128)} %get-tuple-element.16) | copy-start | bytes 294916
  356.6 5.8 %collective-permute-start.7 = (bf16[3,2,16,128]{3,2,1,0:T(8,128)(2,1)S(1)}, bf16[3,2,16,128]{3,2,1,0:T(8,128)(2,1)S(1)}, u32[]{:S(2)}, u32[]{:S(2)}) collective-permute-start(bf16[3,2,16,128]{3,2,1,0:T(8,128)(2,1)S(1)} %fusion.18), channel_id=1, source_target_pairs={{0,1},{1,0},{2,3},{3,2},{4,5},{5,4},{6,7},{7,6},{8,9},{9,8},{10,11... | collective-permute-start | bytes 73736 | tf_op jit(solution)/shard_map/ppermute | solution.py:25
  370.1 0.8 copy-start.8
Sparse Core Ops, SparseCore 0:
  17.0 88.8 all-gather.3
  150.4 79.8 all-gather.5
  244.9 81.9 all-gather.7
  370.3 140.7 reduce-scatter.1
where the time goes:
time: 520 us; the launch traced here: 519 us
  waiting for transfers between devices  396 us (76%)
  blocking collectives  47.4 us (9%)
  starting transfers between devices  24.8 us (5%)
  matrix products  22.5 us (4%)
  between operations  14.1 us (3%)
  local copies, waits for them, and re-layouts  9.66 us (2%)
    all_gather x3, waiting for transfers between devices, collect(): return lax.all_gather(values, 'chan', axis=2, tiled=True)  248 us
    reduce_scatter x1, waiting for transfers between devices, on_device(): lax.psum_scatter(jnp.stack(pieces, axis=1), 'slab', scatter_dimension=0,...  139 us
    all_gather x2, blocking collectives, collect(): return lax.all_gather(values, 'chan', axis=2, tiled=True)  47.4 us
    ppermute x3, starting transfers between devices, padded_2(): lax.ppermute(lax.slice_in_dim(block, block.shape[dim] - width, None, axis...  13.6 us
    dot_general x18, matrix products, convolve(): jnp.einsum('frcw,co->frow', window, out_cols[:, 3 * row_tap + col_tap, :]...  12.4 us
  transfers between devices with their start and end apart: 12, of which 9 were waited for; matrix products, arithmetic and copies ran while one was open for 1% of the time, Pallas kernels for 0%

commit v1 on v0

v1 whole, which is shorter than its diff:
```python
import functools
import math

import jax
import jax.numpy as jnp
from jax import lax
from jax.experimental import pallas as pl
from jax.experimental.pallas import tpu as pltpu
from jax.sharding import PartitionSpec as P

F32 = jnp.float32
BF16 = jnp.bfloat16
VMEM = pl.BlockSpec(memory_space=pltpu.VMEM)
SMEM = pl.BlockSpec(memory_space=pltpu.SMEM)
PARAMS = pltpu.CompilerParams(vmem_limit_bytes=40 * 1024 * 1024)


def dot(a, b):
    return lax.dot_general(a, b, (((1,), (0,)), ((), ())), preferred_element_type=F32)


def dot_nt(a, b):
    return lax.dot_general(a, b, (((1,), (1,)), ((), ())), preferred_element_type=F32)


def shifted(values, step):
    if step == 0:
        return values
    columns = values.shape[-1]
    lane = lax.broadcasted_iota(jnp.int32, values.shape, values.ndim - 1)
    edge = columns - 1 if step == 1 else 0
    moved = pltpu.roll(values, columns - 1 if step == 1 else 1, values.ndim - 1)
    return jnp.where(lane == edge, 0.0, moved)


def logistic(summed):
    return 1.0 / (1.0 + jnp.exp(-summed))


def tap_blocks(rows, outs):
    sums = []
    for row in range(len(rows) - 2):
        total = None
        for col_tap in range(3):
            part = None
            for row_tap in range(3):
                at = (3 * row_tap + col_tap) * outs
                block = rows[row + row_tap][at : at + outs]
                part = block if part is None else part + block
            part = shifted(part, col_tap - 1)
            total = part if total is None else total + part
        sums.append(total)
    return sums


def mix_kernel(tile, low, high, depth, extra, sent, own):
    frames, rows = tile.shape[0], tile.shape[1]
    peers = sent.shape[0]

    def row_of(frame, row):
        if row == 0:
            return low[frame, 0].astype(F32)
        if row == rows + 1:
            return high[frame, 0].astype(F32)
        return tile[frame, row - 1].astype(F32)

    weights = [depth[:, lag : lag + 1] for lag in range(3)]
    for row in range(rows + 2):
        history = [row_of(frame, row) for frame in range(frames)]
        for frame in range(frames):
            total = weights[0] * history[frame]
            for lag in range(1, 3):
                if frame >= lag:
                    total = total + weights[lag] * history[frame - lag]
            own[frame, row] = total.astype(BF16)
    for frame in range(frames):
        for row in range(rows + 2):
            block = own[frame, row]
            for peer in range(peers):
                sent[peer, frame * (rows + 2) + row] = block
    for peer in range(peers):
        sent[peer, frames * (rows + 2)] = extra[...]


def encode_kernel(place, gathered, taps_out, tile, proj_back, out, slope, sent, combo, combo_t):
    frames, rows, outs, columns = tile.shape
    peers, _, part, _ = gathered.shape
    channels = peers * part
    latents = proj_back.shape[0]

    @pl.when(place[0] == 0)
    def _():
        weights = taps_out[...]
        for frame in range(frames):
            products = []
            for row in range(0, rows + 2, 2):
                at = frame * (rows + 2) + row
                pair = jnp.concatenate(
                    [gathered[:, at + k].reshape(channels, columns) for k in range(2)], axis=1
                )
                both = dot(weights, pair)
                products += [both[:, :columns], both[:, columns:]]
            for row, summed in enumerate(tap_blocks(products, outs)):
                sigma = logistic(summed)
                result = (tile[frame, row].astype(F32) + summed * sigma).astype(BF16)
                out[frame, row] = result
                slope[frame, row] = sigma * (1.0 + summed * (1.0 - sigma))
                latent = dot(proj_back[...], result).astype(BF16)
                for peer in range(sent.shape[0]):
                    sent[peer, frame, row] = latent

    @pl.when(place[0] == 1)
    def _():
        factors = gathered[:, frames * (rows + 2)].reshape(channels, columns)
        merged = dot(taps_out[...], factors)
        combo[...] = merged.astype(BF16)
        combo_t[...] = merged.T.astype(BF16)
        sent[...] = jnp.zeros_like(sent)


def stacked(z_rows, frame, frames):
    blank = jnp.zeros_like(z_rows[0])
    return jnp.concatenate(
        [z_rows[frame - lag] if frame >= lag else blank for lag in range(3)], axis=0
    )


def z_row(low, mid, high, frame, row):
    rows = mid.shape[1]
    if row < rows:
        return low[frame, row]
    if row < 2 * rows:
        return mid[frame, row - rows]
    return high[frame, row - 2 * rows]


def decode_kernel(
    scale, place, low, mid, high, own, combo, combo_t, proj_out, proj_back, encoded, out, grad, sent
):
    frames, rows, latents, columns = mid.shape
    outs = own.shape[2]
    deep = 3 * latents

    @pl.when(place[0] == 0)
    def _():
        out[...] = encoded[...]
        sent[...] = jnp.zeros_like(sent)

    @pl.when(place[0] == 1)
    def _():
        weights = combo[...][:, :deep]
        back = combo_t[...][:deep]
        reach = 3 * rows
        mixed = []
        for frame in range(frames):
            wide = jnp.concatenate(
                [
                    stacked(
                        [z_row(low, mid, high, f, row) for f in range(frames)], frame, frames
                    )
                    for row in range(reach)
                ],
                axis=1,
            )
            both = dot(weights, wide)
            products = [both[:, row * columns : (row + 1) * columns] for row in range(reach)]
            moved = []
            for row, summed in enumerate(tap_blocks(products, outs)):
                sigma = logistic(summed)
                slope = sigma * (1.0 + summed * (1.0 - sigma))
                cotangent = own[frame, row].astype(F32) * scale
                slanted = (cotangent * slope).astype(BF16)
                moved.append(
                    [shifted(slanted.astype(F32), 1 - b).astype(BF16) for b in range(3)]
                )
                if 1 <= row <= rows:
                    lifted = dot(proj_out[...], mid[frame, row - 1]).astype(BF16)
                    out[frame, row - 1] = (lifted.astype(F32) + summed * sigma).astype(BF16)
                    grad[frame, row - 1] = slanted
            columns_of = [
                jnp.concatenate(
                    [moved[row - a + 2][b] for a in range(3) for b in range(3)], axis=0
                )
                for row in range(rows)
            ]
            mixed.append(dot(back, jnp.concatenate(columns_of, axis=1)))
        for frame in range(frames):
            total = mixed[frame][:latents]
            for lag in range(1, 3):
                if frame + lag < frames:
                    total = total + mixed[frame + lag][lag * latents : (lag + 1) * latents]
            for row in range(rows):
                direct = dot(proj_back[...], own[frame, row + 1]) * scale
                latent = (direct + total[:, row * columns : (row + 1) * columns]).astype(BF16)
                for peer in range(sent.shape[0]):
                    sent[peer, frame, row] = latent


def grad_kernel(
    place, arrived, slope, gathered, grad, low, mid, high, proj_out, send, keep, scratch
):
    frames, rows, outs, columns = slope.shape
    peers, _, part, _ = gathered.shape
    channels = peers * part
    latents = mid.shape[2]
    pairs, _, share, _ = scratch.shape
    halves = arrived.shape[0] // peers

    def window(grads, frame, row):
        blank = jnp.zeros((outs, columns), BF16)
        return jnp.concatenate(
            [
                grads[frame][row - a][b] if 0 <= row - a < rows else blank
                for a in range(3)
                for b in range(3)
            ],
            axis=0,
        )

    def steps(value):
        return [shifted(value.astype(F32), 1 - b).astype(BF16) for b in range(3)]

    def store(total):
        for pair in range(pairs):
            for side in range(2):
                at = (2 * pair + side) * share
                scratch[pair, side] = total[at : at + share]

    @pl.when(place[0] == 0)
    def _():
        grads = []
        for frame in range(frames):
            grads.append([])
            for row in range(rows):
                latent = arrived[1, frame, row].astype(F32)
                for peer in range(1, peers):
                    latent = latent + arrived[halves * peer + 1, frame, row].astype(F32)
                value = dot(proj_out[...], latent.astype(BF16)) * slope[frame, row]
                grads[-1].append(steps(value.astype(BF16)))
        spots = [(frame, row) for frame in range(frames) for row in range(rows + 2)]
        left = jnp.concatenate(
            [
                gathered[:, frame * (rows + 2) + row].reshape(channels, columns)
                for frame, row in spots
            ],
            axis=1,
        )
        right = jnp.concatenate([window(grads, frame, row) for frame, row in spots], axis=1)
        store(dot_nt(left, right))

    @pl.when(place[0] == 1)
    def _():
        grads = [[steps(grad[frame, row]) for row in range(rows)] for frame in range(frames)]
        spots = [(frame, row) for frame in range(frames) for row in range(rows + 2)]
        left = jnp.concatenate(
            [
                stacked(
                    [z_row(low, mid, high, f, row + 1) for f in range(frames)], frame, frames
                )
                for frame, row in spots
            ],
            axis=1,
        )
        right = jnp.concatenate([window(grads, frame, row) for frame, row in spots], axis=1)
        inner = dot_nt(left, right).astype(BF16)
        factors = gathered[:, frames * (rows + 2)].reshape(channels, columns)
        store(dot(factors[:, : 3 * latents], inner))

    mine = place[1]
    keep[...] = scratch[:, mine]
    send[...] = scratch[:, 1 - mine].astype(BF16)


def call(kernel, shapes, specs, scratch=()):
    return pl.pallas_call(
        kernel,
        out_shape=shapes,
        in_specs=specs,
        out_specs=jax.tree.map(lambda _: VMEM, shapes),
        scratch_shapes=list(scratch),
        compiler_params=PARAMS,
    )


def both_ways(low_side, high_side, axis):
    count = lax.axis_size(axis)
    forward = [(i, i + 1) for i in range(count - 1)]
    backward = [(i + 1, i) for i in range(count - 1)]
    return lax.ppermute(high_side, axis, forward), lax.ppermute(low_side, axis, backward)


def on_device(features, taps, kern, proj):
    shape = jax.ShapeDtypeStruct
    pipe = lax.axis_index("pipe")
    slab = lax.axis_index("slab")
    peers = lax.axis_size("chan")
    slabs = lax.axis_size("slab")
    both = peers * lax.axis_size("pipe")
    tile = features[0]
    frames, rows, part, columns = tile.shape
    channels, latents = proj.shape[1], proj.shape[2]
    share = channels // slabs
    offset = lax.axis_index("chan") * part
    place = jnp.stack([pipe, slab % 2]).astype(jnp.int32)
    scale = 1.0 / math.sqrt(frames * rows * slabs * columns)

    above, below = both_ways(tile[:, :1], tile[:, rows - 1 :], "slab")
    proj_out = lax.dynamic_slice_in_dim(proj[0], offset, part, 0)
    proj_back = proj_out.T
    depth = taps[0].astype(F32).T
    factors = (depth[:, :, None] * proj_out.astype(F32)[:, None, :]).reshape(part, 3 * latents)
    extra = jnp.pad(factors.astype(BF16), ((0, 0), (0, columns - 3 * latents)))
    depth = jnp.where(pipe == 0, depth, jnp.array([[1.0, 0.0, 0.0]], F32))
    sent, own = call(
        mix_kernel,
        (
            shape((peers, frames * (rows + 2) + 1, part, columns), BF16),
            shape((frames, rows + 2, part, columns), BF16),
        ),
        [VMEM] * 5,
    )(tile, above, below, depth, extra)
    gathered = lax.all_to_all(sent, "chan", 0, 0)

    out_cols = lax.dynamic_slice_in_dim(kern[0], offset, part, 2)
    taps_out = out_cols.transpose(1, 2, 0).reshape(9 * part, channels)
    tile_shape = (frames, rows, part, columns)
    latent_shape = (both, frames, rows, latents, columns)
    encoded, slope, sent, combo, combo_t = call(
        encode_kernel,
        (
            shape(tile_shape, BF16),
            shape(tile_shape, F32),
            shape(latent_shape, BF16),
            shape((9 * part, columns), BF16),
            shape((columns, 9 * part), BF16),
        ),
        [SMEM] + [VMEM] * 4,
    )(place, gathered, taps_out, tile, proj_back)

    arrived = lax.all_to_all(sent, ("chan", "pipe"), 0, 0)
    arrived = arrived.reshape((peers, 2) + latent_shape[1:])
    mid = jnp.sum(arrived[:, 0].astype(F32), axis=0).astype(BF16)
    low, high = both_ways(mid, mid, "slab")
    out, grad, sent = call(
        functools.partial(decode_kernel, scale),
        (shape(tile_shape, BF16), shape(tile_shape, BF16), shape(latent_shape, BF16)),
        [SMEM] + [VMEM] * 9,
    )(place, low, mid, high, own, combo, combo_t, proj_out, proj_back, encoded)

    arrived = lax.all_to_all(sent, ("chan", "pipe"), 0, 0)
    pairs = slabs // 2
    send, keep = call(
        grad_kernel,
        (shape((pairs, share, 9 * part), BF16), shape((pairs, share, 9 * part), F32)),
        [SMEM] + [VMEM] * 8,
        [pltpu.VMEM((pairs, 2, share, 9 * part), F32)],
    )(place, arrived, slope, gathered, grad, low, mid, high, proj_out)
    got = lax.ppermute(send, "slab", [(i, i ^ 1) for i in range(slabs)])
    halved = (keep + got.astype(F32)).astype(BF16)
    groups = [[2 * p + q for p in range(pairs)] for q in range(2)]
    pieces = lax.all_to_all(halved, "slab", 0, 0, axis_index_groups=groups)
    total = jnp.sum(pieces.astype(F32), axis=0).reshape(share, 9, part)
    return out[None], total[None]


def solution(mesh):
    placed = (
        P("pipe", None, "slab", "chan", None),
        P("pipe", None, "chan"),
        P("pipe", None, None, None),
        P("pipe", None, None),
    )
    return jax.shard_map(
        on_device,
        mesh=mesh,
        in_specs=placed,
        out_specs=(P("pipe", None, "slab", "chan", None), P("pipe", "slab", None, "chan")),
        check_vma=False,
    )
```

time: 520 us -> 164 us (0.32)
  the two profiles are of different devices: /device:TPU:2 before, /device:TPU:100 now
where the time goes in v1:
time: 164 us
  blocking collectives  93.5 us (57%)
  waiting for transfers between devices  34.1 us (21%)
  starting transfers between devices  22.3 us (14%)
  Pallas kernels  6.49 us (4%)
  local copies, waits for them, and re-layouts  4.92 us (3%)
    all_to_all x1, blocking collectives, on_device(): pieces = lax.all_to_all(halved, 'slab', 0, 0, axis_index_groups=groups)  54.7 us
    all_to_all x2, blocking collectives, on_device(): arrived = lax.all_to_all(sent, ('chan', 'pipe'), 0, 0)  38.8 us
    all_to_all x1, waiting for transfers between devices, on_device(): gathered = lax.all_to_all(sent, 'chan', 0, 0)  20.3 us
    ppermute x2, starting transfers between devices, both_ways(): lax.ppermute(high_side, axis, forward)  7.64 us
    all_to_all x1, starting transfers between devices, on_device(): gathered = lax.all_to_all(sent, 'chan', 0, 0)  7.45 us
    ppermute x1, waiting for transfers between devices, on_device(): got = lax.ppermute(send, 'slab', [(i, i ^ 1) for i in range(slabs)])  6.95 us
    ppermute x2, waiting for transfers between devices, both_ways(): lax.ppermute(low_side, axis, backward)  6.79 us
    ppermute x2, starting transfers between devices, both_ways(): lax.ppermute(low_side, axis, backward)  5.15 us
  transfers between devices with their start and end apart: 6, of which 4 were waited for; matrix products, arithmetic and copies ran while one was open for 2% of the time, Pallas kernels for 0%

profile of v1, /device:TPU:100, one launch (start us, length us, event | category | flops | bytes accessed | tf_op | source)
XLA Modules:
  0.0 163.6 jit_solution(1558251758845231095)
XLA Ops:
  0.6 0.0 copy-start
  0.6 0.8 fusion
  1.4 5.0 %collective-permute-start = (bf16[3,1,32,128]{3,2,1,0:T(8,128)(2,1)S(1)}, bf16[3,1,32,128]{3,2,1,0:T(8,128)(2,1)S(1)}, u32[]{:S(2)}, u32[]{:S(2)}) collective-permute-start(bf16[3,1,32,128]{3,2,1,0:T(8,128)(2,1)S(1)} %get-tuple-element.29), channel_id=1, source_target_pairs={{0,32},{32,64},{64,96},{96,128},{128,160},{160,192},{192,224},{224... | collective-permute-start | bytes 73736 | tf_op jit(solution)/shard_map/ppermute | solution.py:289
  6.4 1.9 %collective-permute-start.1 = (bf16[3,1,32,128]{3,2,1,0:T(8,128)(2,1)S(1)}, bf16[3,1,32,128]{3,2,1,0:T(8,128)(2,1)S(1)}, u32[]{:S(2)}, u32[]{:S(2)}) collective-permute-start(bf16[3,1,32,128]{3,2,1,0:T(8,128)(2,1)S(1)} %get-tuple-element.28), channel_id=1, source_target_pairs={{32,0},{64,32},{96,64},{128,96},{160,128},{192,160},{224,192},{256... | collective-permute-start | bytes 73736 | tf_op jit(solution)/shard_map/ppermute | solution.py:289
  8.4 0.0 copy-done
  8.4 0.1 constant_dynamic-slice_fusion.1
  8.5 0.1 copy.13
  8.6 0.1 copy.14
  8.6 0.7 bitcast_convert_fusion
  9.3 0.1 copy.11
  9.4 0.1 copy.12
  9.5 0.7 broadcast_select_fusion.depth
  10.2 0.1 copy.15
  10.3 0.0 collective-permute-done.low
  10.3 3.1 %collective-permute-done.1.high = bf16[3,1,32,128]{3,2,1,0:T(8,128)(2,1)S(1)} collective-permute-done((bf16[3,1,32,128]{3,2,1,0:T(8,128)(2,1)S(1)}, bf16[3,1,32,128]{3,2,1,0:T(8,128)(2,1)S(1)}, u32[]{:S(2)}, u32[]{:S(2)}) %collective-permute-start.1) | collective-permute-done | bytes 24608 | tf_op jit(solution)/shard_map/ppermute | solution.py:289
  13.4 0.0 copy-start.1
  13.4 0.8 copy-done.1
  14.2 1.5 shard_map.68
  15.7 7.5 %all-to-all-start = ((bf16[16,13,32,128]{3,2,1,0:T(8,128)(2,1)}), bf16[16,13,32,128]{3,2,1,0:T(8,128)(2,1)S(1)}, u32[]{:S(2)}, u32[]{:S(2)}) async-start(bf16[16,13,32,128]{3,2,1,0:T(8,128)(2,1)} %get-tuple-element.14), calls=%async_computation | async-start | bytes 3407872 | tf_op jit(solution)/shard_map/all_to_all | solution.py:322
  23.1 0.0 copy-start.2
  23.1 1.7 %constant_dynamic-slice_fusion = bf16[1,512,9,32]{3,1,2,0:T(8,128)(2,1)S(1)} fusion(bf16[1,512,9,512]{3,1,2,0:T(8,128)(2,1)} %param.7, s32[]{:T(128)S(6)} %select_n.22), kind=kLoop, calls=%fused_computation.7 | loop fusion | bytes 589828 | tf_op jit(solution)/shard_map/dynamic_slice | solution.py:324
  24.8 0.4 copy.21
  25.2 0.1 pad_add_fusion.place
  25.3 0.1 fusion.1.proj_back
  25.3 20.3 %all-to-all-done.gathered = bf16[16,13,32,128]{3,2,1,0:T(8,128)(2,1)S(1)} async-done(((bf16[16,13,32,128]{3,2,1,0:T(8,128)(2,1)}), bf16[16,13,32,128]{3,2,1,0:T(8,128)(2,1)S(1)}, u32[]{:S(2)}, u32[]{:S(2)}) %all-to-all-start) | async-done | bytes 1703968 | tf_op jit(solution)/shard_map/all_to_all | solution.py:322
  45.7 0.0 copy-done.2
  45.7 1.9 %shard_map.69 = (bf16[3,2,32,128]{3,2,1,0:T(8,128)(2,1)S(1)}, f32[3,2,32,128]{3,2,1,0:T(8,128)S(1)}, bf16[32,3,2,16,128]{4,3,2,1,0:T(8,128)(2,1)S(1)}, bf16[288,128]{1,0:T(8,128)(2,1)S(1)}, bf16[128,288]{1,0:T(8,128)(2,1)S(1)}) custom-call(s32[2]{0:T(128)S(1)} %pad_add_fusion.place, bf16[16,13,32,128]{3,2,1,0:T(8,128)(2,1)S(1)} %all-to-all-done.gathered, ...), custom_call_target="tpu_custom_call" | custom-call | tf_op jit(solution)/shard_map/pallas_call | solution.py:328
  47.6 19.5 %all_to_all.20 = bf16[32,3,2,16,128]{4,3,2,1,0:T(8,128)(2,1)S(1)} all-to-all(bf16[32,3,2,16,128]{4,3,2,1,0:T(8,128)(2,1)S(1)} %get-tuple-element.15), channel_id=1, replica_groups=mesh['slab'=32,'chan'=16,'pipe'=2] {'chan','pipe'}, dimensions={0} | all-to-all | bytes 1572864 | tf_op jit(solution)/shard_map/all_to_all | solution.py:340
  67.1 0.1 slice_reduce_fusion.mid
  67.1 2.6 %collective-permute-start.2 = (bf16[3,2,16,128]{3,2,1,0:T(8,128)(2,1)S(1)}, bf16[3,2,16,128]{3,2,1,0:T(8,128)(2,1)S(1)}, u32[]{:S(2)}, u32[]{:S(2)}) collective-permute-start(bf16[3,2,16,128]{3,2,1,0:T(8,128)(2,1)S(1)} %slice_reduce_fusion.mid), channel_id=1, source_target_pairs={{0,32},{32,64},{64,96},{96,128},{128,160},{160,192},{192,224},{224... | collective-permute-start | bytes 73736 | tf_op jit(solution)/shard_map/ppermute | solution.py:289
  69.8 3.2 %collective-permute-start.3 = (bf16[3,2,16,128]{3,2,1,0:T(8,128)(2,1)S(1)}, bf16[3,2,16,128]{3,2,1,0:T(8,128)(2,1)S(1)}, u32[]{:S(2)}, u32[]{:S(2)}) collective-permute-start(bf16[3,2,16,128]{3,2,1,0:T(8,128)(2,1)S(1)} %slice_reduce_fusion.mid), channel_id=1, source_target_pairs={{32,0},{64,32},{96,64},{128,96},{160,128},{192,160},{224,192},{256... | collective-permute-start | bytes 73736 | tf_op jit(solution)/shard_map/ppermute | solution.py:289
  73.0 0.0 collective-permute-done.2.low
  73.0 3.7 %collective-permute-done.3.high = bf16[3,2,16,128]{3,2,1,0:T(8,128)(2,1)S(1)} collective-permute-done((bf16[3,2,16,128]{3,2,1,0:T(8,128)(2,1)S(1)}, bf16[3,2,16,128]{3,2,1,0:T(8,128)(2,1)S(1)}, u32[]{:S(2)}, u32[]{:S(2)}) %collective-permute-start.3) | collective-permute-done | bytes 24608 | tf_op jit(solution)/shard_map/ppermute | solution.py:289
  76.7 1.3 shard_map.70
  78.0 19.3 %all_to_all.21.arrived = bf16[32,3,2,16,128]{4,3,2,1,0:T(8,128)(2,1)S(1)} all-to-all(bf16[32,3,2,16,128]{4,3,2,1,0:T(8,128)(2,1)S(1)} %get-tuple-element.21), channel_id=1, replica_groups=mesh['slab'=32,'chan'=16,'pipe'=2] {'chan','pipe'}, dimensions={0} | all-to-all | bytes 1572864 | tf_op jit(solution)/shard_map/all_to_all | solution.py:350
  97.3 1.8 %shard_map.71 = (bf16[16,16,288]{2,1,0:T(8,128)(2,1)S(1)}, f32[16,16,288]{2,1,0:T(8,128)S(1)}) custom-call(s32[2]{0:T(128)S(1)} %pad_add_fusion.place, bf16[32,3,2,16,128]{4,3,2,1,0:T(8,128)(2,1)S(1)} %all_to_all.21.arrived, f32[3,2,32,128]{3,2,1,0:T(8,128)S(1)} %get-tuple-element.22.slope, bf16[16,13,32,128]{3,2,1,0:T(8,128)(2,1)S(1)} %all-to-all-done.gathered, ...), custom_call_target="tpu_custom_call" | custom-call | tf_op jit(solution)/shard_map/pallas_call | solution.py:352
  99.1 2.0 %collective-permute-start.4 = (bf16[16,16,288]{2,1,0:T(8,128)(2,1)S(1)}, bf16[16,16,288]{2,1,0:T(8,128)(2,1)S(1)}, u32[]{:S(2)}, u32[]{:S(2)}) collective-permute-start(bf16[16,16,288]{2,1,0:T(8,128)(2,1)S(1)} %get-tuple-element.25), channel_id=1, source_target_pairs={{0,32},{32,0},{64,96},{96,64},{128,160},{160,128},{192,224},{224,1... | collective-permute-start | bytes 442376 | tf_op jit(solution)/shard_map/ppermute | solution.py:358
  101.1 7.0 %collective-permute-done.4 = bf16[16,16,288]{2,1,0:T(8,128)(2,1)S(1)} collective-permute-done((bf16[16,16,288]{2,1,0:T(8,128)(2,1)S(1)}, bf16[16,16,288]{2,1,0:T(8,128)(2,1)S(1)}, u32[]{:S(2)}, u32[]{:S(2)}) %collective-permute-start.4) | collective-permute-done | bytes 147488 | tf_op jit(solution)/shard_map/ppermute | solution.py:358
  108.1 0.1 add_convert_fusion
  108.1 54.7 %all_to_all.22 = bf16[16,16,288]{2,1,0:T(8,128)(2,1)S(1)} all-to-all(bf16[16,16,288]{2,1,0:T(8,128)(2,1)S(1)} %add_convert_fusion), channel_id=1, replica_groups={{0,64,128,192,256,320,384,448,512,576,640,704,768,832,896,960},{32,96,1..., dimensions={0} | all-to-all | bytes 294912 | tf_op jit(solution)/shard_map/all_to_all | solution.py:361
  162.9 0.1 broadcast_in_dim_reshape.3
  162.9 0.7 copy.19
  (4 shorter events, 0.1 us)
Async XLA Ops:
  0.6 7.8 %copy-start = (bf16[1,512,16]{1,2,0:T(8,128)(2,1)S(1)}, bf16[1,512,16]{1,2,0:T(8,128)(2,1)}, u32[]{:S(2)}) copy-start(bf16[1,512,16]{1,2,0:T(8,128)(2,1)} %param.8) | copy-start | bytes 49156
  1.4 8.9 %collective-permute-start = (bf16[3,1,32,128]{3,2,1,0:T(8,128)(2,1)S(1)}, bf16[3,1,32,128]{3,2,1,0:T(8,128)(2,1)S(1)}, u32[]{:S(2)}, u32[]{:S(2)}) collective-permute-start(bf16[3,1,32,128]{3,2,1,0:T(8,128)(2,1)S(1)} %get-tuple-element.29), channel_id=1, source_target_pairs={{0,32},{32,64},{64,96},{96,128},{128,160},{160,192},{192,224},{224... | collective-permute-start | bytes 73736 | tf_op jit(solution)/shard_map/ppermute | solution.py:289
  6.4 6.9 %collective-permute-start.1 = (bf16[3,1,32,128]{3,2,1,0:T(8,128)(2,1)S(1)}, bf16[3,1,32,128]{3,2,1,0:T(8,128)(2,1)S(1)}, u32[]{:S(2)}, u32[]{:S(2)}) collective-permute-start(bf16[3,1,32,128]{3,2,1,0:T(8,128)(2,1)S(1)} %get-tuple-element.28), channel_id=1, source_target_pairs={{32,0},{64,32},{96,64},{128,96},{160,128},{192,160},{224,192},{256... | collective-permute-start | bytes 73736 | tf_op jit(solution)/shard_map/ppermute | solution.py:289
  13.4 0.8 copy-start.1
  15.7 30.0 %all-to-all-start = ((bf16[16,13,32,128]{3,2,1,0:T(8,128)(2,1)}), bf16[16,13,32,128]{3,2,1,0:T(8,128)(2,1)S(1)}, u32[]{:S(2)}, u32[]{:S(2)}) async-start(bf16[16,13,32,128]{3,2,1,0:T(8,128)(2,1)} %get-tuple-element.14), calls=%async_computation | async-start | bytes 3407872 | tf_op jit(solution)/shard_map/all_to_all | solution.py:322
  23.1 22.5 %copy-start.2 = (bf16[1,3,2,32,128]{4,3,2,1,0:T(8,128)(2,1)S(1)}, bf16[1,3,2,32,128]{4,3,2,1,0:T(8,128)(2,1)}, u32[]{:S(2)}) copy-start(bf16[1,3,2,32,128]{4,3,2,1,0:T(8,128)(2,1)} %param.5) | copy-start | bytes 147460
  67.1 5.9 %collective-permute-start.2 = (bf16[3,2,16,128]{3,2,1,0:T(8,128)(2,1)S(1)}, bf16[3,2,16,128]{3,2,1,0:T(8,128)(2,1)S(1)}, u32[]{:S(2)}, u32[]{:S(2)}) collective-permute-start(bf16[3,2,16,128]{3,2,1,0:T(8,128)(2,1)S(1)} %slice_reduce_fusion.mid), channel_id=1, source_target_pairs={{0,32},{32,64},{64,96},{96,128},{128,160},{160,192},{192,224},{224... | collective-permute-start | bytes 73736 | tf_op jit(solution)/shard_map/ppermute | solution.py:289
  69.8 6.9 %collective-permute-start.3 = (bf16[3,2,16,128]{3,2,1,0:T(8,128)(2,1)S(1)}, bf16[3,2,16,128]{3,2,1,0:T(8,128)(2,1)S(1)}, u32[]{:S(2)}, u32[]{:S(2)}) collective-permute-start(bf16[3,2,16,128]{3,2,1,0:T(8,128)(2,1)S(1)} %slice_reduce_fusion.mid), channel_id=1, source_target_pairs={{32,0},{64,32},{96,64},{128,96},{160,128},{192,160},{224,192},{256... | collective-permute-start | bytes 73736 | tf_op jit(solution)/shard_map/ppermute | solution.py:289
  99.1 9.0 %collective-permute-start.4 = (bf16[16,16,288]{2,1,0:T(8,128)(2,1)S(1)}, bf16[16,16,288]{2,1,0:T(8,128)(2,1)S(1)}, u32[]{:S(2)}, u32[]{:S(2)}) collective-permute-start(bf16[16,16,288]{2,1,0:T(8,128)(2,1)S(1)} %get-tuple-element.25), channel_id=1, source_target_pairs={{0,32},{32,0},{64,96},{96,64},{128,160},{160,128},{192,224},{224,1... | collective-permute-start | bytes 442376 | tf_op jit(solution)/shard_map/ppermute | solution.py:358

commit v2 on v1

v2 whole, which is shorter than its diff:
```python
import functools
import math

import jax
import jax.numpy as jnp
from jax import lax
from jax.experimental import pallas as pl
from jax.experimental.pallas import tpu as pltpu
from jax.sharding import PartitionSpec as P

F32 = jnp.float32
BF16 = jnp.bfloat16
VMEM = pl.BlockSpec(memory_space=pltpu.VMEM)
SMEM = pl.BlockSpec(memory_space=pltpu.SMEM)
PARAMS = pltpu.CompilerParams(vmem_limit_bytes=40 * 1024 * 1024)


def dot(a, b):
    return lax.dot_general(a, b, (((1,), (0,)), ((), ())), preferred_element_type=F32)


def dot_nt(a, b):
    return lax.dot_general(a, b, (((1,), (1,)), ((), ())), preferred_element_type=F32)


def shifted(values, step):
    if step == 0:
        return values
    columns = values.shape[-1]
    lane = lax.broadcasted_iota(jnp.int32, values.shape, values.ndim - 1)
    edge = columns - 1 if step == 1 else 0
    moved = pltpu.roll(values, columns - 1 if step == 1 else 1, values.ndim - 1)
    return jnp.where(lane == edge, 0.0, moved)


def logistic(summed):
    return 1.0 / (1.0 + jnp.exp(-summed))


def tap_blocks(rows, outs):
    sums = []
    for row in range(len(rows) - 2):
        total = None
        for col_tap in range(3):
            part = None
            for row_tap in range(3):
                at = (3 * row_tap + col_tap) * outs
                block = rows[row + row_tap][at : at + outs]
                part = block if part is None else part + block
            part = shifted(part, col_tap - 1)
            total = part if total is None else total + part
        sums.append(total)
    return sums


def block_of(gathered, at, part):
    rows = pl.ds(pl.multiple_of(at * part, part), part)
    return gathered[:, rows].reshape(gathered.shape[0] * part, gathered.shape[2])


def mix_kernel(tile, low, high, depth, extra, proj_back, sent, own):
    frames, rows, part, _ = tile.shape
    peers, latents = sent.shape[0], proj_back.shape[0]
    splits = peers // (frames * rows)

    def row_of(frame, row):
        if row == 0:
            return low[frame, 0].astype(F32)
        if row == rows + 1:
            return high[frame, 0].astype(F32)
        return tile[frame, row - 1].astype(F32)

    weights = [depth[:, lag : lag + 1] for lag in range(3)]
    for row in range(rows + 2):
        history = [row_of(frame, row) for frame in range(frames)]
        for frame in range(frames):
            total = weights[0] * history[frame]
            for lag in range(1, 3):
                if frame >= lag:
                    total = total + weights[lag] * history[frame - lag]
            block = total.astype(BF16)
            own[frame, row] = block
            at = (frame * (rows + 2) + row) * part
            for peer in range(peers):
                sent[peer, at : at + part] = block
    at = frames * (rows + 2) * part
    for peer in range(peers):
        sent[peer, at : at + part] = extra[...]
        row, turn = peer // splits, peer % splits
        if row < frames * rows and turn == 0:
            direct = dot(proj_back[...], tile[row // rows, row % rows]).astype(BF16)
        else:
            direct = jnp.zeros((latents, tile.shape[3]), BF16)
        sent[peer, at + part : at + part + latents] = direct


def encode_kernel(
    place, gathered, taps_out, tile, proj_t, kern, out, slope, sent, combo, wide_t, wide, held, done
):
    frames, rows, outs, columns = tile.shape
    peers = gathered.shape[0]
    part = outs
    channels = peers * part
    latents = proj_t.shape[0]
    deep = 3 * latents
    span = held.shape[2]
    splits = channels // span
    row_at, turn = place[1] // splits, place[1] % splits
    active = row_at < frames * rows
    fetch = pltpu.make_async_copy(
        kern.at[:, :, pl.ds(pl.multiple_of(turn * span, span), span)], held, done
    )
    fetch.start()

    @pl.when(place[0] == 0)
    def _():
        weights = taps_out[...]
        for frame in range(frames):
            products = []
            for row in range(0, rows + 2, 2):
                at = frame * (rows + 2) + row
                pair = jnp.concatenate(
                    [block_of(gathered, at + k, part) for k in range(2)], axis=1
                )
                both = dot(weights, pair)
                products += [both[:, :columns], both[:, columns:]]
            for row, summed in enumerate(tap_blocks(products, outs)):
                sigma = logistic(summed)
                out[frame, row] = (tile[frame, row].astype(F32) + summed * sigma).astype(BF16)
                slope[frame, row] = sigma * (1.0 + summed * (1.0 - sigma))

    fetch.wait()

    @pl.when(jnp.logical_and(place[0] == 0, active))
    def _():
        base = (row_at // rows) * (rows + 2) + row_at % rows
        turned = [block_of(gathered, base + a, part).T for a in range(3)]
        summed = None
        for b in range(3):
            total = None
            for a in range(3):
                term = dot(turned[a], held[3 * a + b])
                total = term if total is None else total + term
            if b != 1:
                line = lax.broadcasted_iota(jnp.int32, total.shape, 0)
                edge = columns - 1 if b == 2 else 0
                moved = pltpu.roll(total, columns - 1 if b == 2 else 1, 0)
                total = jnp.where(line == edge, 0.0, moved)
            summed = total if summed is None else summed + total
        bent = (summed * logistic(summed)).astype(BF16)
        latent = dot_nt(pick(proj_t, turn, span), bent)
        at = (frames * (rows + 2) + 1) * part
        for peer in range(peers):
            latent = latent + gathered[peer, at : at + latents].astype(F32)
        latent = latent.astype(BF16)
        for peer in range(sent.shape[0]):
            sent[peer] = latent

    @pl.when(jnp.logical_or(place[0] == 1, jnp.logical_not(active)))
    def _():
        sent[...] = jnp.zeros_like(sent)

    @pl.when(place[0] == 1)
    def _():
        factors = block_of(gathered, frames * (rows + 2), part)
        combo[...] = dot(taps_out[...], factors).astype(BF16)
        factors_t = factors.astype(F32).T.astype(BF16)[:deep]
        for tap in range(9):
            wide_t[tap * deep : (tap + 1) * deep] = dot(factors_t, held[tap]).astype(BF16)
        wide[...] = wide_t[...].astype(F32).T.astype(BF16)


def pick(ref, turn, span):
    chosen = ref[:, :span]
    for at in range(1, ref.shape[1] // span):
        chosen = jnp.where(turn == at, ref[:, at * span : (at + 1) * span], chosen)
    return chosen


def stacked(z_rows, frame, frames):
    blank = jnp.zeros_like(z_rows[0])
    return jnp.concatenate(
        [z_rows[frame - lag] if frame >= lag else blank for lag in range(3)], axis=0
    )


def z_row(low, mid, high, frame, row):
    rows = mid.shape[1]
    if row < rows:
        return low[frame, row]
    if row < 2 * rows:
        return mid[frame, row - rows]
    return high[frame, row - 2 * rows]


def decode_kernel(
    scale, place, low, mid, high, own, combo, wide_t, wide, gathered, proj_out, proj_t, encoded,
    out, grad, sent, bank
):
    frames, rows, latents, columns = mid.shape
    outs = own.shape[2]
    part = outs
    deep = 3 * latents
    span = wide.shape[0]
    peers = gathered.shape[0]
    splits = peers * part // span
    row_at, turn = place[1] // splits, place[1] % splits
    active = row_at < frames * rows

    @pl.when(place[0] == 0)
    def _():
        out[...] = encoded[...]

    @pl.when(jnp.logical_or(place[0] == 0, jnp.logical_not(active)))
    def _():
        sent[...] = jnp.zeros_like(sent)

    @pl.when(place[0] == 1)
    def _():
        weights = combo[...][:, :deep]
        reach = range(1, 3 * rows - 1)
        for frame in range(frames):
            band = jnp.concatenate(
                [
                    stacked(
                        [z_row(low, mid, high, f, row) for f in range(frames)], frame, frames
                    )
                    for row in reach
                ],
                axis=1,
            )
            both = dot(weights, band)
            products = [both[:, i * columns : (i + 1) * columns] for i in range(len(reach))]
            for row, summed in enumerate(tap_blocks(products, outs)):
                sigma = logistic(summed)
                cotangent = own[frame, row + 1].astype(F32) * scale
                slope = sigma * (1.0 + summed * (1.0 - sigma))
                grad[frame, row] = (cotangent * slope).astype(BF16)
                lifted = dot(proj_out[...], mid[frame, row]).astype(BF16)
                out[frame, row] = (lifted.astype(F32) + summed * sigma).astype(BF16)

    @pl.when(jnp.logical_and(place[0] == 1, active))
    def _():
        bank[:, 0:2] = jnp.zeros((3, 2) + bank.shape[2:], BF16)
        for frame in range(frames):
            for row in range(3 * rows):
                value = z_row(low, mid, high, frame, row).astype(F32)
                for b in range(3):
                    bank[b, frame + 2, row] = shifted(value, b - 1).astype(BF16)
        frame_at, line = row_at // rows, row_at % rows
        first = turn * (span // part)

        def channel_rows(frame, row):
            at = pl.multiple_of((frame * (rows + 2) + row) * part, part)
            block = gathered[pl.ds(first, span // part), pl.ds(at, part)]
            return block.reshape(span, columns)

        columns_of = []
        for lag in range(3):
            source = jnp.minimum(frame_at + lag, frames - 1)
            for a in range(3):
                columns_of.append(
                    jnp.concatenate(
                        [
                            bank[tap % 3, source - back + 2, line - a + 2 + tap // 3]
                            for tap in range(9)
                            for back in range(3)
                        ],
                        axis=0,
                    )
                )
        summed = dot(wide[...], jnp.concatenate(columns_of, axis=1))
        slanted, weights = [], []
        for lag in range(3):
            source = jnp.minimum(frame_at + lag, frames - 1)
            factor = jnp.where(frame_at + lag < frames, scale, 0.0)
            for a in range(3):
                at = (3 * lag + a) * columns
                value = summed[:, at : at + columns]
                sigma = logistic(value)
                slope = sigma * (1.0 + value * (1.0 - sigma))
                cotangent = channel_rows(source, line - a + 2).astype(F32) * factor
                slanted.append((cotangent * slope).astype(BF16))
                weights.append(
                    jnp.concatenate(
                        [
                            wide_t[(3 * a + b) * deep + lag * latents :][:latents]
                            for b in range(3)
                        ],
                        axis=0,
                    )
                )
        mixed = dot(jnp.concatenate(weights, axis=1), jnp.concatenate(slanted, axis=0))
        latent = dot(pick(proj_t, turn, span), channel_rows(frame_at, line + 1)) * scale
        for b in range(3):
            latent = latent + shifted(mixed[b * latents : (b + 1) * latents], 1 - b)
        latent = latent.astype(BF16)
        for peer in range(sent.shape[0]):
            sent[peer] = latent


def grad_kernel(place, arrived, slope, gathered, grad, low, mid, high, proj_out, sent):
    frames, rows, outs, columns = slope.shape
    peers = gathered.shape[0]
    part = outs
    latents = mid.shape[2]
    near, far, share, _ = sent.shape
    splits = peers // (frames * rows)

    def window(grads, frame, row):
        blank = jnp.zeros((outs, columns), BF16)
        return jnp.concatenate(
            [
                grads[frame][row - a][b] if 0 <= row - a < rows else blank
                for a in range(3)
                for b in range(3)
            ],
            axis=0,
        )

    def steps(value):
        return [shifted(value.astype(F32), 1 - b).astype(BF16) for b in range(3)]

    def store(total):
        for i in range(far):
            for j in range(near):
                at = (near * i + j) * share
                sent[j, i] = total[at : at + share].astype(BF16)

    spots = [(frame, row) for frame in range(frames) for row in range(rows + 2)]

    @pl.when(place[0] == 0)
    def _():
        grads = []
        for frame in range(frames):
            grads.append([])
            for row in range(rows):
                at = (frame * rows + row) * splits
                latent = arrived[2 * at + 1].astype(F32)
                for turn in range(1, splits):
                    latent = latent + arrived[2 * (at + turn) + 1].astype(F32)
                value = dot(proj_out[...], latent.astype(BF16)) * slope[frame, row]
                grads[-1].append(steps(value.astype(BF16)))
        left = jnp.concatenate(
            [block_of(gathered, at, part) for at in range(len(spots))], axis=1
        )
        right = jnp.concatenate([window(grads, frame, row) for frame, row in spots], axis=1)
        store(dot_nt(left, right))

    @pl.when(place[0] == 1)
    def _():
        grads = [[steps(grad[frame, row]) for row in range(rows)] for frame in range(frames)]
        left = jnp.concatenate(
            [
                stacked(
                    [z_row(low, mid, high, f, row + 1) for f in range(frames)], frame, frames
                )
                for frame, row in spots
            ],
            axis=1,
        )
        right = jnp.concatenate([window(grads, frame, row) for frame, row in spots], axis=1)
        inner = dot_nt(left, right).astype(BF16)
        factors = block_of(gathered, len(spots), part)
        store(dot(factors[:, : 3 * latents], inner))


def call(kernel, shapes, specs, scratch=()):
    return pl.pallas_call(
        kernel,
        out_shape=shapes,
        in_specs=specs,
        out_specs=jax.tree.map(lambda _: VMEM, shapes),
        scratch_shapes=list(scratch),
        compiler_params=PARAMS,
    )


def both_ways(low_side, high_side, axis):
    count = lax.axis_size(axis)
    forward = [(i, i + 1) for i in range(count - 1)]
    backward = [(i + 1, i) for i in range(count - 1)]
    return lax.ppermute(high_side, axis, forward), lax.ppermute(low_side, axis, backward)


def on_device(features, taps, kern, proj):
    shape = jax.ShapeDtypeStruct
    pipe = lax.axis_index("pipe")
    slab = lax.axis_index("slab")
    peers = lax.axis_size("chan")
    slabs = lax.axis_size("slab")
    both = peers * lax.axis_size("pipe")
    tile = features[0]
    frames, rows, part, columns = tile.shape
    channels, latents = proj.shape[1], proj.shape[2]
    share = channels // slabs
    offset = lax.axis_index("chan") * part
    place = jnp.stack([pipe, lax.axis_index("chan")]).astype(jnp.int32)
    scale = 1.0 / math.sqrt(frames * rows * slabs * columns)
    splits = peers // (frames * rows)
    span = channels // splits

    above, below = both_ways(tile[:, :1], tile[:, rows - 1 :], "slab")
    proj_t = proj[0].T
    proj_out = lax.dynamic_slice_in_dim(proj[0], offset, part, 0)
    proj_back = proj_out.T
    depth = taps[0].astype(F32).T
    factors = (depth[:, :, None] * proj_out.astype(F32)[:, None, :]).reshape(part, 3 * latents)
    extra = jnp.pad(factors.astype(BF16), ((0, 0), (0, columns - 3 * latents)))
    depth = jnp.where(pipe == 0, depth, jnp.array([[1.0, 0.0, 0.0]], F32))
    height = (frames * (rows + 2) + 1) * part + latents
    sent, own = call(
        mix_kernel,
        (
            shape((peers, height, columns), BF16),
            shape((frames, rows + 2, part, columns), BF16),
        ),
        [VMEM] * 6,
    )(tile, above, below, depth, extra, proj_back)
    gathered = lax.all_to_all(sent, "chan", 0, 0)

    out_cols = lax.dynamic_slice_in_dim(kern[0], offset, part, 2)
    taps_out = out_cols.transpose(1, 2, 0).reshape(9 * part, channels)
    tile_shape = (frames, rows, part, columns)
    latent_shape = (both, latents, columns)
    terms = 27 * latents
    encoded, slope, sent, combo, wide_t, wide = call(
        encode_kernel,
        (
            shape(tile_shape, BF16),
            shape(tile_shape, F32),
            shape(latent_shape, BF16),
            shape((9 * part, columns), BF16),
            shape((terms, span), BF16),
            shape((span, terms), BF16),
        ),
        [SMEM] + [VMEM] * 4 + [pl.BlockSpec(memory_space=pl.ANY)],
        [pltpu.VMEM((9, channels, span), BF16), pltpu.SemaphoreType.DMA],
    )(place, gathered, taps_out, tile, proj_t, kern[0].transpose(1, 0, 2))

    arrived = lax.all_to_all(sent, ("chan", "pipe"), 0, 0)
    arrived = arrived.reshape(peers, 2, latents, columns)[: frames * rows * splits, 0]
    arrived = arrived.reshape(frames, rows, splits, latents, columns)
    mid = jnp.sum(arrived.astype(F32), axis=2).astype(BF16)
    low, high = both_ways(mid, mid, "slab")
    out, grad, sent = call(
        functools.partial(decode_kernel, scale),
        (shape(tile_shape, BF16), shape(tile_shape, BF16), shape(latent_shape, BF16)),
        [SMEM] + [VMEM] * 11,
        [pltpu.VMEM((3, frames + 2, 3 * rows, latents, columns), BF16)],
    )(
        place, low, mid, high, own, combo, wide_t, wide, gathered, proj_out, proj_t, encoded
    )

    arrived = lax.all_to_all(sent, ("chan", "pipe"), 0, 0)
    near = 4
    far = slabs // near
    sent = call(
        grad_kernel,
        shape((near, far, share, 9 * part), BF16),
        [SMEM] + [VMEM] * 8,
    )(place, arrived, slope, gathered, grad, low, mid, high, proj_out)
    groups = [[near * i + j for j in range(near)] for i in range(far)]
    pieces = lax.all_to_all(sent, "slab", 0, 0, axis_index_groups=groups)
    partial = jnp.sum(pieces.astype(F32), axis=0).astype(BF16)
    groups = [[near * i + j for i in range(far)] for j in range(near)]
    pieces = lax.all_to_all(partial, "slab", 0, 0, axis_index_groups=groups)
    total = jnp.sum(pieces.astype(F32), axis=0).reshape(share, 9, part)
    return out[None], total[None]


def solution(mesh):
    placed = (
        P("pipe", None, "slab", "chan", None),
        P("pipe", None, "chan"),
        P("pipe", None, None, None),
        P("pipe", None, None),
    )
    return jax.shard_map(
        on_device,
        mesh=mesh,
        in_specs=placed,
        out_specs=(P("pipe", None, "slab", "chan", None), P("pipe", "slab", None, "chan")),
        check_vma=False,
    )
```

time: 164 us -> 158 us (0.963)
  the two profiles are of different devices: /device:TPU:100 before, /device:TPU:8 now
where the time goes in v2:
time: 158 us
  blocking collectives  90.5 us (57%)
  starting transfers between devices  23.9 us (15%)
  waiting for transfers between devices  23.5 us (15%)
  local copies, waits for them, and re-layouts  10.9 us (7%)
  Pallas kernels  6.54 us (4%)
    all_to_all x1, blocking collectives, on_device(): pieces = lax.all_to_all(partial, 'slab', 0, 0, axis_index_groups=groups)  49.4 us
    all_to_all x2, blocking collectives, on_device(): arrived = lax.all_to_all(sent, ('chan', 'pipe'), 0, 0)  26.8 us
    all_to_all x1, waiting for transfers between devices, on_device(): gathered = lax.all_to_all(sent, 'chan', 0, 0)  18 us
    all_to_all x1, blocking collectives, on_device(): pieces = lax.all_to_all(sent, 'slab', 0, 0, axis_index_groups=groups)  14.3 us
    all_to_all x1, starting transfers between devices, on_device(): gathered = lax.all_to_all(sent, 'chan', 0, 0)  14.1 us
    ppermute x2, starting transfers between devices, both_ways(): lax.ppermute(high_side, axis, forward)  7.29 us
    unnamed x10, local copies, waits for them, and re-layouts  5.42 us
    ppermute x2, waiting for transfers between devices, both_ways(): lax.ppermute(low_side, axis, backward)  5.3 us
  transfers between devices with their start and end apart: 5, of which 4 were waited for; matrix products, arithmetic and copies ran while one was open for 5% of the time, Pallas kernels for 0%

profile of v2, /device:TPU:8, one launch (start us, length us, event | category | flops | bytes accessed | tf_op | source)
XLA Modules:
  0.0 157.7 jit_solution(8005933060021105968)
XLA Ops:
  0.6 0.8 fusion
  1.4 3.8 %collective-permute-start = (bf16[3,1,32,128]{3,2,1,0:T(8,128)(2,1)S(1)}, bf16[3,1,32,128]{3,2,1,0:T(8,128)(2,1)S(1)}, u32[]{:S(2)}, u32[]{:S(2)}) collective-permute-start(bf16[3,1,32,128]{3,2,1,0:T(8,128)(2,1)S(1)} %get-tuple-element.29), channel_id=1, source_target_pairs={{0,32},{32,64},{64,96},{96,128},{128,160},{160,192},{192,224},{224... | collective-permute-start | bytes 73736 | tf_op jit(solution)/shard_map/ppermute | solution.py:383
  5.2 1.3 collective-permute-start.1
  6.5 0.7 bitcast_convert_fusion
  7.2 0.1 copy.18
  7.3 0.8 constant_dynamic-slice_fusion.1
  8.1 0.1 copy.20
  8.2 0.1 copy.21
  8.2 0.1 copy.19
  8.3 0.7 broadcast_select_fusion.depth
  9.0 0.8 fusion.1.proj_back
  9.7 0.1 copy.22
  9.8 0.0 collective-permute-done.low
  9.9 1.1 collective-permute-done.1.high
  10.9 0.0 copy-start.1
  10.9 0.8 copy-done.1
  11.7 1.4 shard_map.68
  13.2 14.1 %all-to-all-start = ((bf16[16,432,128]{2,1,0:T(8,128)(2,1)}), bf16[16,432,128]{2,1,0:T(8,128)(2,1)S(1)}, u32[]{:S(2)}, u32[]{:S(2)}) async-start(bf16[16,432,128]{2,1,0:T(8,128)(2,1)} %get-tuple-element.13), calls=%async_computation | async-start | bytes 3538944 | tf_op jit(solution)/shard_map/all_to_all | solution.py:420
  27.2 0.0 copy-start.2
  27.3 0.0 copy-start.3
  27.3 2.7 %constant_dynamic-slice_fusion = bf16[1,512,9,32]{3,1,2,0:T(8,128)(2,1)} fusion(bf16[1,512,9,512]{3,1,2,0:T(8,128)(2,1)} %param.7, s32[]{:T(128)S(6)} %select_n.14), kind=kLoop, calls=%fused_computation.5 | loop fusion | bytes 589828 | tf_op jit(solution)/shard_map/dynamic_slice | solution.py:422
  30.0 1.6 %copy.27 = bf16[1,512,9,32]{1,3,2,0:T(8,128)(2,1)S(1)} copy(bf16[1,512,9,32]{3,1,2,0:T(8,128)(2,1)} %constant_dynamic-slice_fusion) | data formatting | bytes 589824
  31.6 0.1 pad_add_fusion.place
  31.7 18.0 %all-to-all-done.gathered = bf16[16,432,128]{2,1,0:T(8,128)(2,1)S(1)} async-done(((bf16[16,432,128]{2,1,0:T(8,128)(2,1)}), bf16[16,432,128]{2,1,0:T(8,128)(2,1)S(1)}, u32[]{:S(2)}, u32[]{:S(2)}) %all-to-all-start) | async-done | bytes 1769504 | tf_op jit(solution)/shard_map/all_to_all | solution.py:420
  49.7 0.0 copy-done.2
  49.7 0.0 copy-done.3
  49.7 0.0 copy-start
  49.7 2.3 %copy-done = bf16[1,512,9,512]{3,1,2,0:T(8,128)(2,1)S(1)} copy-done((bf16[1,512,9,512]{3,1,2,0:T(8,128)(2,1)S(1)}, bf16[1,512,9,512]{3,1,2,0:T(8,128)(2,1)}, u32[]{:S(2)}) %copy-start) | copy-done | bytes 4718616
  52.1 2.1 %shard_map.69 = (bf16[3,2,32,128]{3,2,1,0:T(8,128)(2,1)S(1)}, f32[3,2,32,128]{3,2,1,0:T(8,128)S(1)}, bf16[32,16,128]{2,1,0:T(8,128)(2,1)S(1)}, bf16[288,128]{1,0...) custom-call(s32[2]{0:T(128)S(1)} %pad_add_fusion.place, ...), custom_call_target="tpu_custom_call" | custom-call | tf_op jit(solution)/shard_map/pallas_call | solution.py:427
  54.2 14.5 %all_to_all.25 = bf16[32,16,128]{2,1,0:T(8,128)(2,1)S(1)} all-to-all(bf16[32,16,128]{2,1,0:T(8,128)(2,1)S(1)} %get-tuple-element.14), channel_id=1, replica_groups=mesh['slab'=32,'chan'=16,'pipe'=2] {'chan','pipe'}, dimensions={0} | all-to-all | bytes 262144 | tf_op jit(solution)/shard_map/all_to_all | solution.py:441
  68.7 3.5 %collective-permute-start.2 = (bf16[3,2,16,128]{3,2,1,0:T(8,128)(2,1)S(1)}, bf16[3,2,16,128]{3,2,1,0:T(8,128)(2,1)S(1)}, u32[]{:S(2)}, u32[]{:S(2)}) collective-permute-start(bf16[3,2,16,128]{3,2,1,0:T(8,128)(2,1)S(1)} %reduce_sum.33.mid), channel_id=1, source_target_pairs={{0,32},{32,64},{64,96},{96,128},{128,160},{160,192},{192,224},{224... | collective-permute-start | bytes 73736 | tf_op jit(solution)/shard_map/ppermute | solution.py:383
  72.2 1.3 collective-permute-start.3
  73.5 0.2 collective-permute-done.2.low
  73.7 4.2 %collective-permute-done.3.high = bf16[3,2,16,128]{3,2,1,0:T(8,128)(2,1)S(1)} collective-permute-done((bf16[3,2,16,128]{3,2,1,0:T(8,128)(2,1)S(1)}, bf16[3,2,16,128]{3,2,1,0:T(8,128)(2,1)S(1)}, u32[]{:S(2)}, u32[]{:S(2)}) %collective-permute-start.3) | collective-permute-done | bytes 24608 | tf_op jit(solution)/shard_map/ppermute | solution.py:383
  77.9 1.2 shard_map.70
  79.2 12.3 %all_to_all.26.arrived = bf16[32,16,128]{2,1,0:T(8,128)(2,1)S(1)} all-to-all(bf16[32,16,128]{2,1,0:T(8,128)(2,1)S(1)} %get-tuple-element.21), channel_id=1, replica_groups=mesh['slab'=32,'chan'=16,'pipe'=2] {'chan','pipe'}, dimensions={0} | all-to-all | bytes 262144 | tf_op jit(solution)/shard_map/all_to_all | solution.py:455
  91.4 1.7 %shard_map.71 = bf16[4,8,16,288]{3,2,1,0:T(8,128)(2,1)S(1)} custom-call(s32[2]{0:T(128)S(1)} %pad_add_fusion.place, bf16[32,16,128]{2,1,0:T(8,128)(2,1)S(1)} %all_to_all.26.arrived, f32[3,2,32,128]{3,2,1,0:T(8,128)S(1)} %get-tuple-element.22.slope, bf16[16,432,128]{2,1,0:T(8,128)(2,1)S(1)} %all-to-all-done.gathered, ...), custom_call_target="tpu_custom_call" | custom-call | tf_op jit(solution)/shard_map/pallas_call | solution.py:458
  93.2 14.3 %all_to_all.27 = bf16[4,8,16,288]{3,2,1,0:T(8,128)(2,1)S(1)} all-to-all(bf16[4,8,16,288]{3,2,1,0:T(8,128)(2,1)S(1)} %shard_map.71), channel_id=1, replica_groups={{0,32,64,96},{128,160,192,224},{256,288,320,352},{384,416,448,480},{512..., dimensions={0} | all-to-all | bytes 589824 | tf_op jit(solution)/shard_map/all_to_all | solution.py:464
  107.4 0.1 reduce_sum.34
  107.5 49.4 %all_to_all.28 = bf16[8,16,288]{2,1,0:T(8,128)(2,1)S(1)} all-to-all(bf16[8,16,288]{2,1,0:T(8,128)(2,1)S(1)} %reduce_sum.34), channel_id=1, replica_groups={{0,128,256,384,512,640,768,896},{32,160,288,416,544,672,800,928},{64,19..., dimensions={0} | all-to-all | bytes 147456 | tf_op jit(solution)/shard_map/all_to_all | solution.py:467
  157.0 0.1 broadcast_in_dim_reshape.3
  157.0 0.7 copy.25
  (6 shorter events, 0.1 us)
Async XLA Ops:
  1.4 8.4 %collective-permute-start = (bf16[3,1,32,128]{3,2,1,0:T(8,128)(2,1)S(1)}, bf16[3,1,32,128]{3,2,1,0:T(8,128)(2,1)S(1)}, u32[]{:S(2)}, u32[]{:S(2)}) collective-permute-start(bf16[3,1,32,128]{3,2,1,0:T(8,128)(2,1)S(1)} %get-tuple-element.29), channel_id=1, source_target_pairs={{0,32},{32,64},{64,96},{96,128},{128,160},{160,192},{192,224},{224... | collective-permute-start | bytes 73736 | tf_op jit(solution)/shard_map/ppermute | solution.py:383
  5.2 5.7 %collective-permute-start.1 = (bf16[3,1,32,128]{3,2,1,0:T(8,128)(2,1)S(1)}, bf16[3,1,32,128]{3,2,1,0:T(8,128)(2,1)S(1)}, u32[]{:S(2)}, u32[]{:S(2)}) collective-permute-start(bf16[3,1,32,128]{3,2,1,0:T(8,128)(2,1)S(1)} %get-tuple-element.28), channel_id=1, source_target_pairs={{32,0},{64,32},{96,64},{128,96},{160,128},{192,160},{224,192},{256... | collective-permute-start | bytes 73736 | tf_op jit(solution)/shard_map/ppermute | solution.py:383
  10.9 0.8 copy-start.1
  13.2 36.5 %all-to-all-start = ((bf16[16,432,128]{2,1,0:T(8,128)(2,1)}), bf16[16,432,128]{2,1,0:T(8,128)(2,1)S(1)}, u32[]{:S(2)}, u32[]{:S(2)}) async-start(bf16[16,432,128]{2,1,0:T(8,128)(2,1)} %get-tuple-element.13), calls=%async_computation | async-start | bytes 3538944 | tf_op jit(solution)/shard_map/all_to_all | solution.py:420
  27.2 22.5 %copy-start.2 = (bf16[1,3,2,32,128]{4,3,2,1,0:T(8,128)(2,1)S(1)}, bf16[1,3,2,32,128]{4,3,2,1,0:T(8,128)(2,1)}, u32[]{:S(2)}) copy-start(bf16[1,3,2,32,128]{4,3,2,1,0:T(8,128)(2,1)} %param.5) | copy-start | bytes 147460
  27.3 22.5 %copy-start.3 = (bf16[1,512,16]{1,2,0:T(8,128)(2,1)S(1)}, bf16[1,512,16]{1,2,0:T(8,128)(2,1)}, u32[]{:S(2)}) copy-start(bf16[1,512,16]{1,2,0:T(8,128)(2,1)} %param.8) | copy-start | bytes 49156
  49.7 2.3 %copy-start = (bf16[1,512,9,512]{3,1,2,0:T(8,128)(2,1)S(1)}, bf16[1,512,9,512]{3,1,2,0:T(8,128)(2,1)}, u32[]{:S(2)}) copy-start(bf16[1,512,9,512]{3,1,2,0:T(8,128)(2,1)} %param.7) | copy-start | bytes 14155780
  68.7 5.0 %collective-permute-start.2 = (bf16[3,2,16,128]{3,2,1,0:T(8,128)(2,1)S(1)}, bf16[3,2,16,128]{3,2,1,0:T(8,128)(2,1)S(1)}, u32[]{:S(2)}, u32[]{:S(2)}) collective-permute-start(bf16[3,2,16,128]{3,2,1,0:T(8,128)(2,1)S(1)} %reduce_sum.33.mid), channel_id=1, source_target_pairs={{0,32},{32,64},{64,96},{96,128},{128,160},{160,192},{192,224},{224... | collective-permute-start | bytes 73736 | tf_op jit(solution)/shard_map/ppermute | solution.py:383
  72.2 5.7 %collective-permute-start.3 = (bf16[3,2,16,128]{3,2,1,0:T(8,128)(2,1)S(1)}, bf16[3,2,16,128]{3,2,1,0:T(8,128)(2,1)S(1)}, u32[]{:S(2)}, u32[]{:S(2)}) collective-permute-start(bf16[3,2,16,128]{3,2,1,0:T(8,128)(2,1)S(1)} %reduce_sum.33.mid), channel_id=1, source_target_pairs={{32,0},{64,32},{96,64},{128,96},{160,128},{192,160},{224,192},{256... | collective-permute-start | bytes 73736 | tf_op jit(solution)/shard_map/ppermute | solution.py:383

commit v3 on v2

--- a/solution.py
+++ b/solution.py
@@ -11,7 +11,6 @@
 F32 = jnp.float32
 BF16 = jnp.bfloat16
 VMEM = pl.BlockSpec(memory_space=pltpu.VMEM)
-SMEM = pl.BlockSpec(memory_space=pltpu.SMEM)
 PARAMS = pltpu.CompilerParams(vmem_limit_bytes=40 * 1024 * 1024)
 
 
@@ -58,19 +57,44 @@
     return gathered[:, rows].reshape(gathered.shape[0] * part, gathered.shape[2])
 
 
-def mix_kernel(tile, low, high, depth, extra, proj_back, sent, own):
-    frames, rows, part, _ = tile.shape
-    peers, latents = sent.shape[0], proj_back.shape[0]
+def column(row):
+    count = row.shape[1]
+    square = jnp.broadcast_to(row, (count, count))
+    line = lax.broadcasted_iota(jnp.int32, square.shape, 0)
+    lane = lax.broadcasted_iota(jnp.int32, square.shape, 1)
+    return jnp.sum(jnp.where(line == lane, square, 0.0), axis=1, keepdims=True)
+
+
+def mix_kernel(tile, low, high, taps, proj_t, sent, own, proj_out):
+    frames, rows, part, columns = tile.shape
+    peers, latents = sent.shape[0], proj_t.shape[0]
     splits = peers // (frames * rows)
+    encoder = lax.axis_index("pipe") == 0
 
     def row_of(frame, row):
         if row == 0:
-            return low[frame, 0].astype(F32)
+            return low[frame, rows - 1].astype(F32)
         if row == rows + 1:
             return high[frame, 0].astype(F32)
         return tile[frame, row - 1].astype(F32)
 
-    weights = [depth[:, lag : lag + 1] for lag in range(3)]
+    proj_back = pick(proj_t, lax.axis_index("chan"), part)
+    line = lax.broadcasted_iota(jnp.int32, (part, part), 0)
+    lane = lax.broadcasted_iota(jnp.int32, (part, part), 1)
+    turned = dot_nt(jnp.where(line == lane, 1.0, 0.0).astype(BF16), proj_back).astype(BF16)
+    proj_out[...] = turned
+    depth = [column(taps[lag : lag + 1].astype(F32)) for lag in range(3)]
+    line = lax.broadcasted_iota(jnp.int32, (latents, columns), 0)
+    lane = lax.broadcasted_iota(jnp.int32, (latents, columns), 1)
+    extra = None
+    for lag in range(3):
+        spot = jnp.where(lane == line + lag * latents, 1.0, 0.0).astype(BF16)
+        term = depth[lag] * dot(turned, spot)
+        extra = term if extra is None else extra + term
+    extra = extra.astype(BF16)
+    weights = [
+        jnp.where(encoder, depth[lag], 1.0 if lag == 0 else 0.0) for lag in range(3)
+    ]
     for row in range(rows + 2):
         history = [row_of(frame, row) for frame in range(frames)]
         for frame in range(frames):
@@ -85,17 +109,17 @@
                 sent[peer, at : at + part] = block
     at = frames * (rows + 2) * part
     for peer in range(peers):
-        sent[peer, at : at + part] = extra[...]
+        sent[peer, at : at + part] = extra
         row, turn = peer // splits, peer % splits
         if row < frames * rows and turn == 0:
-            direct = dot(proj_back[...], tile[row // rows, row % rows]).astype(BF16)
+            direct = dot(proj_back, tile[row // rows, row % rows]).astype(BF16)
         else:
-            direct = jnp.zeros((latents, tile.shape[3]), BF16)
+            direct = jnp.zeros((latents, columns), BF16)
         sent[peer, at + part : at + part + latents] = direct
 
 
 def encode_kernel(
-    place, gathered, taps_out, tile, proj_t, kern, out, slope, sent, combo, wide_t, wide, held, done
+    gathered, taps_out, tile, proj_t, held, out, slope, sent, combo, wide_t, wide
 ):
     frames, rows, outs, columns = tile.shape
     peers = gathered.shape[0]
@@ -105,14 +129,11 @@
     deep = 3 * latents
     span = held.shape[2]
     splits = channels // span
-    row_at, turn = place[1] // splits, place[1] % splits
+    encoder, chan = lax.axis_index("pipe") == 0, lax.axis_index("chan")
+    row_at, turn = chan // splits, chan % splits
     active = row_at < frames * rows
-    fetch = pltpu.make_async_copy(
-        kern.at[:, :, pl.ds(pl.multiple_of(turn * span, span), span)], held, done
-    )
-    fetch.start()
-
-    @pl.when(place[0] == 0)
+
+    @pl.when(encoder)
     def _():
         weights = taps_out[...]
         for frame in range(frames):
@@ -129,9 +150,7 @@
                 out[frame, row] = (tile[frame, row].astype(F32) + summed * sigma).astype(BF16)
                 slope[frame, row] = sigma * (1.0 + summed * (1.0 - sigma))
 
-    fetch.wait()
-
-    @pl.when(jnp.logical_and(place[0] == 0, active))
+    @pl.when(jnp.logical_and(encoder, active))
     def _():
         base = (row_at // rows) * (rows + 2) + row_at % rows
         turned = [block_of(gathered, base + a, part).T for a in range(3)]
@@ -156,11 +175,11 @@
         for peer in range(sent.shape[0]):
             sent[peer] = latent
 
-    @pl.when(jnp.logical_or(place[0] == 1, jnp.logical_not(active)))
+    @pl.when(jnp.logical_not(jnp.logical_and(encoder, active)))
     def _():
         sent[...] = jnp.zeros_like(sent)
 
-    @pl.when(place[0] == 1)
+    @pl.when(jnp.logical_not(encoder))
     def _():
         factors = block_of(gathered, frames * (rows + 2), part)
         combo[...] = dot(taps_out[...], factors).astype(BF16)
@@ -194,7 +213,7 @@
 
 
 def decode_kernel(
-    scale, place, low, mid, high, own, combo, wide_t, wide, gathered, proj_out, proj_t, encoded,
+    scale, low, mid, high, own, combo, wide_t, wide, gathered, proj_out, proj_t, encoded,
     out, grad, sent, bank
 ):
     frames, rows, latents, columns = mid.shape
@@ -204,18 +223,19 @@
     span = wide.shape[0]
     peers = gathered.shape[0]
     splits = peers * part // span
-    row_at, turn = place[1] // splits, place[1] % splits
+    encoder, chan = lax.axis_index("pipe") == 0, lax.axis_index("chan")
+    row_at, turn = chan // splits, chan % splits
     active = row_at < frames * rows
 
-    @pl.when(place[0] == 0)
+    @pl.when(encoder)
     def _():
         out[...] = encoded[...]
 
-    @pl.when(jnp.logical_or(place[0] == 0, jnp.logical_not(active)))
+    @pl.when(jnp.logical_or(encoder, jnp.logical_not(active)))
     def _():
         sent[...] = jnp.zeros_like(sent)
 
-    @pl.when(place[0] == 1)
+    @pl.when(jnp.logical_not(encoder))
     def _():
         weights = combo[...][:, :deep]
         reach = range(1, 3 * rows - 1)
@@ -239,7 +259,7 @@
                 lifted = dot(proj_out[...], mid[frame, row]).astype(BF16)
                 out[frame, row] = (lifted.astype(F32) + summed * sigma).astype(BF16)
 
-    @pl.when(jnp.logical_and(place[0] == 1, active))
+    @pl.when(jnp.logical_and(jnp.logical_not(encoder), active))
     def _():
         bank[:, 0:2] = jnp.zeros((3, 2) + bank.shape[2:], BF16)
         for frame in range(frames):
@@ -299,12 +319,16 @@
             sent[peer] = latent
 
 
-def grad_kernel(place, arrived, slope, gathered, grad, low, mid, high, proj_out, sent):
+def grad_kernel(
+    arrived, slope, gathered, grad, low, mid, high, proj_out, send, keep, scratch
+):
     frames, rows, outs, columns = slope.shape
     peers = gathered.shape[0]
     part = outs
     latents = mid.shape[2]
-    near, far, share, _ = sent.shape
+    pairs = scratch.shape[0]
+    share = peers * part // (2 * pairs)
+    encoder = lax.axis_index("pipe") == 0
     splits = peers // (frames * rows)
 
     def window(grads, frame, row):
@@ -322,14 +346,24 @@
         return [shifted(value.astype(F32), 1 - b).astype(BF16) for b in range(3)]
 
     def store(total):
-        for i in range(far):
-            for j in range(near):
-                at = (near * i + j) * share
-                sent[j, i] = total[at : at + share].astype(BF16)
+        wide = (9 * outs // columns) * columns
+        for pair in range(pairs):
+            for side in range(2):
+                at = (2 * pair + side) * share
+                block = total[at : at + share]
+                for i in range(wide // columns):
+                    scratch[pair, side, i * share : (i + 1) * share] = block[
+                        :, i * columns : (i + 1) * columns
+                    ]
+                folds = columns // (9 * outs - wide)
+                few = share // folds
+                scratch[pair, side, wide // columns * share :] = jnp.concatenate(
+                    [block[i * few : (i + 1) * few, wide:] for i in range(folds)], axis=1
+                )
 
     spots = [(frame, row) for frame in range(frames) for row in range(rows + 2)]
 
-    @pl.when(place[0] == 0)
+    @pl.when(encoder)
     def _():
         grads = []
         for frame in range(frames):
@@ -347,7 +381,7 @@
         right = jnp.concatenate([window(grads, frame, row) for frame, row in spots], axis=1)
         store(dot_nt(left, right))
 
-    @pl.when(place[0] == 1)
+    @pl.when(jnp.logical_not(encoder))
     def _():
         grads = [[steps(grad[frame, row]) for row in range(rows)] for frame in range(frames)]
         left = jnp.concatenate(
@@ -364,6 +398,27 @@
         factors = block_of(gathered, len(spots), part)
         store(dot(factors[:, : 3 * latents], inner))
 
+    mine = lax.axis_index("slab") % 2
+    keep[...] = scratch[:, mine]
+    send[...] = scratch[:, 1 - mine].astype(BF16)
+
+
+def fold_kernel(pieces, out):
+    taps, share, outs = out.shape
+    columns = pieces.shape[2]
+    total = pieces[0].astype(F32)
+    for pair in range(1, pieces.shape[0]):
+        total = total + pieces[pair].astype(F32)
+    across = columns // outs
+    for tap in range(taps - 1):
+        at = tap // across * share
+        lane = tap % across * outs
+        out[tap] = total[at : at + share, lane : lane + outs]
+    rest = total[(taps - 1) // across * share :]
+    out[taps - 1] = jnp.concatenate(
+        [rest[:, i * outs : (i + 1) * outs] for i in range(across)], axis=0
+    )
+
 
 def call(kernel, shapes, specs, scratch=()):
     return pl.pallas_call(
@@ -385,8 +440,6 @@
 
 def on_device(features, taps, kern, proj):
     shape = jax.ShapeDtypeStruct
-    pipe = lax.axis_index("pipe")
-    slab = lax.axis_index("slab")
     peers = lax.axis_size("chan")
     slabs = lax.axis_size("slab")
     both = peers * lax.axis_size("pipe")
@@ -394,31 +447,28 @@
     frames, rows, part, columns = tile.shape
     channels, latents = proj.shape[1], proj.shape[2]
     share = channels // slabs
-    offset = lax.axis_index("chan") * part
-    place = jnp.stack([pipe, lax.axis_index("chan")]).astype(jnp.int32)
+    chan = lax.axis_index("chan")
+    offset = chan * part
     scale = 1.0 / math.sqrt(frames * rows * slabs * columns)
     splits = peers // (frames * rows)
     span = channels // splits
 
-    above, below = both_ways(tile[:, :1], tile[:, rows - 1 :], "slab")
+    above, below = both_ways(tile, tile, "slab")
     proj_t = proj[0].T
-    proj_out = lax.dynamic_slice_in_dim(proj[0], offset, part, 0)
-    proj_back = proj_out.T
-    depth = taps[0].astype(F32).T
-    factors = (depth[:, :, None] * proj_out.astype(F32)[:, None, :]).reshape(part, 3 * latents)
-    extra = jnp.pad(factors.astype(BF16), ((0, 0), (0, columns - 3 * latents)))
-    depth = jnp.where(pipe == 0, depth, jnp.array([[1.0, 0.0, 0.0]], F32))
     height = (frames * (rows + 2) + 1) * part + latents
-    sent, own = call(
+    sent, own, proj_out = call(
         mix_kernel,
         (
             shape((peers, height, columns), BF16),
             shape((frames, rows + 2, part, columns), BF16),
+            shape((part, latents), BF16),
         ),
-        [VMEM] * 6,
-    )(tile, above, below, depth, extra, proj_back)
+        [VMEM] * 5,
+    )(tile, above, below, taps[0], proj_t)
     gathered = lax.all_to_all(sent, "chan", 0, 0)
 
+    by_tap = kern[0].transpose(1, 0, 2)
+    held = lax.dynamic_slice_in_dim(by_tap, chan % splits * span, span, 2)
     out_cols = lax.dynamic_slice_in_dim(kern[0], offset, part, 2)
     taps_out = out_cols.transpose(1, 2, 0).reshape(9 * part, channels)
     tile_shape = (frames, rows, part, columns)
@@ -434,9 +484,8 @@
             shape((terms, span), BF16),
             shape((span, terms), BF16),
         ),
-        [SMEM] + [VMEM] * 4 + [pl.BlockSpec(memory_space=pl.ANY)],
-        [pltpu.VMEM((9, channels, span), BF16), pltpu.SemaphoreType.DMA],
-    )(place, gathered, taps_out, tile, proj_t, kern[0].transpose(1, 0, 2))
+        [VMEM] * 5,
+    )(gathered, taps_out, tile, proj_t, held)
 
     arrived = lax.all_to_all(sent, ("chan", "pipe"), 0, 0)
     arrived = arrived.reshape(peers, 2, latents, columns)[: frames * rows * splits, 0]
@@ -446,26 +495,27 @@
     out, grad, sent = call(
         functools.partial(decode_kernel, scale),
         (shape(tile_shape, BF16), shape(tile_shape, BF16), shape(latent_shape, BF16)),
-        [SMEM] + [VMEM] * 11,
+        [VMEM] * 11,
         [pltpu.VMEM((3, frames + 2, 3 * rows, latents, columns), BF16)],
     )(
-        place, low, mid, high, own, combo, wide_t, wide, gathered, proj_out, proj_t, encoded
+        low, mid, high, own, combo, wide_t, wide, gathered, proj_out, proj_t, encoded
     )
 
     arrived = lax.all_to_all(sent, ("chan", "pipe"), 0, 0)
-    near = 4
-    far = slabs // near
-    sent = call(
+    pairs = slabs // 2
+    lines = share * 9 * part // columns
+    send, keep = call(
         grad_kernel,
-        shape((near, far, share, 9 * part), BF16),
-        [SMEM] + [VMEM] * 8,
-    )(place, arrived, slope, gathered, grad, low, mid, high, proj_out)
-    groups = [[near * i + j for j in range(near)] for i in range(far)]
-    pieces = lax.all_to_all(sent, "slab", 0, 0, axis_index_groups=groups)
-    partial = jnp.sum(pieces.astype(F32), axis=0).astype(BF16)
-    groups = [[near * i + j for i in range(far)] for j in range(near)]
-    pieces = lax.all_to_all(partial, "slab", 0, 0, axis_index_groups=groups)
-    total = jnp.sum(pieces.astype(F32), axis=0).reshape(share, 9, part)
+        (shape((pairs, lines, columns), BF16), shape((pairs, lines, columns), F32)),
+        [VMEM] * 8,
+        [pltpu.VMEM((pairs, 2, lines, columns), F32)],
+    )(arrived, slope, gathered, grad, low, mid, high, proj_out)
+    got = lax.ppermute(send, "slab", [(i, i ^ 1) for i in range(slabs)])
+    halved = (keep + got.astype(F32)).astype(BF16)
+    groups = [[2 * p + q for p in range(pairs)] for q in range(2)]
+    pieces = lax.all_to_all(halved, "slab", 0, 0, axis_index_groups=groups)
+    total = call(fold_kernel, shape((9, share, part), F32), [VMEM])(pieces)
+    total = total.transpose(1, 0, 2)
     return out[None], total[None]
 
 

time: 158 us -> 151 us (0.956)
  the two profiles are of different devices: /device:TPU:8 before, /device:TPU:120 now
where the time goes in v3:
time: 151 us; the launch traced here: 150 us
  blocking collectives  75 us (50%)
  starting transfers between devices  28.4 us (19%)
  waiting for transfers between devices  28.1 us (19%)
  local copies, waits for them, and re-layouts  11.5 us (8%)
  Pallas kernels  6.61 us (4%)
    all_to_all x1, blocking collectives, on_device(): pieces = lax.all_to_all(halved, 'slab', 0, 0, axis_index_groups=groups)  52 us
    all_to_all x2, blocking collectives, on_device(): arrived = lax.all_to_all(sent, ('chan', 'pipe'), 0, 0)  23 us
    all_to_all x1, waiting for transfers between devices, on_device(): gathered = lax.all_to_all(sent, 'chan', 0, 0)  17.5 us
    ppermute x2, starting transfers between devices, both_ways(): lax.ppermute(low_side, axis, backward)  10.3 us
    all_to_all x1, starting transfers between devices, on_device(): gathered = lax.all_to_all(sent, 'chan', 0, 0)  7.17 us
    ppermute x2, starting transfers between devices, both_ways(): lax.ppermute(high_side, axis, forward)  6.96 us
    ppermute x2, waiting for transfers between devices, both_ways(): lax.ppermute(high_side, axis, forward)  5.49 us
    unnamed x13, local copies, waits for them, and re-layouts  5.49 us
  transfers between devices with their start and end apart: 6, of which 5 were waited for; matrix products, arithmetic and copies ran while one was open for 5% of the time, Pallas kernels for 0%

profile of v3, /device:TPU:120, one launch (start us, length us, event | category | flops | bytes accessed | tf_op | source)
XLA Modules:
  0.0 150.3 jit_solution(460918744747492796)
XLA Ops:
  0.6 2.0 %collective-permute-start.1 = (bf16[3,2,32,128]{3,2,1,0:T(8,128)(2,1)}, bf16[3,2,32,128]{3,2,1,0:T(8,128)(2,1)S(1)}, u32[]{:S(2)}, u32[]{:S(2)}) collective-permute-start(bf16[3,2,32,128]{3,2,1,0:T(8,128)(2,1)} %bitcast.21), channel_id=1, source_target_pairs={{32,0},{64,32},{96,64},{128,96},{160,128},{192,160},{224,192},{256... | collective-permute-start | bytes 147464 | tf_op jit(solution)/shard_map/ppermute | solution.py:438
  2.7 5.0 %collective-permute-start = (bf16[3,2,32,128]{3,2,1,0:T(8,128)(2,1)}, bf16[3,2,32,128]{3,2,1,0:T(8,128)(2,1)S(1)}, u32[]{:S(2)}, u32[]{:S(2)}) collective-permute-start(bf16[3,2,32,128]{3,2,1,0:T(8,128)(2,1)} %bitcast.22), channel_id=1, source_target_pairs={{0,32},{32,64},{64,96},{96,128},{128,160},{160,192},{192,224},{224... | collective-permute-start | bytes 147464 | tf_op jit(solution)/shard_map/ppermute | solution.py:438
  7.7 0.3 collective-permute-done.1.high
  8.0 1.7 %collective-permute-done.low = bf16[3,2,32,128]{3,2,1,0:T(8,128)(2,1)S(1)} collective-permute-done((bf16[3,2,32,128]{3,2,1,0:T(8,128)(2,1)}, bf16[3,2,32,128]{3,2,1,0:T(8,128)(2,1)S(1)}, u32[]{:S(2)}, u32[]{:S(2)}) %collective-permute-start) | collective-permute-done | bytes 49184 | tf_op jit(solution)/shard_map/ppermute | solution.py:438
  9.7 0.0 copy-start.1
  9.8 0.8 copy-done.1
  10.5 0.0 copy-start.3
  10.5 0.7 copy-done.3
  11.3 0.0 copy-start.5
  11.3 0.7 copy-done.5
  11.9 2.6 %shard_map.59 = (bf16[16,432,128]{2,1,0:T(8,128)(2,1)}, bf16[3,4,32,128]{3,2,1,0:T(8,128)(2,1)S(1)}, bf16[32,16]{1,0:T(8,128)(2,1)S(1)}) custom-call(bf16[3,2,32,128]{3,2,1,0:T(8,128)(2,1)S(1)} %bitcast.23, bf16[3,2,32,128]{3,2,1,0:T(8,128)(2,1)S(1)} %collective-permute-done.low, bf16[3,2,32,128]{3,2,1,0:T(8,128)(2,1)S(1)} %collective-permute-done.1.high, ...), custom_call_target="tpu_custom_call" | custom-call | tf_op jit(solution)/shard_map/pallas_call | solution.py:459
  14.5 7.2 %all-to-all-start = ((bf16[16,432,128]{2,1,0:T(8,128)(2,1)}), bf16[16,432,128]{2,1,0:T(8,128)(2,1)S(1)}, u32[]{:S(2)}, u32[]{:S(2)}) async-start(bf16[16,432,128]{2,1,0:T(8,128)(2,1)} %get-tuple-element.16), calls=%async_computation | async-start | bytes 3538944 | tf_op jit(solution)/shard_map/all_to_all | solution.py:468
  21.7 2.7 %constant_dynamic-slice_fusion = bf16[1,512,9,32]{3,1,2,0:T(8,128)(2,1)} fusion(bf16[1,512,9,512]{3,1,2,0:T(8,128)(2,1)} %param.6, s32[]{:T(128)S(6)} %select_n.13), kind=kLoop, calls=%fused_computation.2 | loop fusion | bytes 589828 | tf_op jit(solution)/shard_map/dynamic_slice | solution.py:472
  24.4 1.6 %copy.7 = bf16[1,512,9,32]{1,3,2,0:T(8,128)(2,1)S(1)} copy(bf16[1,512,9,32]{3,1,2,0:T(8,128)(2,1)} %constant_dynamic-slice_fusion) | data formatting | bytes 589824
  26.0 0.0 copy-start.2
  26.0 0.0 copy-start.4
  26.0 3.3 %dynamic-slice_bitcast_fusion.held = bf16[9,512,256]{2,1,0:T(8,128)(2,1)} fusion(bf16[1,512,9,512]{3,1,2,0:T(8,128)(2,1)} %param.6, s32[]{:T(128)S(6)} %select_n.15), kind=kLoop, calls=%fused_computation | loop fusion | bytes 4718596 | tf_op jit(solution)/shard_map/dynamic_slice | solution.py:471
  29.3 17.5 %all-to-all-done.gathered = bf16[16,432,128]{2,1,0:T(8,128)(2,1)S(1)} async-done(((bf16[16,432,128]{2,1,0:T(8,128)(2,1)}), bf16[16,432,128]{2,1,0:T(8,128)(2,1)S(1)}, u32[]{:S(2)}, u32[]{:S(2)}) %all-to-all-start) | async-done | bytes 1769504 | tf_op jit(solution)/shard_map/all_to_all | solution.py:468
  46.8 0.0 copy-done.2
  46.8 0.0 copy-done.4
  46.9 0.0 copy-start
  46.9 1.7 %copy-done = bf16[9,512,256]{2,1,0:T(8,128)(2,1)S(1)} copy-done((bf16[9,512,256]{2,1,0:T(8,128)(2,1)S(1)}, bf16[9,512,256]{2,1,0:T(8,128)(2,1)}, u32[]{:S(2)}) %copy-start) | copy-done | bytes 2359320
  48.5 1.4 shard_map.60
  49.9 10.8 %all_to_all.20 = bf16[32,16,128]{2,1,0:T(8,128)(2,1)S(1)} all-to-all(bf16[32,16,128]{2,1,0:T(8,128)(2,1)S(1)} %get-tuple-element.17), channel_id=1, replica_groups=mesh['slab'=32,'chan'=16,'pipe'=2] {'chan','pipe'}, dimensions={0} | all-to-all | bytes 262144 | tf_op jit(solution)/shard_map/all_to_all | solution.py:490
  60.7 8.3 %collective-permute-start.3 = (bf16[3,2,16,128]{3,2,1,0:T(8,128)(2,1)S(1)}, bf16[3,2,16,128]{3,2,1,0:T(8,128)(2,1)S(1)}, u32[]{:S(2)}, u32[]{:S(2)}) collective-permute-start(bf16[3,2,16,128]{3,2,1,0:T(8,128)(2,1)S(1)} %reduce_sum.12.mid), channel_id=1, source_target_pairs={{32,0},{64,32},{96,64},{128,96},{160,128},{192,160},{224,192},{256... | collective-permute-start | bytes 73736 | tf_op jit(solution)/shard_map/ppermute | solution.py:438
  69.0 1.9 %collective-permute-start.2 = (bf16[3,2,16,128]{3,2,1,0:T(8,128)(2,1)S(1)}, bf16[3,2,16,128]{3,2,1,0:T(8,128)(2,1)S(1)}, u32[]{:S(2)}, u32[]{:S(2)}) collective-permute-start(bf16[3,2,16,128]{3,2,1,0:T(8,128)(2,1)S(1)} %reduce_sum.12.mid), channel_id=1, source_target_pairs={{0,32},{32,64},{64,96},{96,128},{128,160},{160,192},{192,224},{224... | collective-permute-start | bytes 73736 | tf_op jit(solution)/shard_map/ppermute | solution.py:438
  71.0 0.0 collective-permute-done.3.high
  71.0 3.8 %collective-permute-done.2.low = bf16[3,2,16,128]{3,2,1,0:T(8,128)(2,1)S(1)} collective-permute-done((bf16[3,2,16,128]{3,2,1,0:T(8,128)(2,1)S(1)}, bf16[3,2,16,128]{3,2,1,0:T(8,128)(2,1)S(1)}, u32[]{:S(2)}, u32[]{:S(2)}) %collective-permute-start.2) | collective-permute-done | bytes 24608 | tf_op jit(solution)/shard_map/ppermute | solution.py:438
  74.8 0.6 shard_map.61
  75.4 12.3 %all_to_all.21.arrived = bf16[32,16,128]{2,1,0:T(8,128)(2,1)S(1)} all-to-all(bf16[32,16,128]{2,1,0:T(8,128)(2,1)S(1)} %get-tuple-element.25), channel_id=1, replica_groups=mesh['slab'=32,'chan'=16,'pipe'=2] {'chan','pipe'}, dimensions={0} | all-to-all | bytes 262144 | tf_op jit(solution)/shard_map/all_to_all | solution.py:504
  87.7 1.2 shard_map.62
  88.9 3.9 %collective-permute-start.4 = (bf16[16,36,128]{2,1,0:T(8,128)(2,1)S(1)}, bf16[16,36,128]{2,1,0:T(8,128)(2,1)S(1)}, u32[]{:S(2)}, u32[]{:S(2)}) collective-permute-start(bf16[16,36,128]{2,1,0:T(8,128)(2,1)S(1)} %get-tuple-element.29), channel_id=1, source_target_pairs={{0,32},{32,0},{64,96},{96,64},{128,160},{160,128},{192,224},{224,1... | collective-permute-start | bytes 442376 | tf_op jit(solution)/shard_map/ppermute | solution.py:513
  92.8 4.7 %collective-permute-done.4 = bf16[16,36,128]{2,1,0:T(8,128)(2,1)S(1)} collective-permute-done((bf16[16,36,128]{2,1,0:T(8,128)(2,1)S(1)}, bf16[16,36,128]{2,1,0:T(8,128)(2,1)S(1)}, u32[]{:S(2)}, u32[]{:S(2)}) %collective-permute-start.4) | collective-permute-done | bytes 147488 | tf_op jit(solution)/shard_map/ppermute | solution.py:513
  97.6 52.0 %all_to_all.22.pieces = bf16[16,36,128]{2,1,0:T(8,128)(2,1)S(1)} all-to-all(bf16[16,36,128]{2,1,0:T(8,128)(2,1)S(1)} %add_convert_fusion), channel_id=1, replica_groups={{0,64,128,192,256,320,384,448,512,576,640,704,768,832,896,960},{32,96,1..., dimensions={0} | all-to-all | bytes 294912 | tf_op jit(solution)/shard_map/all_to_all | solution.py:516
  149.5 0.7 shard_map.63
  (3 shorter events, 0.1 us)
Async XLA Ops:
  0.6 7.4 %collective-permute-start.1 = (bf16[3,2,32,128]{3,2,1,0:T(8,128)(2,1)}, bf16[3,2,32,128]{3,2,1,0:T(8,128)(2,1)S(1)}, u32[]{:S(2)}, u32[]{:S(2)}) collective-permute-start(bf16[3,2,32,128]{3,2,1,0:T(8,128)(2,1)} %bitcast.21), channel_id=1, source_target_pairs={{32,0},{64,32},{96,64},{128,96},{160,128},{192,160},{224,192},{256... | collective-permute-start | bytes 147464 | tf_op jit(solution)/shard_map/ppermute | solution.py:438
  2.7 7.1 %collective-permute-start = (bf16[3,2,32,128]{3,2,1,0:T(8,128)(2,1)}, bf16[3,2,32,128]{3,2,1,0:T(8,128)(2,1)S(1)}, u32[]{:S(2)}, u32[]{:S(2)}) collective-permute-start(bf16[3,2,32,128]{3,2,1,0:T(8,128)(2,1)} %bitcast.22), channel_id=1, source_target_pairs={{0,32},{32,64},{64,96},{96,128},{128,160},{160,192},{192,224},{224... | collective-permute-start | bytes 147464 | tf_op jit(solution)/shard_map/ppermute | solution.py:438
  9.7 0.8 copy-start.1
  10.5 0.7 copy-start.3
  11.3 0.7 copy-start.5
  14.5 32.3 %all-to-all-start = ((bf16[16,432,128]{2,1,0:T(8,128)(2,1)}), bf16[16,432,128]{2,1,0:T(8,128)(2,1)S(1)}, u32[]{:S(2)}, u32[]{:S(2)}) async-start(bf16[16,432,128]{2,1,0:T(8,128)(2,1)} %get-tuple-element.16), calls=%async_computation | async-start | bytes 3538944 | tf_op jit(solution)/shard_map/all_to_all | solution.py:468
  26.0 20.8 %copy-start.2 = (bf16[1,3,2,32,128]{4,3,2,1,0:T(8,128)(2,1)S(1)}, bf16[1,3,2,32,128]{4,3,2,1,0:T(8,128)(2,1)}, u32[]{:S(2)}) copy-start(bf16[1,3,2,32,128]{4,3,2,1,0:T(8,128)(2,1)} %param.4) | copy-start | bytes 147460
  26.0 20.8 %copy-start.4 = (bf16[1,512,16]{1,2,0:T(8,128)(2,1)S(1)}, bf16[1,512,16]{1,2,0:T(8,128)(2,1)}, u32[]{:S(2)}) copy-start(bf16[1,512,16]{1,2,0:T(8,128)(2,1)} %param.7) | copy-start | bytes 49156
  46.9 1.7 %copy-start = (bf16[9,512,256]{2,1,0:T(8,128)(2,1)S(1)}, bf16[9,512,256]{2,1,0:T(8,128)(2,1)}, u32[]{:S(2)}) copy-start(bf16[9,512,256]{2,1,0:T(8,128)(2,1)} %dynamic-slice_bitcast_fusion.held) | copy-start | bytes 7077892
  60.7 10.2 %collective-permute-start.3 = (bf16[3,2,16,128]{3,2,1,0:T(8,128)(2,1)S(1)}, bf16[3,2,16,128]{3,2,1,0:T(8,128)(2,1)S(1)}, u32[]{:S(2)}, u32[]{:S(2)}) collective-permute-start(bf16[3,2,16,128]{3,2,1,0:T(8,128)(2,1)S(1)} %reduce_sum.12.mid), channel_id=1, source_target_pairs={{32,0},{64,32},{96,64},{128,96},{160,128},{192,160},{224,192},{256... | collective-permute-start | bytes 73736 | tf_op jit(solution)/shard_map/ppermute | solution.py:438
  69.0 5.7 %collective-permute-start.2 = (bf16[3,2,16,128]{3,2,1,0:T(8,128)(2,1)S(1)}, bf16[3,2,16,128]{3,2,1,0:T(8,128)(2,1)S(1)}, u32[]{:S(2)}, u32[]{:S(2)}) collective-permute-start(bf16[3,2,16,128]{3,2,1,0:T(8,128)(2,1)S(1)} %reduce_sum.12.mid), channel_id=1, source_target_pairs={{0,32},{32,64},{64,96},{96,128},{128,160},{160,192},{192,224},{224... | collective-permute-start | bytes 73736 | tf_op jit(solution)/shard_map/ppermute | solution.py:438
  88.9 8.6 %collective-permute-start.4 = (bf16[16,36,128]{2,1,0:T(8,128)(2,1)S(1)}, bf16[16,36,128]{2,1,0:T(8,128)(2,1)S(1)}, u32[]{:S(2)}, u32[]{:S(2)}) collective-permute-start(bf16[16,36,128]{2,1,0:T(8,128)(2,1)S(1)} %get-tuple-element.29), channel_id=1, source_target_pairs={{0,32},{32,0},{64,96},{96,64},{128,160},{160,128},{192,224},{224,1... | collective-permute-start | bytes 442376 | tf_op jit(solution)/shard_map/ppermute | solution.py:513

commit v4 on v3

--- a/solution.py
+++ b/solution.py
@@ -11,6 +11,7 @@
 F32 = jnp.float32
 BF16 = jnp.bfloat16
 VMEM = pl.BlockSpec(memory_space=pltpu.VMEM)
+HBM = pl.BlockSpec(memory_space=pltpu.HBM)
 PARAMS = pltpu.CompilerParams(vmem_limit_bytes=40 * 1024 * 1024)
 
 
@@ -52,9 +53,16 @@
     return sums
 
 
-def block_of(gathered, at, part):
+def block_of(pair, at, part, first=0, count=None):
+    mine, theirs = pair
+    count = mine.shape[0] if count is None else count
     rows = pl.ds(pl.multiple_of(at * part, part), part)
-    return gathered[:, rows].reshape(gathered.shape[0] * part, gathered.shape[2])
+    left = mine[pl.ds(first, count), rows]
+    right = theirs[pl.ds(first, count), rows]
+    swap = lax.axis_index("chan") % 2 == 1
+    even = jnp.where(swap, right, left)
+    odd = jnp.where(swap, left, right)
+    return jnp.concatenate([half[i] for i in range(count) for half in (even, odd)], axis=0)
 
 
 def column(row):
@@ -65,72 +73,99 @@
     return jnp.sum(jnp.where(line == lane, square, 0.0), axis=1, keepdims=True)
 
 
-def mix_kernel(tile, low, high, taps, proj_t, sent, own, proj_out):
+def mix_weights(taps):
+    encoder = lax.axis_index("pipe") == 0
+    depth = [column(taps[lag : lag + 1].astype(F32)) for lag in range(3)]
+    return [jnp.where(encoder, depth[lag], 1.0 if lag == 0 else 0.0) for lag in range(3)], depth
+
+
+def mix_rows(history, weights):
+    mixed = []
+    for frame in range(len(history)):
+        total = weights[0] * history[frame]
+        for lag in range(1, 3):
+            if frame >= lag:
+                total = total + weights[lag] * history[frame - lag]
+        mixed.append(total.astype(BF16))
+    return mixed
+
+
+def prepare_kernel(
+    tile, taps, proj_t, kern, mid, extra, direct, proj_out, taps_out, held, done
+):
     frames, rows, part, columns = tile.shape
-    peers, latents = sent.shape[0], proj_t.shape[0]
-    splits = peers // (frames * rows)
-    encoder = lax.axis_index("pipe") == 0
-
-    def row_of(frame, row):
-        if row == 0:
-            return low[frame, rows - 1].astype(F32)
-        if row == rows + 1:
-            return high[frame, 0].astype(F32)
-        return tile[frame, row - 1].astype(F32)
-
-    proj_back = pick(proj_t, lax.axis_index("chan"), part)
+    latents = proj_t.shape[0]
+    chan = lax.axis_index("chan")
+    across = columns // part
+    lanes = pl.ds(pl.multiple_of(chan // across * columns, columns), columns)
+    fetch = pltpu.make_async_copy(kern.at[:, :, lanes], held, done)
+    fetch.start()
+    proj_back = pick(proj_t, chan, part)
     line = lax.broadcasted_iota(jnp.int32, (part, part), 0)
     lane = lax.broadcasted_iota(jnp.int32, (part, part), 1)
     turned = dot_nt(jnp.where(line == lane, 1.0, 0.0).astype(BF16), proj_back).astype(BF16)
     proj_out[...] = turned
-    depth = [column(taps[lag : lag + 1].astype(F32)) for lag in range(3)]
+    weights, depth = mix_weights(taps)
     line = lax.broadcasted_iota(jnp.int32, (latents, columns), 0)
     lane = lax.broadcasted_iota(jnp.int32, (latents, columns), 1)
-    extra = None
+    total = None
     for lag in range(3):
         spot = jnp.where(lane == line + lag * latents, 1.0, 0.0).astype(BF16)
         term = depth[lag] * dot(turned, spot)
-        extra = term if extra is None else extra + term
-    extra = extra.astype(BF16)
-    weights = [
-        jnp.where(encoder, depth[lag], 1.0 if lag == 0 else 0.0) for lag in range(3)
-    ]
-    for row in range(rows + 2):
-        history = [row_of(frame, row) for frame in range(frames)]
+        total = term if total is None else total + term
+    extra[...] = total.astype(BF16)
+    for row in range(rows):
+        mixed = mix_rows([tile[frame, row].astype(F32) for frame in range(frames)], weights)
         for frame in range(frames):
-            total = weights[0] * history[frame]
-            for lag in range(1, 3):
-                if frame >= lag:
-                    total = total + weights[lag] * history[frame - lag]
-            block = total.astype(BF16)
-            own[frame, row] = block
+            mid[frame, row] = mixed[frame]
+            direct[frame * rows + row] = dot(proj_back, tile[frame, row]).astype(BF16)
+    fetch.wait()
+    for tap in range(9):
+        block = held[tap].T
+        chosen = block[:part]
+        for at in range(1, across):
+            chosen = jnp.where(chan % across == at, block[at * part : (at + 1) * part], chosen)
+        taps_out[tap * part : (tap + 1) * part] = chosen
+
+
+def mix_kernel(low, high, taps, mid, extra, direct, sent, own):
+    frames, rows, part, columns = mid.shape
+    chips = sent.shape[0]
+    latents = direct.shape[1]
+    weights, _ = mix_weights(taps)
+    before = mix_rows([low[frame, rows - 1].astype(F32) for frame in range(frames)], weights)
+    after = mix_rows([high[frame, 0].astype(F32) for frame in range(frames)], weights)
+    for frame in range(frames):
+        blocks = [before[frame]] + [mid[frame, row] for row in range(rows)] + [after[frame]]
+        for row in range(rows + 2):
+            own[frame, row] = blocks[row]
             at = (frame * (rows + 2) + row) * part
-            for peer in range(peers):
-                sent[peer, at : at + part] = block
+            for chip in range(chips):
+                sent[chip, at : at + part] = blocks[row]
     at = frames * (rows + 2) * part
-    for peer in range(peers):
-        sent[peer, at : at + part] = extra
-        row, turn = peer // splits, peer % splits
-        if row < frames * rows and turn == 0:
-            direct = dot(proj_back, tile[row // rows, row % rows]).astype(BF16)
+    for chip in range(chips):
+        sent[chip, at : at + part] = extra[...]
+        if chip < frames * rows:
+            sent[chip, at + part : at + part + latents] = direct[chip]
         else:
-            direct = jnp.zeros((latents, columns), BF16)
-        sent[peer, at + part : at + part + latents] = direct
+            sent[chip, at + part : at + part + latents] = jnp.zeros((latents, columns), BF16)
 
 
 def encode_kernel(
-    gathered, taps_out, tile, proj_t, held, out, slope, sent, combo, wide_t, wide
+    mine, theirs, taps_out, tile, proj_t, kern, out, slope, sent, combo, wide_t, wide, held, done
 ):
     frames, rows, outs, columns = tile.shape
-    peers = gathered.shape[0]
+    gathered = (mine, theirs)
     part = outs
-    channels = peers * part
     latents = proj_t.shape[0]
     deep = 3 * latents
     span = held.shape[2]
-    splits = channels // span
     encoder, chan = lax.axis_index("pipe") == 0, lax.axis_index("chan")
-    row_at, turn = chan // splits, chan % splits
+    row_at, turn = chan // 2, chan % 2
+    fetch = pltpu.make_async_copy(
+        kern.at[:, :, pl.ds(pl.multiple_of(turn * span, span), span)], held, done
+    )
+    fetch.start()
     active = row_at < frames * rows
 
     @pl.when(encoder)
@@ -149,6 +184,8 @@
                 sigma = logistic(summed)
                 out[frame, row] = (tile[frame, row].astype(F32) + summed * sigma).astype(BF16)
                 slope[frame, row] = sigma * (1.0 + summed * (1.0 - sigma))
+
+    fetch.wait()
 
     @pl.when(jnp.logical_and(encoder, active))
     def _():
@@ -169,9 +206,11 @@
         bent = (summed * logistic(summed)).astype(BF16)
         latent = dot_nt(pick(proj_t, turn, span), bent)
         at = (frames * (rows + 2) + 1) * part
-        for peer in range(peers):
-            latent = latent + gathered[peer, at : at + latents].astype(F32)
-        latent = latent.astype(BF16)
+        direct = jnp.zeros_like(latent)
+        for chip in range(mine.shape[0]):
+            for half in gathered:
+                direct = direct + half[chip, at : at + latents].astype(F32)
+        latent = (latent + jnp.where(turn == 0, direct, 0.0)).astype(BF16)
         for peer in range(sent.shape[0]):
             sent[peer] = latent
 
@@ -213,7 +252,7 @@
 
 
 def decode_kernel(
-    scale, low, mid, high, own, combo, wide_t, wide, gathered, proj_out, proj_t, encoded,
+    scale, low, mid, high, own, combo, wide_t, wide, mine, theirs, proj_out, proj_t, encoded,
     out, grad, sent, bank
 ):
     frames, rows, latents, columns = mid.shape
@@ -221,10 +260,9 @@
     part = outs
     deep = 3 * latents
     span = wide.shape[0]
-    peers = gathered.shape[0]
-    splits = peers * part // span
+    gathered = (mine, theirs)
     encoder, chan = lax.axis_index("pipe") == 0, lax.axis_index("chan")
-    row_at, turn = chan // splits, chan % splits
+    row_at, turn = chan // 2, chan % 2
     active = row_at < frames * rows
 
     @pl.when(encoder)
@@ -268,12 +306,10 @@
                 for b in range(3):
                     bank[b, frame + 2, row] = shifted(value, b - 1).astype(BF16)
         frame_at, line = row_at // rows, row_at % rows
-        first = turn * (span // part)
+        chips = mine.shape[0] // 2
 
         def channel_rows(frame, row):
-            at = pl.multiple_of((frame * (rows + 2) + row) * part, part)
-            block = gathered[pl.ds(first, span // part), pl.ds(at, part)]
-            return block.reshape(span, columns)
+            return block_of(gathered, frame * (rows + 2) + row, part, turn * chips, chips)
 
         columns_of = []
         for lag in range(3):
@@ -320,16 +356,15 @@
 
 
 def grad_kernel(
-    arrived, slope, gathered, grad, low, mid, high, proj_out, send, keep, scratch
+    arrived, slope, mine, theirs, grad, low, mid, high, proj_out, sent
 ):
     frames, rows, outs, columns = slope.shape
-    peers = gathered.shape[0]
+    gathered = (mine, theirs)
     part = outs
+    near, far = sent.shape[:2]
+    share = 2 * mine.shape[0] * part // (near * far)
     latents = mid.shape[2]
-    pairs = scratch.shape[0]
-    share = peers * part // (2 * pairs)
     encoder = lax.axis_index("pipe") == 0
-    splits = peers // (frames * rows)
 
     def window(grads, frame, row):
         blank = jnp.zeros((outs, columns), BF16)
@@ -346,20 +381,18 @@
         return [shifted(value.astype(F32), 1 - b).astype(BF16) for b in range(3)]
 
     def store(total):
+        total = total.astype(BF16).astype(F32)
         wide = (9 * outs // columns) * columns
-        for pair in range(pairs):
-            for side in range(2):
-                at = (2 * pair + side) * share
+        folds = columns // (9 * outs - wide)
+        few = share // folds
+        for i in range(far):
+            for j in range(near):
+                at = (near * i + j) * share
                 block = total[at : at + share]
-                for i in range(wide // columns):
-                    scratch[pair, side, i * share : (i + 1) * share] = block[
-                        :, i * columns : (i + 1) * columns
-                    ]
-                folds = columns // (9 * outs - wide)
-                few = share // folds
-                scratch[pair, side, wide // columns * share :] = jnp.concatenate(
-                    [block[i * few : (i + 1) * few, wide:] for i in range(folds)], axis=1
-                )
+                pieces = [block[:, k : k + columns] for k in range(0, wide, columns)]
+                rest = [block[k * few : (k + 1) * few, wide:] for k in range(folds)]
+                pieces.append(jnp.concatenate(rest, axis=1))
+                sent[j, i] = jnp.concatenate(pieces, axis=0).astype(BF16)
 
     spots = [(frame, row) for frame in range(frames) for row in range(rows + 2)]
 
@@ -369,10 +402,8 @@
         for frame in range(frames):
             grads.append([])
             for row in range(rows):
-                at = (frame * rows + row) * splits
-                latent = arrived[2 * at + 1].astype(F32)
-                for turn in range(1, splits):
-                    latent = latent + arrived[2 * (at + turn) + 1].astype(F32)
+                at = 4 * (frame * rows + row)
+                latent = arrived[at + 1].astype(F32) + arrived[at + 3].astype(F32)
                 value = dot(proj_out[...], latent.astype(BF16)) * slope[frame, row]
                 grads[-1].append(steps(value.astype(BF16)))
         left = jnp.concatenate(
@@ -398,10 +429,6 @@
         factors = block_of(gathered, len(spots), part)
         store(dot(factors[:, : 3 * latents], inner))
 
-    mine = lax.axis_index("slab") % 2
-    keep[...] = scratch[:, mine]
-    send[...] = scratch[:, 1 - mine].astype(BF16)
-
 
 def fold_kernel(pieces, out):
     taps, share, outs = out.shape
@@ -447,30 +474,37 @@
     frames, rows, part, columns = tile.shape
     channels, latents = proj.shape[1], proj.shape[2]
     share = channels // slabs
-    chan = lax.axis_index("chan")
-    offset = chan * part
     scale = 1.0 / math.sqrt(frames * rows * slabs * columns)
-    splits = peers // (frames * rows)
-    span = channels // splits
+    span = channels // 2
+    by_tap = kern[0].transpose(1, 0, 2)
 
     above, below = both_ways(tile, tile, "slab")
     proj_t = proj[0].T
     height = (frames * (rows + 2) + 1) * part + latents
-    sent, own, proj_out = call(
+    middle, extra, direct, proj_out, taps_out = call(
+        prepare_kernel,
+        (
+            shape(tile.shape, BF16),
+            shape((part, columns), BF16),
+            shape((frames * rows, latents, columns), BF16),
+            shape((part, latents), BF16),
+            shape((9 * part, channels), BF16),
+        ),
+        [VMEM] * 3 + [HBM],
+        [pltpu.VMEM((9, channels, columns), BF16), pltpu.SemaphoreType.DMA],
+    )(tile, taps[0], proj_t, by_tap)
+    sent, own = call(
         mix_kernel,
         (
-            shape((peers, height, columns), BF16),
+            shape((peers // 2, height, columns), BF16),
             shape((frames, rows + 2, part, columns), BF16),
-            shape((part, latents), BF16),
         ),
-        [VMEM] * 5,
-    )(tile, above, below, taps[0], proj_t)
-    gathered = lax.all_to_all(sent, "chan", 0, 0)
-
-    by_tap = kern[0].transpose(1, 0, 2)
-    held = lax.dynamic_slice_in_dim(by_tap, chan % splits * span, span, 2)
-    out_cols = lax.dynamic_slice_in_dim(kern[0], offset, part, 2)
-    taps_out = out_cols.transpose(1, 2, 0).reshape(9 * part, channels)
+        [VMEM] * 6,
+    )(above, below, taps[0], middle, extra, direct)
+    groups = [[2 * chip + core for chip in range(peers // 2)] for core in range(2)]
+    mine = lax.all_to_all(sent, "chan", 0, 0, axis_index_groups=groups)
+    theirs = lax.ppermute(mine, "chan", [(i, i ^ 1) for i in range(peers)])
+
     tile_shape = (frames, rows, part, columns)
     latent_shape = (both, latents, columns)
     terms = 27 * latents
@@ -484,36 +518,37 @@
             shape((terms, span), BF16),
             shape((span, terms), BF16),
         ),
-        [VMEM] * 5,
-    )(gathered, taps_out, tile, proj_t, held)
+        [VMEM] * 5 + [HBM],
+        [pltpu.VMEM((9, channels, span), BF16), pltpu.SemaphoreType.DMA],
+    )(mine, theirs, taps_out, tile, proj_t, by_tap)
 
     arrived = lax.all_to_all(sent, ("chan", "pipe"), 0, 0)
-    arrived = arrived.reshape(peers, 2, latents, columns)[: frames * rows * splits, 0]
-    arrived = arrived.reshape(frames, rows, splits, latents, columns)
+    arrived = arrived.reshape(peers, 2, latents, columns)[: frames * rows * 2, 0]
+    arrived = arrived.reshape(frames, rows, 2, latents, columns)
     mid = jnp.sum(arrived.astype(F32), axis=2).astype(BF16)
     low, high = both_ways(mid, mid, "slab")
     out, grad, sent = call(
         functools.partial(decode_kernel, scale),
         (shape(tile_shape, BF16), shape(tile_shape, BF16), shape(latent_shape, BF16)),
-        [VMEM] * 11,
+        [VMEM] * 12,
         [pltpu.VMEM((3, frames + 2, 3 * rows, latents, columns), BF16)],
     )(
-        low, mid, high, own, combo, wide_t, wide, gathered, proj_out, proj_t, encoded
+        low, mid, high, own, combo, wide_t, wide, mine, theirs, proj_out, proj_t,
+        encoded,
     )
 
     arrived = lax.all_to_all(sent, ("chan", "pipe"), 0, 0)
-    pairs = slabs // 2
+    near = 4
+    far = slabs // near
     lines = share * 9 * part // columns
-    send, keep = call(
-        grad_kernel,
-        (shape((pairs, lines, columns), BF16), shape((pairs, lines, columns), F32)),
-        [VMEM] * 8,
-        [pltpu.VMEM((pairs, 2, lines, columns), F32)],
-    )(arrived, slope, gathered, grad, low, mid, high, proj_out)
-    got = lax.ppermute(send, "slab", [(i, i ^ 1) for i in range(slabs)])
-    halved = (keep + got.astype(F32)).astype(BF16)
-    groups = [[2 * p + q for p in range(pairs)] for q in range(2)]
-    pieces = lax.all_to_all(halved, "slab", 0, 0, axis_index_groups=groups)
+    sent = call(grad_kernel, shape((near, far, lines, columns), BF16), [VMEM] * 9)(
+        arrived, slope, mine, theirs, grad, low, mid, high, proj_out
+    )
+    groups = [[near * i + j for j in range(near)] for i in range(far)]
+    pieces = lax.all_to_all(sent, "slab", 0, 0, axis_index_groups=groups)
+    partial = jnp.sum(pieces.astype(F32), axis=0).astype(BF16)
+    groups = [[near * i + j for i in range(far)] for j in range(near)]
+    pieces = lax.all_to_all(partial, "slab", 0, 0, axis_index_groups=groups)
     total = call(fold_kernel, shape((9, share, part), F32), [VMEM])(pieces)
     total = total.transpose(1, 0, 2)
     return out[None], total[None]

time: 151 us -> 142 us (0.940)
  the two profiles are of different devices: /device:TPU:120 before, /device:TPU:64 now
where the time goes in v4:
time: 142 us; the launch traced here: 141 us
  blocking collectives  102 us (72%)
  starting transfers between devices  15.2 us (11%)
  waiting for transfers between devices  12.8 us (9%)
  Pallas kernels  6.19 us (4%)
  local copies, waits for them, and re-layouts  4.59 us (3%)
    all_to_all x1, blocking collectives, on_device(): pieces = lax.all_to_all(partial, 'slab', 0, 0, axis_index_groups=groups)  51.8 us
    all_to_all x2, blocking collectives, on_device(): arrived = lax.all_to_all(sent, ('chan', 'pipe'), 0, 0)  23.4 us
    all_to_all x1, blocking collectives, on_device(): mine = lax.all_to_all(sent, 'chan', 0, 0, axis_index_groups=groups)  15.2 us
    all_to_all x1, blocking collectives, on_device(): pieces = lax.all_to_all(sent, 'slab', 0, 0, axis_index_groups=groups)  11.5 us
    ppermute x2, waiting for transfers between devices, both_ways(): lax.ppermute(high_side, axis, forward)  10.4 us
    ppermute x2, starting transfers between devices, both_ways(): lax.ppermute(low_side, axis, backward)  7.5 us
    ppermute x2, starting transfers between devices, both_ways(): lax.ppermute(high_side, axis, forward)  5.75 us
    unnamed x14, local copies, waits for them, and re-layouts  4.53 us
  transfers between devices with their start and end apart: 5, of which 3 were waited for; matrix products, arithmetic and copies ran while one was open for 0% of the time, Pallas kernels for 1%

profile of v4, /device:TPU:64, one launch (start us, length us, event | category | flops | bytes accessed | tf_op | source)
XLA Modules:
  0.0 141.5 jit_solution(5335621063216628455)
XLA Ops:
  0.6 2.0 %collective-permute-start.1 = (bf16[3,2,32,128]{3,2,1,0:T(8,128)(2,1)}, bf16[3,2,32,128]{3,2,1,0:T(8,128)(2,1)S(1)}, u32[]{:S(2)}, u32[]{:S(2)}) collective-permute-start(bf16[3,2,32,128]{3,2,1,0:T(8,128)(2,1)} %bitcast.16), channel_id=1, source_target_pairs={{32,0},{64,32},{96,64},{128,96},{160,128},{192,160},{224,192},{256... | collective-permute-start | bytes 147464 | tf_op jit(solution)/shard_map/ppermute | solution.py:465
  2.7 3.8 %collective-permute-start = (bf16[3,2,32,128]{3,2,1,0:T(8,128)(2,1)}, bf16[3,2,32,128]{3,2,1,0:T(8,128)(2,1)S(1)}, u32[]{:S(2)}, u32[]{:S(2)}) collective-permute-start(bf16[3,2,32,128]{3,2,1,0:T(8,128)(2,1)} %bitcast.17), channel_id=1, source_target_pairs={{0,32},{32,64},{64,96},{96,128},{128,160},{160,192},{192,224},{224... | collective-permute-start | bytes 147464 | tf_op jit(solution)/shard_map/ppermute | solution.py:465
  6.5 0.0 copy-start
  6.5 2.3 %copy-done = bf16[1,512,9,512]{3,1,2,0:T(8,128)(2,1)S(1)} copy-done((bf16[1,512,9,512]{3,1,2,0:T(8,128)(2,1)S(1)}, bf16[1,512,9,512]{3,1,2,0:T(8,128)(2,1)}, u32[]{:S(2)}) %copy-start) | copy-done | bytes 4718616
  8.8 0.0 copy-start.2
  8.8 0.8 copy-done.2
  9.6 0.0 copy-start.4
  9.6 0.7 copy-done.4
  10.3 0.0 copy-start.6
  10.3 0.7 copy-done.6
  11.0 0.0 copy-start.1
  11.0 0.0 copy-start.3
  11.0 0.0 copy-start.5
  11.0 1.9 %shard_map.59 = (bf16[3,2,32,128]{3,2,1,0:T(8,128)(2,1)S(1)}, bf16[32,128]{1,0:T(8,128)(2,1)S(1)}, bf16[6,16,128]{2,1,0:T(8,128)(2,1)S(1)}, bf16[32,16]{1,0:T(8,128)(2,1)S(1)}, bf16[288,512]{1,0:T(8,128)(2,1)S(1)}) custom-call(bf16[3,2,32,128]{3,2,1,0:T(8,128)(2,1)S(1)} %bitcast.18, bf16[3,32]{1,0:T(4,128)(2,1)S(1)} %bitcast.23, ...), custom_call_target="tpu_custom_call" | custom-call | tf_op jit(solution)/shard_map/pallas_call | solution.py:484
  13.0 0.0 collective-permute-done.1.high
  13.0 6.6 %collective-permute-done.low = bf16[3,2,32,128]{3,2,1,0:T(8,128)(2,1)S(1)} collective-permute-done((bf16[3,2,32,128]{3,2,1,0:T(8,128)(2,1)}, bf16[3,2,32,128]{3,2,1,0:T(8,128)(2,1)S(1)}, u32[]{:S(2)}, u32[]{:S(2)}) %collective-permute-start) | collective-permute-done | bytes 49184 | tf_op jit(solution)/shard_map/ppermute | solution.py:465
  19.6 0.1 shard_map.60
  19.7 15.2 %all_to_all.25.mine = bf16[8,432,128]{2,1,0:T(8,128)(2,1)S(1)} all-to-all(bf16[8,432,128]{2,1,0:T(8,128)(2,1)S(1)} %get-tuple-element.21), channel_id=1, replica_groups={{0,4,8,12,16,20,24,28},{2,6,10,14,18,22,26,30},{1,5,9,13,17,21,25,29},{..., dimensions={0} | all-to-all | bytes 1769472 | tf_op jit(solution)/shard_map/all_to_all | solution.py:505
  34.9 1.9 %collective-permute-start.2 = (bf16[8,432,128]{2,1,0:T(8,128)(2,1)S(1)}, bf16[8,432,128]{2,1,0:T(8,128)(2,1)S(1)}, u32[]{:S(2)}, u32[]{:S(2)}) collective-permute-start(bf16[8,432,128]{2,1,0:T(8,128)(2,1)S(1)} %all_to_all.25.mine), channel_id=1, source_target_pairs={{0,2},{2,0},{4,6},{6,4},{8,10},{10,8},{12,14},{14,12},{16,18},{18,... | collective-permute-start | bytes 2654216 | tf_op jit(solution)/shard_map/ppermute | solution.py:506
  36.8 2.4 %collective-permute-done.2.theirs = bf16[8,432,128]{2,1,0:T(8,128)(2,1)S(1)} collective-permute-done((bf16[8,432,128]{2,1,0:T(8,128)(2,1)S(1)}, bf16[8,432,128]{2,1,0:T(8,128)(2,1)S(1)}, u32[]{:S(2)}, u32[]{:S(2)}) %collective-permute-start.2) | collective-permute-done | bytes 884768 | tf_op jit(solution)/shard_map/ppermute | solution.py:506
  39.2 0.0 copy-done.1
  39.2 0.0 copy-done.3
  39.2 0.0 copy-done.5
  39.3 1.6 %shard_map.61 = (bf16[3,2,32,128]{3,2,1,0:T(8,128)(2,1)S(1)}, f32[3,2,32,128]{3,2,1,0:T(8,128)S(1)}, bf16[32,16,128]{2,1,0:T(8,128)(2,1)S(1)}, bf16[288,128]{1,0...) custom-call(bf16[8,432,128]{2,1,0:T(8,128)(2,1)S(1)} %all_to_all.25.mine, ...), custom_call_target="tpu_custom_call" | custom-call | tf_op jit(solution)/shard_map/pallas_call | solution.py:511
  40.9 11.1 %all_to_all.26 = bf16[32,16,128]{2,1,0:T(8,128)(2,1)S(1)} all-to-all(bf16[32,16,128]{2,1,0:T(8,128)(2,1)S(1)} %get-tuple-element.23), channel_id=1, replica_groups=mesh['slab'=32,'chan'=16,'pipe'=2] {'chan','pipe'}, dimensions={0} | all-to-all | bytes 262144 | tf_op jit(solution)/shard_map/all_to_all | solution.py:525
  52.0 5.5 %collective-permute-start.4 = (bf16[3,2,16,128]{3,2,1,0:T(8,128)(2,1)S(1)}, bf16[3,2,16,128]{3,2,1,0:T(8,128)(2,1)S(1)}, u32[]{:S(2)}, u32[]{:S(2)}) collective-permute-start(bf16[3,2,16,128]{3,2,1,0:T(8,128)(2,1)S(1)} %reduce_sum.24.mid), channel_id=1, source_target_pairs={{32,0},{64,32},{96,64},{128,96},{160,128},{192,160},{224,192},{256... | collective-permute-start | bytes 73736 | tf_op jit(solution)/shard_map/ppermute | solution.py:465
  57.5 1.9 %collective-permute-start.3 = (bf16[3,2,16,128]{3,2,1,0:T(8,128)(2,1)S(1)}, bf16[3,2,16,128]{3,2,1,0:T(8,128)(2,1)S(1)}, u32[]{:S(2)}, u32[]{:S(2)}) collective-permute-start(bf16[3,2,16,128]{3,2,1,0:T(8,128)(2,1)S(1)} %reduce_sum.24.mid), channel_id=1, source_target_pairs={{0,32},{32,64},{64,96},{96,128},{128,160},{160,192},{192,224},{224... | collective-permute-start | bytes 73736 | tf_op jit(solution)/shard_map/ppermute | solution.py:465
  59.4 0.0 collective-permute-done.4.high
  59.4 3.8 %collective-permute-done.3.low = bf16[3,2,16,128]{3,2,1,0:T(8,128)(2,1)S(1)} collective-permute-done((bf16[3,2,16,128]{3,2,1,0:T(8,128)(2,1)S(1)}, bf16[3,2,16,128]{3,2,1,0:T(8,128)(2,1)S(1)}, u32[]{:S(2)}, u32[]{:S(2)}) %collective-permute-start.3) | collective-permute-done | bytes 24608 | tf_op jit(solution)/shard_map/ppermute | solution.py:465
  63.2 0.6 shard_map.62
  63.9 12.3 %all_to_all.27.arrived = bf16[32,16,128]{2,1,0:T(8,128)(2,1)S(1)} all-to-all(bf16[32,16,128]{2,1,0:T(8,128)(2,1)S(1)} %get-tuple-element.31), channel_id=1, replica_groups=mesh['slab'=32,'chan'=16,'pipe'=2] {'chan','pipe'}, dimensions={0} | all-to-all | bytes 262144 | tf_op jit(solution)/shard_map/all_to_all | solution.py:540
  76.1 1.2 shard_map.63
  77.4 11.5 %all_to_all.28 = bf16[4,8,36,128]{3,1,2,0:T(8,128)(2,1)S(1)} all-to-all(bf16[4,8,36,128]{3,1,2,0:T(8,128)(2,1)S(1)} %copy.7), channel_id=1, replica_groups={{0,32,64,96},{128,160,192,224},{256,288,320,352},{384,416,448,480},{512..., dimensions={0} | all-to-all | bytes 589824 | tf_op jit(solution)/shard_map/all_to_all | solution.py:548
  88.9 51.8 %all_to_all.29.pieces = bf16[8,36,128]{2,1,0:T(8,128)(2,1)S(1)} all-to-all(bf16[8,36,128]{2,1,0:T(8,128)(2,1)S(1)} %copy.8), channel_id=1, replica_groups={{0,128,256,384,512,640,768,896},{32,160,288,416,544,672,800,928},{64,19..., dimensions={0} | all-to-all | bytes 147456 | tf_op jit(solution)/shard_map/all_to_all | solution.py:551
  140.8 0.7 shard_map.64
  (5 shorter events, 0.1 us)
Async XLA Ops:
  0.6 12.3 %collective-permute-start.1 = (bf16[3,2,32,128]{3,2,1,0:T(8,128)(2,1)}, bf16[3,2,32,128]{3,2,1,0:T(8,128)(2,1)S(1)}, u32[]{:S(2)}, u32[]{:S(2)}) collective-permute-start(bf16[3,2,32,128]{3,2,1,0:T(8,128)(2,1)} %bitcast.16), channel_id=1, source_target_pairs={{32,0},{64,32},{96,64},{128,96},{160,128},{192,160},{224,192},{256... | collective-permute-start | bytes 147464 | tf_op jit(solution)/shard_map/ppermute | solution.py:465
  2.7 16.9 %collective-permute-start = (bf16[3,2,32,128]{3,2,1,0:T(8,128)(2,1)}, bf16[3,2,32,128]{3,2,1,0:T(8,128)(2,1)S(1)}, u32[]{:S(2)}, u32[]{:S(2)}) collective-permute-start(bf16[3,2,32,128]{3,2,1,0:T(8,128)(2,1)} %bitcast.17), channel_id=1, source_target_pairs={{0,32},{32,64},{64,96},{96,128},{128,160},{160,192},{192,224},{224... | collective-permute-start | bytes 147464 | tf_op jit(solution)/shard_map/ppermute | solution.py:465
  6.5 2.3 %copy-start = (bf16[1,512,9,512]{3,1,2,0:T(8,128)(2,1)S(1)}, bf16[1,512,9,512]{3,1,2,0:T(8,128)(2,1)}, u32[]{:S(2)}) copy-start(bf16[1,512,9,512]{3,1,2,0:T(8,128)(2,1)} %param.6) | copy-start | bytes 14155780
  8.8 0.8 copy-start.2
  9.6 0.7 copy-start.4
  10.3 0.7 copy-start.6
  11.0 28.2 %copy-start.1 = (bf16[1,512,9,512]{3,1,2,0:T(8,128)(2,1)S(1)}, bf16[1,512,9,512]{3,1,2,0:T(8,128)(2,1)}, u32[]{:S(2)}) copy-start(bf16[1,512,9,512]{3,1,2,0:T(8,128)(2,1)} %param.6) | copy-start | bytes 14155780
  11.0 28.2 %copy-start.3 = (bf16[1,3,2,32,128]{4,3,2,1,0:T(8,128)(2,1)S(1)}, bf16[1,3,2,32,128]{4,3,2,1,0:T(8,128)(2,1)}, u32[]{:S(2)}) copy-start(bf16[1,3,2,32,128]{4,3,2,1,0:T(8,128)(2,1)} %param.4) | copy-start | bytes 147460
  11.0 28.2 %copy-start.5 = (bf16[1,512,16]{1,2,0:T(8,128)(2,1)S(1)}, bf16[1,512,16]{1,2,0:T(8,128)(2,1)}, u32[]{:S(2)}) copy-start(bf16[1,512,16]{1,2,0:T(8,128)(2,1)} %param.7) | copy-start | bytes 49156
  34.9 4.3 %collective-permute-start.2 = (bf16[8,432,128]{2,1,0:T(8,128)(2,1)S(1)}, bf16[8,432,128]{2,1,0:T(8,128)(2,1)S(1)}, u32[]{:S(2)}, u32[]{:S(2)}) collective-permute-start(bf16[8,432,128]{2,1,0:T(8,128)(2,1)S(1)} %all_to_all.25.mine), channel_id=1, source_target_pairs={{0,2},{2,0},{4,6},{6,4},{8,10},{10,8},{12,14},{14,12},{16,18},{18,... | collective-permute-start | bytes 2654216 | tf_op jit(solution)/shard_map/ppermute | solution.py:506
  52.0 7.4 %collective-permute-start.4 = (bf16[3,2,16,128]{3,2,1,0:T(8,128)(2,1)S(1)}, bf16[3,2,16,128]{3,2,1,0:T(8,128)(2,1)S(1)}, u32[]{:S(2)}, u32[]{:S(2)}) collective-permute-start(bf16[3,2,16,128]{3,2,1,0:T(8,128)(2,1)S(1)} %reduce_sum.24.mid), channel_id=1, source_target_pairs={{32,0},{64,32},{96,64},{128,96},{160,128},{192,160},{224,192},{256... | collective-permute-start | bytes 73736 | tf_op jit(solution)/shard_map/ppermute | solution.py:465
  57.5 5.7 %collective-permute-start.3 = (bf16[3,2,16,128]{3,2,1,0:T(8,128)(2,1)S(1)}, bf16[3,2,16,128]{3,2,1,0:T(8,128)(2,1)S(1)}, u32[]{:S(2)}, u32[]{:S(2)}) collective-permute-start(bf16[3,2,16,128]{3,2,1,0:T(8,128)(2,1)S(1)} %reduce_sum.24.mid), channel_id=1, source_target_pairs={{0,32},{32,64},{64,96},{96,128},{128,160},{160,192},{192,224},{224... | collective-permute-start | bytes 73736 | tf_op jit(solution)/shard_map/ppermute | solution.py:465

commit v5 on v4

--- a/solution.py
+++ b/solution.py
@@ -12,7 +12,6 @@
 BF16 = jnp.bfloat16
 VMEM = pl.BlockSpec(memory_space=pltpu.VMEM)
 HBM = pl.BlockSpec(memory_space=pltpu.HBM)
-PARAMS = pltpu.CompilerParams(vmem_limit_bytes=40 * 1024 * 1024)
 
 
 def dot(a, b):
@@ -152,20 +151,16 @@
 
 
 def encode_kernel(
-    mine, theirs, taps_out, tile, proj_t, kern, out, slope, sent, combo, wide_t, wide, held, done
+    mine, theirs, taps_out, tile, proj_t, kern, out, slope, sent, combo, wide_t, wide
 ):
     frames, rows, outs, columns = tile.shape
     gathered = (mine, theirs)
     part = outs
     latents = proj_t.shape[0]
     deep = 3 * latents
-    span = held.shape[2]
+    span = wide.shape[0]
     encoder, chan = lax.axis_index("pipe") == 0, lax.axis_index("chan")
     row_at, turn = chan // 2, chan % 2
-    fetch = pltpu.make_async_copy(
-        kern.at[:, :, pl.ds(pl.multiple_of(turn * span, span), span)], held, done
-    )
-    fetch.start()
     active = row_at < frames * rows
 
     @pl.when(encoder)
@@ -185,8 +180,6 @@
                 out[frame, row] = (tile[frame, row].astype(F32) + summed * sigma).astype(BF16)
                 slope[frame, row] = sigma * (1.0 + summed * (1.0 - sigma))
 
-    fetch.wait()
-
     @pl.when(jnp.logical_and(encoder, active))
     def _():
         base = (row_at // rows) * (rows + 2) + row_at % rows
@@ -195,7 +188,7 @@
         for b in range(3):
             total = None
             for a in range(3):
-                term = dot(turned[a], held[3 * a + b])
+                term = dot(turned[a], kern[3 * a + b])
                 total = term if total is None else total + term
             if b != 1:
                 line = lax.broadcasted_iota(jnp.int32, total.shape, 0)
@@ -204,13 +197,13 @@
                 total = jnp.where(line == edge, 0.0, moved)
             summed = total if summed is None else summed + total
         bent = (summed * logistic(summed)).astype(BF16)
-        latent = dot_nt(pick(proj_t, turn, span), bent)
+        latent = dot_nt(proj_t[...], bent)
         at = (frames * (rows + 2) + 1) * part
-        direct = jnp.zeros_like(latent)
         for chip in range(mine.shape[0]):
             for half in gathered:
-                direct = direct + half[chip, at : at + latents].astype(F32)
-        latent = (latent + jnp.where(turn == 0, direct, 0.0)).astype(BF16)
+                latent = latent + half[chip, at : at + latents].astype(F32)
+        few = latents // 2
+        latent = jnp.where(turn == 0, latent[:few], latent[few:]).astype(BF16)
         for peer in range(sent.shape[0]):
             sent[peer] = latent
 
@@ -224,7 +217,8 @@
         combo[...] = dot(taps_out[...], factors).astype(BF16)
         factors_t = factors.astype(F32).T.astype(BF16)[:deep]
         for tap in range(9):
-            wide_t[tap * deep : (tap + 1) * deep] = dot(factors_t, held[tap]).astype(BF16)
+            block = pick(kern.at[tap], turn, span)
+            wide_t[tap * deep : (tap + 1) * deep] = dot(factors_t, block).astype(BF16)
         wide[...] = wide_t[...].astype(F32).T.astype(BF16)
 
 
@@ -447,14 +441,14 @@
     )
 
 
-def call(kernel, shapes, specs, scratch=()):
+def call(kernel, shapes, specs, scratch=(), limit=40):
     return pl.pallas_call(
         kernel,
         out_shape=shapes,
         in_specs=specs,
         out_specs=jax.tree.map(lambda _: VMEM, shapes),
         scratch_shapes=list(scratch),
-        compiler_params=PARAMS,
+        compiler_params=pltpu.CompilerParams(vmem_limit_bytes=limit * 1024 * 1024),
     )
 
 
@@ -492,6 +486,7 @@
         ),
         [VMEM] * 3 + [HBM],
         [pltpu.VMEM((9, channels, columns), BF16), pltpu.SemaphoreType.DMA],
+        limit=52,
     )(tile, taps[0], proj_t, by_tap)
     sent, own = call(
         mix_kernel,
@@ -513,19 +508,17 @@
         (
             shape(tile_shape, BF16),
             shape(tile_shape, F32),
-            shape(latent_shape, BF16),
+            shape((both, latents // 2, columns), BF16),
             shape((9 * part, columns), BF16),
             shape((terms, span), BF16),
             shape((span, terms), BF16),
         ),
-        [VMEM] * 5 + [HBM],
-        [pltpu.VMEM((9, channels, span), BF16), pltpu.SemaphoreType.DMA],
+        [VMEM] * 6,
     )(mine, theirs, taps_out, tile, proj_t, by_tap)
 
     arrived = lax.all_to_all(sent, ("chan", "pipe"), 0, 0)
-    arrived = arrived.reshape(peers, 2, latents, columns)[: frames * rows * 2, 0]
-    arrived = arrived.reshape(frames, rows, 2, latents, columns)
-    mid = jnp.sum(arrived.astype(F32), axis=2).astype(BF16)
+    arrived = arrived.reshape(peers, 2, latents // 2, columns)[: frames * rows * 2, 0]
+    mid = arrived.reshape(frames, rows, latents, columns)
     low, high = both_ways(mid, mid, "slab")
     out, grad, sent = call(
         functools.partial(decode_kernel, scale),

time: 142 us -> 141 us (level)
  local copies, waits for them, and re-layouts: 4.59 us -> 2.26 us
    unnamed x14 -> x8, local copies, waits for them, and re-layouts: 4.53 us -> 2.2 us
  transfers between devices with their start and end apart: 5 -> 5, of which waited for: 3 -> 3; matrix products, arithmetic and copies ran while one was open for 0% -> 0% of each run, Pallas kernels for 1% -> 2%
where the time goes in v5:
time: 141 us; the launch traced here: 140 us
  blocking collectives  101 us (72%)
  starting transfers between devices  14.7 us (10%)
  waiting for transfers between devices  14.2 us (10%)
  Pallas kernels  7.36 us (5%)
  local copies, waits for them, and re-layouts  2.26 us (2%)
    all_to_all x1, blocking collectives, on_device(): pieces = lax.all_to_all(partial, 'slab', 0, 0, axis_index_groups=groups)  51.8 us
    all_to_all x2, blocking collectives, on_device(): arrived = lax.all_to_all(sent, ('chan', 'pipe'), 0, 0)  22.9 us
    all_to_all x1, blocking collectives, on_device(): mine = lax.all_to_all(sent, 'chan', 0, 0, axis_index_groups=groups)  14.5 us
    ppermute x2, waiting for transfers between devices, both_ways(): lax.ppermute(high_side, axis, forward)  11.8 us
    all_to_all x1, blocking collectives, on_device(): pieces = lax.all_to_all(sent, 'slab', 0, 0, axis_index_groups=groups)  11.5 us
    ppermute x2, starting transfers between devices, both_ways(): lax.ppermute(low_side, axis, backward)  7.06 us
    ppermute x2, starting transfers between devices, both_ways(): lax.ppermute(high_side, axis, forward)  5.75 us
    pallas_call x1, Pallas kernels, on_device(): call(prepare_kernel, (shape(tile.shape, BF16), shape((part, columns), BF1...  2.89 us
  transfers between devices with their start and end apart: 5, of which 3 were waited for; matrix products, arithmetic and copies ran while one was open for 0% of the time, Pallas kernels for 2%

profile of v5, /device:TPU:64, one launch (start us, length us, event | category | flops | bytes accessed | tf_op | source)
XLA Modules:
  0.0 140.1 jit_solution(11473484354694640963)
XLA Ops:
  0.6 0.0 copy-start
  0.6 2.3 %collective-permute-start.1 = (bf16[3,2,32,128]{3,2,1,0:T(8,128)(2,1)}, bf16[3,2,32,128]{3,2,1,0:T(8,128)(2,1)S(1)}, u32[]{:S(2)}, u32[]{:S(2)}) collective-permute-start(bf16[3,2,32,128]{3,2,1,0:T(8,128)(2,1)} %bitcast.22), channel_id=1, source_target_pairs={{32,0},{64,32},{96,64},{128,96},{160,128},{192,160},{224,192},{256... | collective-permute-start | bytes 147464 | tf_op jit(solution)/shard_map/ppermute | solution.py:459
  2.9 3.8 %collective-permute-start = (bf16[3,2,32,128]{3,2,1,0:T(8,128)(2,1)}, bf16[3,2,32,128]{3,2,1,0:T(8,128)(2,1)S(1)}, u32[]{:S(2)}, u32[]{:S(2)}) collective-permute-start(bf16[3,2,32,128]{3,2,1,0:T(8,128)(2,1)} %bitcast.23), channel_id=1, source_target_pairs={{0,32},{32,64},{64,96},{96,128},{128,160},{160,192},{192,224},{224... | collective-permute-start | bytes 147464 | tf_op jit(solution)/shard_map/ppermute | solution.py:459
  6.8 0.0 copy-start.1
  6.8 0.8 copy-done.1
  7.6 0.0 copy-start.2
  7.6 0.7 copy-done.2
  8.3 0.0 copy-start.3
  8.3 0.7 copy-done.3
  9.0 2.9 %shard_map.59 = (bf16[3,2,32,128]{3,2,1,0:T(8,128)(2,1)S(1)}, bf16[32,128]{1,0:T(8,128)(2,1)S(1)}, bf16[6,16,128]{2,1,0:T(8,128)(2,1)S(1)}, bf16[32,16]{1,0:T(8,128)(2,1)S(1)}, bf16[288,512]{1,0:T(8,128)(2,1)S(1)}) custom-call(bf16[3,2,32,128]{3,2,1,0:T(8,128)(2,1)S(1)} %bitcast.24, bf16[3,32]{1,0:T(4,128)(2,1)S(1)} %bitcast.29, ...), custom_call_target="tpu_custom_call" | custom-call | tf_op jit(solution)/shard_map/pallas_call | solution.py:478
  11.9 0.0 collective-permute-done.1.high
  11.9 8.0 %collective-permute-done.low = bf16[3,2,32,128]{3,2,1,0:T(8,128)(2,1)S(1)} collective-permute-done((bf16[3,2,32,128]{3,2,1,0:T(8,128)(2,1)}, bf16[3,2,32,128]{3,2,1,0:T(8,128)(2,1)S(1)}, u32[]{:S(2)}, u32[]{:S(2)}) %collective-permute-start) | collective-permute-done | bytes 49184 | tf_op jit(solution)/shard_map/ppermute | solution.py:459
  19.9 0.1 shard_map.60
  20.0 14.5 %all_to_all.25.mine = bf16[8,432,128]{2,1,0:T(8,128)(2,1)S(1)} all-to-all(bf16[8,432,128]{2,1,0:T(8,128)(2,1)S(1)} %get-tuple-element.21), channel_id=1, replica_groups={{0,4,8,12,16,20,24,28},{2,6,10,14,18,22,26,30},{1,5,9,13,17,21,25,29},{..., dimensions={0} | all-to-all | bytes 1769472 | tf_op jit(solution)/shard_map/all_to_all | solution.py:500
  34.5 1.9 %collective-permute-start.2 = (bf16[8,432,128]{2,1,0:T(8,128)(2,1)S(1)}, bf16[8,432,128]{2,1,0:T(8,128)(2,1)S(1)}, u32[]{:S(2)}, u32[]{:S(2)}) collective-permute-start(bf16[8,432,128]{2,1,0:T(8,128)(2,1)S(1)} %all_to_all.25.mine), channel_id=1, source_target_pairs={{0,2},{2,0},{4,6},{6,4},{8,10},{10,8},{12,14},{14,12},{16,18},{18,... | collective-permute-start | bytes 2654216 | tf_op jit(solution)/shard_map/ppermute | solution.py:501
  36.5 2.4 %collective-permute-done.2.theirs = bf16[8,432,128]{2,1,0:T(8,128)(2,1)S(1)} collective-permute-done((bf16[8,432,128]{2,1,0:T(8,128)(2,1)S(1)}, bf16[8,432,128]{2,1,0:T(8,128)(2,1)S(1)}, u32[]{:S(2)}, u32[]{:S(2)}) %collective-permute-start.2) | collective-permute-done | bytes 884768 | tf_op jit(solution)/shard_map/ppermute | solution.py:501
  38.8 0.0 copy-done
  38.8 1.8 %shard_map.61 = (bf16[3,2,32,128]{3,2,1,0:T(8,128)(2,1)S(1)}, f32[3,2,32,128]{3,2,1,0:T(8,128)S(1)}, bf16[32,8,128]{2,1,0:T(8,128)(2,1)S(1)}, bf16[288,128]{1,0:...) custom-call(bf16[8,432,128]{2,1,0:T(8,128)(2,1)S(1)} %all_to_all.25.mine, ...), custom_call_target="tpu_custom_call" | custom-call | tf_op jit(solution)/shard_map/pallas_call | solution.py:506
  40.7 10.6 %all_to_all.26 = bf16[32,8,128]{2,1,0:T(8,128)(2,1)S(1)} all-to-all(bf16[32,8,128]{2,1,0:T(8,128)(2,1)S(1)} %get-tuple-element.23), channel_id=1, replica_groups=mesh['slab'=32,'chan'=16,'pipe'=2] {'chan','pipe'}, dimensions={0} | all-to-all | bytes 131072 | tf_op jit(solution)/shard_map/all_to_all | solution.py:519
  51.3 4.8 %collective-permute-start.4 = (bf16[3,2,16,128]{3,2,1,0:T(8,128)(2,1)S(1)}, bf16[3,2,16,128]{3,2,1,0:T(8,128)(2,1)S(1)}, u32[]{:S(2)}, u32[]{:S(2)}) collective-permute-start(bf16[3,2,16,128]{3,2,1,0:T(8,128)(2,1)S(1)} %bitcast.18), channel_id=1, source_target_pairs={{32,0},{64,32},{96,64},{128,96},{160,128},{192,160},{224,192},{256... | collective-permute-start | bytes 73736 | tf_op jit(solution)/shard_map/ppermute | solution.py:459
  56.1 1.9 %collective-permute-start.3 = (bf16[3,2,16,128]{3,2,1,0:T(8,128)(2,1)S(1)}, bf16[3,2,16,128]{3,2,1,0:T(8,128)(2,1)S(1)}, u32[]{:S(2)}, u32[]{:S(2)}) collective-permute-start(bf16[3,2,16,128]{3,2,1,0:T(8,128)(2,1)S(1)} %bitcast.19), channel_id=1, source_target_pairs={{0,32},{32,64},{64,96},{96,128},{128,160},{160,192},{192,224},{224... | collective-permute-start | bytes 73736 | tf_op jit(solution)/shard_map/ppermute | solution.py:459
  58.0 0.0 collective-permute-done.4.high
  58.0 3.8 %collective-permute-done.3.low = bf16[3,2,16,128]{3,2,1,0:T(8,128)(2,1)S(1)} collective-permute-done((bf16[3,2,16,128]{3,2,1,0:T(8,128)(2,1)S(1)}, bf16[3,2,16,128]{3,2,1,0:T(8,128)(2,1)S(1)}, u32[]{:S(2)}, u32[]{:S(2)}) %collective-permute-start.3) | collective-permute-done | bytes 24608 | tf_op jit(solution)/shard_map/ppermute | solution.py:459
  61.8 0.6 shard_map.62
  62.5 12.3 %all_to_all.27.arrived = bf16[32,16,128]{2,1,0:T(8,128)(2,1)S(1)} all-to-all(bf16[32,16,128]{2,1,0:T(8,128)(2,1)S(1)} %get-tuple-element.31), channel_id=1, replica_groups=mesh['slab'=32,'chan'=16,'pipe'=2] {'chan','pipe'}, dimensions={0} | all-to-all | bytes 262144 | tf_op jit(solution)/shard_map/all_to_all | solution.py:533
  74.7 1.2 shard_map.63
  76.0 11.5 %all_to_all.28 = bf16[4,8,36,128]{3,1,2,0:T(8,128)(2,1)S(1)} all-to-all(bf16[4,8,36,128]{3,1,2,0:T(8,128)(2,1)S(1)} %copy.10), channel_id=1, replica_groups={{0,32,64,96},{128,160,192,224},{256,288,320,352},{384,416,448,480},{512..., dimensions={0} | all-to-all | bytes 589824 | tf_op jit(solution)/shard_map/all_to_all | solution.py:541
  87.5 51.8 %all_to_all.29.pieces = bf16[8,36,128]{2,1,0:T(8,128)(2,1)S(1)} all-to-all(bf16[8,36,128]{2,1,0:T(8,128)(2,1)S(1)} %copy.11), channel_id=1, replica_groups={{0,128,256,384,512,640,768,896},{32,160,288,416,544,672,800,928},{64,19..., dimensions={0} | all-to-all | bytes 147456 | tf_op jit(solution)/shard_map/all_to_all | solution.py:544
  139.3 0.7 shard_map.64
  (4 shorter events, 0.1 us)
Async XLA Ops:
  0.6 38.2 %copy-start = (bf16[1,512,9,512]{3,1,2,0:T(8,128)(2,1)S(1)}, bf16[1,512,9,512]{3,1,2,0:T(8,128)(2,1)}, u32[]{:S(2)}) copy-start(bf16[1,512,9,512]{3,1,2,0:T(8,128)(2,1)} %param.6) | copy-start | bytes 14155780
  0.6 11.2 %collective-permute-start.1 = (bf16[3,2,32,128]{3,2,1,0:T(8,128)(2,1)}, bf16[3,2,32,128]{3,2,1,0:T(8,128)(2,1)S(1)}, u32[]{:S(2)}, u32[]{:S(2)}) collective-permute-start(bf16[3,2,32,128]{3,2,1,0:T(8,128)(2,1)} %bitcast.22), channel_id=1, source_target_pairs={{32,0},{64,32},{96,64},{128,96},{160,128},{192,160},{224,192},{256... | collective-permute-start | bytes 147464 | tf_op jit(solution)/shard_map/ppermute | solution.py:459
  2.9 16.9 %collective-permute-start = (bf16[3,2,32,128]{3,2,1,0:T(8,128)(2,1)}, bf16[3,2,32,128]{3,2,1,0:T(8,128)(2,1)S(1)}, u32[]{:S(2)}, u32[]{:S(2)}) collective-permute-start(bf16[3,2,32,128]{3,2,1,0:T(8,128)(2,1)} %bitcast.23), channel_id=1, source_target_pairs={{0,32},{32,64},{64,96},{96,128},{128,160},{160,192},{192,224},{224... | collective-permute-start | bytes 147464 | tf_op jit(solution)/shard_map/ppermute | solution.py:459
  6.8 0.8 copy-start.1
  7.6 0.7 copy-start.2
  8.3 0.7 copy-start.3
  34.5 4.3 %collective-permute-start.2 = (bf16[8,432,128]{2,1,0:T(8,128)(2,1)S(1)}, bf16[8,432,128]{2,1,0:T(8,128)(2,1)S(1)}, u32[]{:S(2)}, u32[]{:S(2)}) collective-permute-start(bf16[8,432,128]{2,1,0:T(8,128)(2,1)S(1)} %all_to_all.25.mine), channel_id=1, source_target_pairs={{0,2},{2,0},{4,6},{6,4},{8,10},{10,8},{12,14},{14,12},{16,18},{18,... | collective-permute-start | bytes 2654216 | tf_op jit(solution)/shard_map/ppermute | solution.py:501
  51.3 6.7 %collective-permute-start.4 = (bf16[3,2,16,128]{3,2,1,0:T(8,128)(2,1)S(1)}, bf16[3,2,16,128]{3,2,1,0:T(8,128)(2,1)S(1)}, u32[]{:S(2)}, u32[]{:S(2)}) collective-permute-start(bf16[3,2,16,128]{3,2,1,0:T(8,128)(2,1)S(1)} %bitcast.18), channel_id=1, source_target_pairs={{32,0},{64,32},{96,64},{128,96},{160,128},{192,160},{224,192},{256... | collective-permute-start | bytes 73736 | tf_op jit(solution)/shard_map/ppermute | solution.py:459
  56.1 5.7 %collective-permute-start.3 = (bf16[3,2,16,128]{3,2,1,0:T(8,128)(2,1)S(1)}, bf16[3,2,16,128]{3,2,1,0:T(8,128)(2,1)S(1)}, u32[]{:S(2)}, u32[]{:S(2)}) collective-permute-start(bf16[3,2,16,128]{3,2,1,0:T(8,128)(2,1)S(1)} %bitcast.19), channel_id=1, source_target_pairs={{0,32},{32,64},{64,96},{96,128},{128,160},{160,192},{192,224},{224... | collective-permute-start | bytes 73736 | tf_op jit(solution)/shard_map/ppermute | solution.py:459

commit v6 on v5

--- a/solution.py
+++ b/solution.py
@@ -52,12 +52,11 @@
     return sums
 
 
-def block_of(pair, at, part, first=0, count=None):
+def block_of(pair, at, part):
     mine, theirs = pair
-    count = mine.shape[0] if count is None else count
+    count = mine.shape[0]
     rows = pl.ds(pl.multiple_of(at * part, part), part)
-    left = mine[pl.ds(first, count), rows]
-    right = theirs[pl.ds(first, count), rows]
+    left, right = mine[:, rows], theirs[:, rows]
     swap = lax.axis_index("chan") % 2 == 1
     even = jnp.where(swap, right, left)
     odd = jnp.where(swap, left, right)
@@ -89,16 +88,10 @@
     return mixed
 
 
-def prepare_kernel(
-    tile, taps, proj_t, kern, mid, extra, direct, proj_out, taps_out, held, done
-):
+def prepare_kernel(tile, taps, proj_t, mid, extra, direct, proj_out):
     frames, rows, part, columns = tile.shape
     latents = proj_t.shape[0]
     chan = lax.axis_index("chan")
-    across = columns // part
-    lanes = pl.ds(pl.multiple_of(chan // across * columns, columns), columns)
-    fetch = pltpu.make_async_copy(kern.at[:, :, lanes], held, done)
-    fetch.start()
     proj_back = pick(proj_t, chan, part)
     line = lax.broadcasted_iota(jnp.int32, (part, part), 0)
     lane = lax.broadcasted_iota(jnp.int32, (part, part), 1)
@@ -118,6 +111,15 @@
         for frame in range(frames):
             mid[frame, row] = mixed[frame]
             direct[frame * rows + row] = dot(proj_back, tile[frame, row]).astype(BF16)
+
+def turn_kernel(after, kern, taps_out, held, done):
+    columns = held.shape[2]
+    part = taps_out.shape[0] // 9
+    chan = lax.axis_index("chan")
+    across = columns // part
+    lanes = pl.ds(pl.multiple_of(chan // across * columns, columns), columns)
+    fetch = pltpu.make_async_copy(kern.at[:, :, lanes], held, done)
+    fetch.start()
     fetch.wait()
     for tap in range(9):
         block = held[tap].T
@@ -142,43 +144,25 @@
             for chip in range(chips):
                 sent[chip, at : at + part] = blocks[row]
     at = frames * (rows + 2) * part
+    encoder = lax.axis_index("pipe") == 0
+    blank = jnp.zeros((part - latents, columns), BF16)
     for chip in range(chips):
-        sent[chip, at : at + part] = extra[...]
-        if chip < frames * rows:
-            sent[chip, at + part : at + part + latents] = direct[chip]
-        else:
-            sent[chip, at + part : at + part + latents] = jnp.zeros((latents, columns), BF16)
+        first = direct[min(chip, frames * rows - 1)]
+        last = jnp.where(encoder, jnp.concatenate([first, blank], axis=0), extra[...])
+        sent[chip, at : at + part] = last
 
 
 def encode_kernel(
-    mine, theirs, taps_out, tile, proj_t, kern, out, slope, sent, combo, wide_t, wide
+    mine, theirs, taps_out, proj_t, kern, sent, combo, wide_t, wide, *, frames, rows
 ):
-    frames, rows, outs, columns = tile.shape
+    columns = mine.shape[2]
     gathered = (mine, theirs)
-    part = outs
+    part = taps_out.shape[0] // 9
     latents = proj_t.shape[0]
     deep = 3 * latents
-    span = wide.shape[0]
     encoder, chan = lax.axis_index("pipe") == 0, lax.axis_index("chan")
     row_at, turn = chan // 2, chan % 2
     active = row_at < frames * rows
-
-    @pl.when(encoder)
-    def _():
-        weights = taps_out[...]
-        for frame in range(frames):
-            products = []
-            for row in range(0, rows + 2, 2):
-                at = frame * (rows + 2) + row
-                pair = jnp.concatenate(
-                    [block_of(gathered, at + k, part) for k in range(2)], axis=1
-                )
-                both = dot(weights, pair)
-                products += [both[:, :columns], both[:, columns:]]
-            for row, summed in enumerate(tap_blocks(products, outs)):
-                sigma = logistic(summed)
-                out[frame, row] = (tile[frame, row].astype(F32) + summed * sigma).astype(BF16)
-                slope[frame, row] = sigma * (1.0 + summed * (1.0 - sigma))
 
     @pl.when(jnp.logical_and(encoder, active))
     def _():
@@ -198,7 +182,7 @@
             summed = total if summed is None else summed + total
         bent = (summed * logistic(summed)).astype(BF16)
         latent = dot_nt(proj_t[...], bent)
-        at = (frames * (rows + 2) + 1) * part
+        at = frames * (rows + 2) * part
         for chip in range(mine.shape[0]):
             for half in gathered:
                 latent = latent + half[chip, at : at + latents].astype(F32)
@@ -217,8 +201,7 @@
         combo[...] = dot(taps_out[...], factors).astype(BF16)
         factors_t = factors.astype(F32).T.astype(BF16)[:deep]
         for tap in range(9):
-            block = pick(kern.at[tap], turn, span)
-            wide_t[tap * deep : (tap + 1) * deep] = dot(factors_t, block).astype(BF16)
+            wide_t[tap * deep : (tap + 1) * deep] = dot(factors_t, kern[tap]).astype(BF16)
         wide[...] = wide_t[...].astype(F32).T.astype(BF16)
 
 
@@ -246,14 +229,14 @@
 
 
 def decode_kernel(
-    scale, low, mid, high, own, combo, wide_t, wide, mine, theirs, proj_out, proj_t, encoded,
-    out, grad, sent, bank
+    scale, low, mid, high, own, combo, wide_t, wide, mine, theirs, proj_out, proj_t, taps_out, tile,
+    out, slope, grad, sent, bank
 ):
     frames, rows, latents, columns = mid.shape
     outs = own.shape[2]
     part = outs
     deep = 3 * latents
-    span = wide.shape[0]
+    channels = wide.shape[0]
     gathered = (mine, theirs)
     encoder, chan = lax.axis_index("pipe") == 0, lax.axis_index("chan")
     row_at, turn = chan // 2, chan % 2
@@ -261,7 +244,20 @@
 
     @pl.when(encoder)
     def _():
-        out[...] = encoded[...]
+        weights = taps_out[...]
+        for frame in range(frames):
+            products = []
+            for row in range(0, rows + 2, 2):
+                at = frame * (rows + 2) + row
+                pair = jnp.concatenate(
+                    [block_of(gathered, at + k, part) for k in range(2)], axis=1
+                )
+                both = dot(weights, pair)
+                products += [both[:, :columns], both[:, columns:]]
+            for row, summed in enumerate(tap_blocks(products, outs)):
+                sigma = logistic(summed)
+                out[frame, row] = (tile[frame, row].astype(F32) + summed * sigma).astype(BF16)
+                slope[frame, row] = sigma * (1.0 + summed * (1.0 - sigma))
 
     @pl.when(jnp.logical_or(encoder, jnp.logical_not(active)))
     def _():
@@ -286,8 +282,8 @@
             for row, summed in enumerate(tap_blocks(products, outs)):
                 sigma = logistic(summed)
                 cotangent = own[frame, row + 1].astype(F32) * scale
-                slope = sigma * (1.0 + summed * (1.0 - sigma))
-                grad[frame, row] = (cotangent * slope).astype(BF16)
+                bend = sigma * (1.0 + summed * (1.0 - sigma))
+                grad[frame, row] = (cotangent * bend).astype(BF16)
                 lifted = dot(proj_out[...], mid[frame, row]).astype(BF16)
                 out[frame, row] = (lifted.astype(F32) + summed * sigma).astype(BF16)
 
@@ -300,10 +296,8 @@
                 for b in range(3):
                     bank[b, frame + 2, row] = shifted(value, b - 1).astype(BF16)
         frame_at, line = row_at // rows, row_at % rows
-        chips = mine.shape[0] // 2
-
         def channel_rows(frame, row):
-            return block_of(gathered, frame * (rows + 2) + row, part, turn * chips, chips)
+            return block_of(gathered, frame * (rows + 2) + row, part)
 
         columns_of = []
         for lag in range(3):
@@ -328,9 +322,9 @@
                 at = (3 * lag + a) * columns
                 value = summed[:, at : at + columns]
                 sigma = logistic(value)
-                slope = sigma * (1.0 + value * (1.0 - sigma))
+                bend = sigma * (1.0 + value * (1.0 - sigma))
                 cotangent = channel_rows(source, line - a + 2).astype(F32) * factor
-                slanted.append((cotangent * slope).astype(BF16))
+                slanted.append((cotangent * bend).astype(BF16))
                 weights.append(
                     jnp.concatenate(
                         [
@@ -341,10 +335,11 @@
                     )
                 )
         mixed = dot(jnp.concatenate(weights, axis=1), jnp.concatenate(slanted, axis=0))
-        latent = dot(pick(proj_t, turn, span), channel_rows(frame_at, line + 1)) * scale
+        latent = dot(proj_t[...], channel_rows(frame_at, line + 1)) * scale
         for b in range(3):
             latent = latent + shifted(mixed[b * latents : (b + 1) * latents], 1 - b)
-        latent = latent.astype(BF16)
+        few = latents // 2
+        latent = jnp.where(turn == 0, latent[:few], latent[few:]).astype(BF16)
         for peer in range(sent.shape[0]):
             sent[peer] = latent
 
@@ -397,7 +392,9 @@
             grads.append([])
             for row in range(rows):
                 at = 4 * (frame * rows + row)
-                latent = arrived[at + 1].astype(F32) + arrived[at + 3].astype(F32)
+                latent = jnp.concatenate(
+                    [arrived[at + 1].astype(F32), arrived[at + 3].astype(F32)], axis=0
+                )
                 value = dot(proj_out[...], latent.astype(BF16)) * slope[frame, row]
                 grads[-1].append(steps(value.astype(BF16)))
         left = jnp.concatenate(
@@ -469,25 +466,21 @@
     channels, latents = proj.shape[1], proj.shape[2]
     share = channels // slabs
     scale = 1.0 / math.sqrt(frames * rows * slabs * columns)
-    span = channels // 2
     by_tap = kern[0].transpose(1, 0, 2)
 
     above, below = both_ways(tile, tile, "slab")
     proj_t = proj[0].T
-    height = (frames * (rows + 2) + 1) * part + latents
-    middle, extra, direct, proj_out, taps_out = call(
+    height = (frames * (rows + 2) + 1) * part
+    middle, extra, direct, proj_out = call(
         prepare_kernel,
         (
             shape(tile.shape, BF16),
             shape((part, columns), BF16),
             shape((frames * rows, latents, columns), BF16),
             shape((part, latents), BF16),
-            shape((9 * part, channels), BF16),
         ),
-        [VMEM] * 3 + [HBM],
-        [pltpu.VMEM((9, channels, columns), BF16), pltpu.SemaphoreType.DMA],
-        limit=52,
-    )(tile, taps[0], proj_t, by_tap)
+        [VMEM] * 3,
+    )(tile, taps[0], proj_t)
     sent, own = call(
         mix_kernel,
         (
@@ -500,34 +493,44 @@
     mine = lax.all_to_all(sent, "chan", 0, 0, axis_index_groups=groups)
     theirs = lax.ppermute(mine, "chan", [(i, i ^ 1) for i in range(peers)])
 
+    taps_out = call(
+        turn_kernel,
+        shape((9 * part, channels), BF16),
+        [HBM] * 2,
+        [pltpu.VMEM((9, channels, columns), BF16), pltpu.SemaphoreType.DMA],
+        limit=51,
+    )(mine, by_tap)
     tile_shape = (frames, rows, part, columns)
-    latent_shape = (both, latents, columns)
+    latent_shape = (both, latents // 2, columns)
     terms = 27 * latents
-    encoded, slope, sent, combo, wide_t, wide = call(
-        encode_kernel,
+    sent, combo, wide_t, wide = call(
+        functools.partial(encode_kernel, frames=frames, rows=rows),
         (
-            shape(tile_shape, BF16),
-            shape(tile_shape, F32),
-            shape((both, latents // 2, columns), BF16),
+            shape(latent_shape, BF16),
             shape((9 * part, columns), BF16),
-            shape((terms, span), BF16),
-            shape((span, terms), BF16),
+            shape((terms, channels), BF16),
+            shape((channels, terms), BF16),
         ),
-        [VMEM] * 6,
-    )(mine, theirs, taps_out, tile, proj_t, by_tap)
+        [VMEM] * 5,
+    )(mine, theirs, taps_out, proj_t, by_tap)
 
     arrived = lax.all_to_all(sent, ("chan", "pipe"), 0, 0)
     arrived = arrived.reshape(peers, 2, latents // 2, columns)[: frames * rows * 2, 0]
     mid = arrived.reshape(frames, rows, latents, columns)
     low, high = both_ways(mid, mid, "slab")
-    out, grad, sent = call(
+    out, slope, grad, sent = call(
         functools.partial(decode_kernel, scale),
-        (shape(tile_shape, BF16), shape(tile_shape, BF16), shape(latent_shape, BF16)),
-        [VMEM] * 12,
+        (
+            shape(tile_shape, BF16),
+            shape(tile_shape, F32),
+            shape(tile_shape, BF16),
+            shape(latent_shape, BF16),
+        ),
+        [VMEM] * 13,
         [pltpu.VMEM((3, frames + 2, 3 * rows, latents, columns), BF16)],
     )(
         low, mid, high, own, combo, wide_t, wide, mine, theirs, proj_out, proj_t,
-        encoded,
+        taps_out, tile,
     )
 
     arrived = lax.all_to_all(sent, ("chan", "pipe"), 0, 0)

time: 141 us -> 138 us (0.979)
  blocking collectives: 101 us -> 99.3 us
    ppermute x1, waiting for transfers between devices: 2.39 us -> 0.67 us  [on_device(): theirs = lax.ppermute(mine, 'chan', [(i, i ^ 1) for i in range(peers)])]
    ppermute x2, waiting for transfers between devices: 11.8 us -> 13.3 us  [both_ways(): lax.ppermute(high_side, axis, forward)]
    pallas_call x1, Pallas kernels: 2.89 us -> 1.35 us  [on_device(): call(prepare_kernel, (shape(tile.shape, BF16), shape((part, columns), BF1...]
where the time goes in v6:
time: 138 us
  blocking collectives  99.3 us (72%)
  waiting for transfers between devices  14 us (10%)
  starting transfers between devices  13.9 us (10%)
  Pallas kernels  7.41 us (5%)
  local copies, waits for them, and re-layouts  2.27 us (2%)
    all_to_all x1, blocking collectives, on_device(): pieces = lax.all_to_all(partial, 'slab', 0, 0, axis_index_groups=groups)  51.5 us
    all_to_all x2, blocking collectives, on_device(): arrived = lax.all_to_all(sent, ('chan', 'pipe'), 0, 0)  22.4 us
    all_to_all x1, blocking collectives, on_device(): mine = lax.all_to_all(sent, 'chan', 0, 0, axis_index_groups=groups)  14.5 us
    ppermute x2, waiting for transfers between devices, both_ways(): lax.ppermute(high_side, axis, forward)  13.3 us
    all_to_all x1, blocking collectives, on_device(): pieces = lax.all_to_all(sent, 'slab', 0, 0, axis_index_groups=groups)  11 us
    ppermute x2, starting transfers between devices, both_ways(): lax.ppermute(low_side, axis, backward)  6.2 us
    ppermute x2, starting transfers between devices, both_ways(): lax.ppermute(high_side, axis, forward)  5.75 us
  transfers between devices with their start and end apart: 5, of which 3 were waited for; matrix products, arithmetic and copies ran while one was open for 0% of the time, Pallas kernels for 2%

profile of v6, /device:TPU:64, one launch (start us, length us, event | category | flops | bytes accessed | tf_op | source)
XLA Modules:
  0.0 137.7 jit_solution(17847375270683540189)
XLA Ops:
  0.6 0.0 copy-start
  0.6 2.3 %collective-permute-start.1 = (bf16[3,2,32,128]{3,2,1,0:T(8,128)(2,1)}, bf16[3,2,32,128]{3,2,1,0:T(8,128)(2,1)S(1)}, u32[]{:S(2)}, u32[]{:S(2)}) collective-permute-start(bf16[3,2,32,128]{3,2,1,0:T(8,128)(2,1)} %bitcast.22), channel_id=1, source_target_pairs={{32,0},{64,32},{96,64},{128,96},{160,128},{192,160},{224,192},{256... | collective-permute-start | bytes 147464 | tf_op jit(solution)/shard_map/ppermute | solution.py:456
  2.9 3.8 %collective-permute-start = (bf16[3,2,32,128]{3,2,1,0:T(8,128)(2,1)}, bf16[3,2,32,128]{3,2,1,0:T(8,128)(2,1)S(1)}, u32[]{:S(2)}, u32[]{:S(2)}) collective-permute-start(bf16[3,2,32,128]{3,2,1,0:T(8,128)(2,1)} %bitcast.23), channel_id=1, source_target_pairs={{0,32},{32,64},{64,96},{96,128},{128,160},{160,192},{192,224},{224... | collective-permute-start | bytes 147464 | tf_op jit(solution)/shard_map/ppermute | solution.py:456
  6.8 0.0 copy-start.1
  6.8 0.8 copy-done.1
  7.6 0.0 copy-start.3
  7.6 0.7 copy-done.3
  8.3 0.0 copy-start.5
  8.3 0.7 copy-done.5
  9.0 0.0 copy-start.4
  9.0 1.3 shard_map.59
  10.3 0.0 collective-permute-done.1.high
  10.3 9.5 %collective-permute-done.low = bf16[3,2,32,128]{3,2,1,0:T(8,128)(2,1)S(1)} collective-permute-done((bf16[3,2,32,128]{3,2,1,0:T(8,128)(2,1)}, bf16[3,2,32,128]{3,2,1,0:T(8,128)(2,1)S(1)}, u32[]{:S(2)}, u32[]{:S(2)}) %collective-permute-start) | collective-permute-done | bytes 49184 | tf_op jit(solution)/shard_map/ppermute | solution.py:456
  19.9 0.1 shard_map.60
  20.0 14.5 %all_to_all.25.after.mine = bf16[8,416,128]{2,1,0:T(8,128)(2,1)S(1)} all-to-all(bf16[8,416,128]{2,1,0:T(8,128)(2,1)S(1)} %get-tuple-element.19), channel_id=1, replica_groups={{0,4,8,12,16,20,24,28},{2,6,10,14,18,22,26,30},{1,5,9,13,17,21,25,29},{..., dimensions={0} | all-to-all | bytes 1703936 | tf_op jit(solution)/shard_map/all_to_all | solution.py:493
  34.4 1.9 %collective-permute-start.2 = (bf16[8,416,128]{2,1,0:T(8,128)(2,1)S(1)}, bf16[8,416,128]{2,1,0:T(8,128)(2,1)S(1)}, u32[]{:S(2)}, u32[]{:S(2)}) collective-permute-start(bf16[8,416,128]{2,1,0:T(8,128)(2,1)S(1)} %all_to_all.25.after.mine), channel_id=1, source_target_pairs={{0,2},{2,0},{4,6},{6,4},{8,10},{10,8},{12,14},{14,12},{16,18},{18,... | collective-permute-start | bytes 2555912 | tf_op jit(solution)/shard_map/ppermute | solution.py:494
  36.4 1.7 %shard_map.61.taps_out = bf16[288,512]{1,0:T(8,128)(2,1)S(1)} custom-call(bf16[8,416,128]{2,1,0:T(8,128)(2,1)S(1)} %all_to_all.25.after.mine, bf16[9,512,512]{2,1,0:T(8,128)(2,1)} %bitcast.16), custom_call_target="tpu_custom_call" | custom-call | tf_op jit(solution)/shard_map/pallas_call | solution.py:496
  38.0 0.0 copy-start.2
  38.0 0.7 collective-permute-done.2.theirs
  38.7 0.0 copy-done
  38.7 0.0 copy-done.4
  38.7 1.0 shard_map.62
  39.8 10.6 %all_to_all.26 = bf16[32,8,128]{2,1,0:T(8,128)(2,1)S(1)} all-to-all(bf16[32,8,128]{2,1,0:T(8,128)(2,1)S(1)} %get-tuple-element.20), channel_id=1, replica_groups=mesh['slab'=32,'chan'=16,'pipe'=2] {'chan','pipe'}, dimensions={0} | all-to-all | bytes 131072 | tf_op jit(solution)/shard_map/all_to_all | solution.py:517
  50.4 3.9 %collective-permute-start.4 = (bf16[3,2,16,128]{3,2,1,0:T(8,128)(2,1)S(1)}, bf16[3,2,16,128]{3,2,1,0:T(8,128)(2,1)S(1)}, u32[]{:S(2)}, u32[]{:S(2)}) collective-permute-start(bf16[3,2,16,128]{3,2,1,0:T(8,128)(2,1)S(1)} %bitcast.18), channel_id=1, source_target_pairs={{32,0},{64,32},{96,64},{128,96},{160,128},{192,160},{224,192},{256... | collective-permute-start | bytes 73736 | tf_op jit(solution)/shard_map/ppermute | solution.py:456
  54.3 1.9 %collective-permute-start.3 = (bf16[3,2,16,128]{3,2,1,0:T(8,128)(2,1)S(1)}, bf16[3,2,16,128]{3,2,1,0:T(8,128)(2,1)S(1)}, u32[]{:S(2)}, u32[]{:S(2)}) collective-permute-start(bf16[3,2,16,128]{3,2,1,0:T(8,128)(2,1)S(1)} %bitcast.19), channel_id=1, source_target_pairs={{0,32},{32,64},{64,96},{96,128},{128,160},{160,192},{192,224},{224... | collective-permute-start | bytes 73736 | tf_op jit(solution)/shard_map/ppermute | solution.py:456
  56.3 0.0 collective-permute-done.4.high
  56.3 3.8 %collective-permute-done.3.low = bf16[3,2,16,128]{3,2,1,0:T(8,128)(2,1)S(1)} collective-permute-done((bf16[3,2,16,128]{3,2,1,0:T(8,128)(2,1)S(1)}, bf16[3,2,16,128]{3,2,1,0:T(8,128)(2,1)S(1)}, u32[]{:S(2)}, u32[]{:S(2)}) %collective-permute-start.3) | collective-permute-done | bytes 24608 | tf_op jit(solution)/shard_map/ppermute | solution.py:456
  60.1 0.0 copy-done.2
  60.1 1.4 shard_map.63
  61.4 11.7 %all_to_all.27.arrived = bf16[32,8,128]{2,1,0:T(8,128)(2,1)S(1)} all-to-all(bf16[32,8,128]{2,1,0:T(8,128)(2,1)S(1)} %get-tuple-element.27), channel_id=1, replica_groups=mesh['slab'=32,'chan'=16,'pipe'=2] {'chan','pipe'}, dimensions={0} | all-to-all | bytes 131072 | tf_op jit(solution)/shard_map/all_to_all | solution.py:536
  73.1 1.2 shard_map.64
  74.4 11.0 %all_to_all.28 = bf16[4,8,36,128]{3,1,2,0:T(8,128)(2,1)S(1)} all-to-all(bf16[4,8,36,128]{3,1,2,0:T(8,128)(2,1)S(1)} %copy.10), channel_id=1, replica_groups={{0,32,64,96},{128,160,192,224},{256,288,320,352},{384,416,448,480},{512..., dimensions={0} | all-to-all | bytes 589824 | tf_op jit(solution)/shard_map/all_to_all | solution.py:544
  85.5 51.5 %all_to_all.29.pieces = bf16[8,36,128]{2,1,0:T(8,128)(2,1)S(1)} all-to-all(bf16[8,36,128]{2,1,0:T(8,128)(2,1)S(1)} %copy.11), channel_id=1, replica_groups={{0,128,256,384,512,640,768,896},{32,160,288,416,544,672,800,928},{64,19..., dimensions={0} | all-to-all | bytes 147456 | tf_op jit(solution)/shard_map/all_to_all | solution.py:547
  136.9 0.7 shard_map.65
  (4 shorter events, 0.1 us)
Async XLA Ops:
  0.6 38.1 %copy-start = (bf16[1,512,9,512]{3,1,2,0:T(8,128)(2,1)S(1)}, bf16[1,512,9,512]{3,1,2,0:T(8,128)(2,1)}, u32[]{:S(2)}) copy-start(bf16[1,512,9,512]{3,1,2,0:T(8,128)(2,1)} %param.6) | copy-start | bytes 14155780
  0.6 9.7 %collective-permute-start.1 = (bf16[3,2,32,128]{3,2,1,0:T(8,128)(2,1)}, bf16[3,2,32,128]{3,2,1,0:T(8,128)(2,1)S(1)}, u32[]{:S(2)}, u32[]{:S(2)}) collective-permute-start(bf16[3,2,32,128]{3,2,1,0:T(8,128)(2,1)} %bitcast.22), channel_id=1, source_target_pairs={{32,0},{64,32},{96,64},{128,96},{160,128},{192,160},{224,192},{256... | collective-permute-start | bytes 147464 | tf_op jit(solution)/shard_map/ppermute | solution.py:456
  2.9 16.9 %collective-permute-start = (bf16[3,2,32,128]{3,2,1,0:T(8,128)(2,1)}, bf16[3,2,32,128]{3,2,1,0:T(8,128)(2,1)S(1)}, u32[]{:S(2)}, u32[]{:S(2)}) collective-permute-start(bf16[3,2,32,128]{3,2,1,0:T(8,128)(2,1)} %bitcast.23), channel_id=1, source_target_pairs={{0,32},{32,64},{64,96},{96,128},{128,160},{160,192},{192,224},{224... | collective-permute-start | bytes 147464 | tf_op jit(solution)/shard_map/ppermute | solution.py:456
  6.8 0.8 copy-start.1
  7.6 0.7 copy-start.3
  8.3 0.7 copy-start.5
  9.0 29.7 %copy-start.4 = (bf16[1,512,16]{1,2,0:T(8,128)(2,1)S(1)}, bf16[1,512,16]{1,2,0:T(8,128)(2,1)}, u32[]{:S(2)}) copy-start(bf16[1,512,16]{1,2,0:T(8,128)(2,1)} %param.7) | copy-start | bytes 49156
  34.4 4.3 %collective-permute-start.2 = (bf16[8,416,128]{2,1,0:T(8,128)(2,1)S(1)}, bf16[8,416,128]{2,1,0:T(8,128)(2,1)S(1)}, u32[]{:S(2)}, u32[]{:S(2)}) collective-permute-start(bf16[8,416,128]{2,1,0:T(8,128)(2,1)S(1)} %all_to_all.25.after.mine), channel_id=1, source_target_pairs={{0,2},{2,0},{4,6},{6,4},{8,10},{10,8},{12,14},{14,12},{16,18},{18,... | collective-permute-start | bytes 2555912 | tf_op jit(solution)/shard_map/ppermute | solution.py:494
  38.0 22.0 %copy-start.2 = (bf16[1,3,2,32,128]{4,3,2,1,0:T(8,128)(2,1)S(1)}, bf16[1,3,2,32,128]{4,3,2,1,0:T(8,128)(2,1)}, u32[]{:S(2)}) copy-start(bf16[1,3,2,32,128]{4,3,2,1,0:T(8,128)(2,1)} %param.4) | copy-start | bytes 147460
  50.4 5.9 %collective-permute-start.4 = (bf16[3,2,16,128]{3,2,1,0:T(8,128)(2,1)S(1)}, bf16[3,2,16,128]{3,2,1,0:T(8,128)(2,1)S(1)}, u32[]{:S(2)}, u32[]{:S(2)}) collective-permute-start(bf16[3,2,16,128]{3,2,1,0:T(8,128)(2,1)S(1)} %bitcast.18), channel_id=1, source_target_pairs={{32,0},{64,32},{96,64},{128,96},{160,128},{192,160},{224,192},{256... | collective-permute-start | bytes 73736 | tf_op jit(solution)/shard_map/ppermute | solution.py:456
  54.3 5.7 %collective-permute-start.3 = (bf16[3,2,16,128]{3,2,1,0:T(8,128)(2,1)S(1)}, bf16[3,2,16,128]{3,2,1,0:T(8,128)(2,1)S(1)}, u32[]{:S(2)}, u32[]{:S(2)}) collective-permute-start(bf16[3,2,16,128]{3,2,1,0:T(8,128)(2,1)S(1)} %bitcast.19), channel_id=1, source_target_pairs={{0,32},{32,64},{64,96},{96,128},{128,160},{160,192},{192,224},{224... | collective-permute-start | bytes 73736 | tf_op jit(solution)/shard_map/ppermute | solution.py:456

commit v7 on v6

--- a/solution.py
+++ b/solution.py
@@ -33,7 +33,7 @@
 
 
 def logistic(summed):
-    return 1.0 / (1.0 + jnp.exp(-summed))
+    return 0.5 + 0.5 * jnp.tanh(0.5 * summed)
 
 
 def tap_blocks(rows, outs):

time: 138 us -> 138 us (level)
  no operation moved by 1% of the time
where the time goes in v7:
time: 138 us
  blocking collectives  99.2 us (72%)
  waiting for transfers between devices  14 us (10%)
  starting transfers between devices  13.9 us (10%)
  Pallas kernels  7.39 us (5%)
  local copies, waits for them, and re-layouts  2.27 us (2%)
    all_to_all x1, blocking collectives, on_device(): pieces = lax.all_to_all(partial, 'slab', 0, 0, axis_index_groups=groups)  51.5 us
    all_to_all x2, blocking collectives, on_device(): arrived = lax.all_to_all(sent, ('chan', 'pipe'), 0, 0)  22.3 us
    all_to_all x1, blocking collectives, on_device(): mine = lax.all_to_all(sent, 'chan', 0, 0, axis_index_groups=groups)  14.5 us
    ppermute x2, waiting for transfers between devices, both_ways(): lax.ppermute(high_side, axis, forward)  13.3 us
    all_to_all x1, blocking collectives, on_device(): pieces = lax.all_to_all(sent, 'slab', 0, 0, axis_index_groups=groups)  11 us
    ppermute x2, starting transfers between devices, both_ways(): lax.ppermute(low_side, axis, backward)  6.2 us
    ppermute x2, starting transfers between devices, both_ways(): lax.ppermute(high_side, axis, forward)  5.75 us
  transfers between devices with their start and end apart: 5, of which 3 were waited for; matrix products, arithmetic and copies ran while one was open for 0% of the time, Pallas kernels for 2%

profile of v7, /device:TPU:64, one launch (start us, length us, event | category | flops | bytes accessed | tf_op | source)
XLA Modules:
  0.0 137.6 jit_solution(4333410744511309035)
XLA Ops:
  0.6 0.0 copy-start
  0.6 2.3 %collective-permute-start.1 = (bf16[3,2,32,128]{3,2,1,0:T(8,128)(2,1)}, bf16[3,2,32,128]{3,2,1,0:T(8,128)(2,1)S(1)}, u32[]{:S(2)}, u32[]{:S(2)}) collective-permute-start(bf16[3,2,32,128]{3,2,1,0:T(8,128)(2,1)} %bitcast.22), channel_id=1, source_target_pairs={{32,0},{64,32},{96,64},{128,96},{160,128},{192,160},{224,192},{256... | collective-permute-start | bytes 147464 | tf_op jit(solution)/shard_map/ppermute | solution.py:456
  2.9 3.8 %collective-permute-start = (bf16[3,2,32,128]{3,2,1,0:T(8,128)(2,1)}, bf16[3,2,32,128]{3,2,1,0:T(8,128)(2,1)S(1)}, u32[]{:S(2)}, u32[]{:S(2)}) collective-permute-start(bf16[3,2,32,128]{3,2,1,0:T(8,128)(2,1)} %bitcast.23), channel_id=1, source_target_pairs={{0,32},{32,64},{64,96},{96,128},{128,160},{160,192},{192,224},{224... | collective-permute-start | bytes 147464 | tf_op jit(solution)/shard_map/ppermute | solution.py:456
  6.8 0.0 copy-start.1
  6.8 0.8 copy-done.1
  7.6 0.0 copy-start.3
  7.6 0.7 copy-done.3
  8.3 0.0 copy-start.5
  8.3 0.7 copy-done.5
  9.0 0.0 copy-start.4
  9.0 1.3 shard_map.59
  10.3 0.0 collective-permute-done.1.high
  10.3 9.5 %collective-permute-done.low = bf16[3,2,32,128]{3,2,1,0:T(8,128)(2,1)S(1)} collective-permute-done((bf16[3,2,32,128]{3,2,1,0:T(8,128)(2,1)}, bf16[3,2,32,128]{3,2,1,0:T(8,128)(2,1)S(1)}, u32[]{:S(2)}, u32[]{:S(2)}) %collective-permute-start) | collective-permute-done | bytes 49184 | tf_op jit(solution)/shard_map/ppermute | solution.py:456
  19.9 0.1 shard_map.60
  20.0 14.5 %all_to_all.25.after.mine = bf16[8,416,128]{2,1,0:T(8,128)(2,1)S(1)} all-to-all(bf16[8,416,128]{2,1,0:T(8,128)(2,1)S(1)} %get-tuple-element.19), channel_id=1, replica_groups={{0,4,8,12,16,20,24,28},{2,6,10,14,18,22,26,30},{1,5,9,13,17,21,25,29},{..., dimensions={0} | all-to-all | bytes 1703936 | tf_op jit(solution)/shard_map/all_to_all | solution.py:493
  34.4 1.9 %collective-permute-start.2 = (bf16[8,416,128]{2,1,0:T(8,128)(2,1)S(1)}, bf16[8,416,128]{2,1,0:T(8,128)(2,1)S(1)}, u32[]{:S(2)}, u32[]{:S(2)}) collective-permute-start(bf16[8,416,128]{2,1,0:T(8,128)(2,1)S(1)} %all_to_all.25.after.mine), channel_id=1, source_target_pairs={{0,2},{2,0},{4,6},{6,4},{8,10},{10,8},{12,14},{14,12},{16,18},{18,... | collective-permute-start | bytes 2555912 | tf_op jit(solution)/shard_map/ppermute | solution.py:494
  36.4 1.7 %shard_map.61.taps_out = bf16[288,512]{1,0:T(8,128)(2,1)S(1)} custom-call(bf16[8,416,128]{2,1,0:T(8,128)(2,1)S(1)} %all_to_all.25.after.mine, bf16[9,512,512]{2,1,0:T(8,128)(2,1)} %bitcast.16), custom_call_target="tpu_custom_call" | custom-call | tf_op jit(solution)/shard_map/pallas_call | solution.py:496
  38.0 0.0 copy-start.2
  38.0 0.7 collective-permute-done.2.theirs
  38.7 0.0 copy-done
  38.7 0.0 copy-done.4
  38.7 1.0 shard_map.62
  39.7 10.6 %all_to_all.26 = bf16[32,8,128]{2,1,0:T(8,128)(2,1)S(1)} all-to-all(bf16[32,8,128]{2,1,0:T(8,128)(2,1)S(1)} %get-tuple-element.20), channel_id=1, replica_groups=mesh['slab'=32,'chan'=16,'pipe'=2] {'chan','pipe'}, dimensions={0} | all-to-all | bytes 131072 | tf_op jit(solution)/shard_map/all_to_all | solution.py:517
  50.4 3.9 %collective-permute-start.4 = (bf16[3,2,16,128]{3,2,1,0:T(8,128)(2,1)S(1)}, bf16[3,2,16,128]{3,2,1,0:T(8,128)(2,1)S(1)}, u32[]{:S(2)}, u32[]{:S(2)}) collective-permute-start(bf16[3,2,16,128]{3,2,1,0:T(8,128)(2,1)S(1)} %bitcast.18), channel_id=1, source_target_pairs={{32,0},{64,32},{96,64},{128,96},{160,128},{192,160},{224,192},{256... | collective-permute-start | bytes 73736 | tf_op jit(solution)/shard_map/ppermute | solution.py:456
  54.3 1.9 %collective-permute-start.3 = (bf16[3,2,16,128]{3,2,1,0:T(8,128)(2,1)S(1)}, bf16[3,2,16,128]{3,2,1,0:T(8,128)(2,1)S(1)}, u32[]{:S(2)}, u32[]{:S(2)}) collective-permute-start(bf16[3,2,16,128]{3,2,1,0:T(8,128)(2,1)S(1)} %bitcast.19), channel_id=1, source_target_pairs={{0,32},{32,64},{64,96},{96,128},{128,160},{160,192},{192,224},{224... | collective-permute-start | bytes 73736 | tf_op jit(solution)/shard_map/ppermute | solution.py:456
  56.2 0.0 collective-permute-done.4.high
  56.3 3.8 %collective-permute-done.3.low = bf16[3,2,16,128]{3,2,1,0:T(8,128)(2,1)S(1)} collective-permute-done((bf16[3,2,16,128]{3,2,1,0:T(8,128)(2,1)S(1)}, bf16[3,2,16,128]{3,2,1,0:T(8,128)(2,1)S(1)}, u32[]{:S(2)}, u32[]{:S(2)}) %collective-permute-start.3) | collective-permute-done | bytes 24608 | tf_op jit(solution)/shard_map/ppermute | solution.py:456
  60.0 0.0 copy-done.2
  60.0 1.4 shard_map.63
  61.4 11.7 %all_to_all.27.arrived = bf16[32,8,128]{2,1,0:T(8,128)(2,1)S(1)} all-to-all(bf16[32,8,128]{2,1,0:T(8,128)(2,1)S(1)} %get-tuple-element.27), channel_id=1, replica_groups=mesh['slab'=32,'chan'=16,'pipe'=2] {'chan','pipe'}, dimensions={0} | all-to-all | bytes 131072 | tf_op jit(solution)/shard_map/all_to_all | solution.py:536
  73.1 1.2 shard_map.64
  74.3 11.0 %all_to_all.28 = bf16[4,8,36,128]{3,1,2,0:T(8,128)(2,1)S(1)} all-to-all(bf16[4,8,36,128]{3,1,2,0:T(8,128)(2,1)S(1)} %copy.10), channel_id=1, replica_groups={{0,32,64,96},{128,160,192,224},{256,288,320,352},{384,416,448,480},{512..., dimensions={0} | all-to-all | bytes 589824 | tf_op jit(solution)/shard_map/all_to_all | solution.py:544
  85.4 51.5 %all_to_all.29.pieces = bf16[8,36,128]{2,1,0:T(8,128)(2,1)S(1)} all-to-all(bf16[8,36,128]{2,1,0:T(8,128)(2,1)S(1)} %copy.11), channel_id=1, replica_groups={{0,128,256,384,512,640,768,896},{32,160,288,416,544,672,800,928},{64,19..., dimensions={0} | all-to-all | bytes 147456 | tf_op jit(solution)/shard_map/all_to_all | solution.py:547
  136.8 0.7 shard_map.65
  (4 shorter events, 0.1 us)
Async XLA Ops:
  0.6 38.1 %copy-start = (bf16[1,512,9,512]{3,1,2,0:T(8,128)(2,1)S(1)}, bf16[1,512,9,512]{3,1,2,0:T(8,128)(2,1)}, u32[]{:S(2)}) copy-start(bf16[1,512,9,512]{3,1,2,0:T(8,128)(2,1)} %param.6) | copy-start | bytes 14155780
  0.6 9.7 %collective-permute-start.1 = (bf16[3,2,32,128]{3,2,1,0:T(8,128)(2,1)}, bf16[3,2,32,128]{3,2,1,0:T(8,128)(2,1)S(1)}, u32[]{:S(2)}, u32[]{:S(2)}) collective-permute-start(bf16[3,2,32,128]{3,2,1,0:T(8,128)(2,1)} %bitcast.22), channel_id=1, source_target_pairs={{32,0},{64,32},{96,64},{128,96},{160,128},{192,160},{224,192},{256... | collective-permute-start | bytes 147464 | tf_op jit(solution)/shard_map/ppermute | solution.py:456
  2.9 16.9 %collective-permute-start = (bf16[3,2,32,128]{3,2,1,0:T(8,128)(2,1)}, bf16[3,2,32,128]{3,2,1,0:T(8,128)(2,1)S(1)}, u32[]{:S(2)}, u32[]{:S(2)}) collective-permute-start(bf16[3,2,32,128]{3,2,1,0:T(8,128)(2,1)} %bitcast.23), channel_id=1, source_target_pairs={{0,32},{32,64},{64,96},{96,128},{128,160},{160,192},{192,224},{224... | collective-permute-start | bytes 147464 | tf_op jit(solution)/shard_map/ppermute | solution.py:456
  6.8 0.8 copy-start.1
  7.6 0.7 copy-start.3
  8.3 0.7 copy-start.5
  9.0 29.7 %copy-start.4 = (bf16[1,512,16]{1,2,0:T(8,128)(2,1)S(1)}, bf16[1,512,16]{1,2,0:T(8,128)(2,1)}, u32[]{:S(2)}) copy-start(bf16[1,512,16]{1,2,0:T(8,128)(2,1)} %param.7) | copy-start | bytes 49156
  34.4 4.3 %collective-permute-start.2 = (bf16[8,416,128]{2,1,0:T(8,128)(2,1)S(1)}, bf16[8,416,128]{2,1,0:T(8,128)(2,1)S(1)}, u32[]{:S(2)}, u32[]{:S(2)}) collective-permute-start(bf16[8,416,128]{2,1,0:T(8,128)(2,1)S(1)} %all_to_all.25.after.mine), channel_id=1, source_target_pairs={{0,2},{2,0},{4,6},{6,4},{8,10},{10,8},{12,14},{14,12},{16,18},{18,... | collective-permute-start | bytes 2555912 | tf_op jit(solution)/shard_map/ppermute | solution.py:494
  38.0 22.0 %copy-start.2 = (bf16[1,3,2,32,128]{4,3,2,1,0:T(8,128)(2,1)S(1)}, bf16[1,3,2,32,128]{4,3,2,1,0:T(8,128)(2,1)}, u32[]{:S(2)}) copy-start(bf16[1,3,2,32,128]{4,3,2,1,0:T(8,128)(2,1)} %param.4) | copy-start | bytes 147460
  50.4 5.9 %collective-permute-start.4 = (bf16[3,2,16,128]{3,2,1,0:T(8,128)(2,1)S(1)}, bf16[3,2,16,128]{3,2,1,0:T(8,128)(2,1)S(1)}, u32[]{:S(2)}, u32[]{:S(2)}) collective-permute-start(bf16[3,2,16,128]{3,2,1,0:T(8,128)(2,1)S(1)} %bitcast.18), channel_id=1, source_target_pairs={{32,0},{64,32},{96,64},{128,96},{160,128},{192,160},{224,192},{256... | collective-permute-start | bytes 73736 | tf_op jit(solution)/shard_map/ppermute | solution.py:456
  54.3 5.7 %collective-permute-start.3 = (bf16[3,2,16,128]{3,2,1,0:T(8,128)(2,1)S(1)}, bf16[3,2,16,128]{3,2,1,0:T(8,128)(2,1)S(1)}, u32[]{:S(2)}, u32[]{:S(2)}) collective-permute-start(bf16[3,2,16,128]{3,2,1,0:T(8,128)(2,1)S(1)} %bitcast.19), channel_id=1, source_target_pairs={{0,32},{32,64},{64,96},{96,128},{128,160},{160,192},{192,224},{224... | collective-permute-start | bytes 73736 | tf_op jit(solution)/shard_map/ppermute | solution.py:456

commit v8 on v6

--- a/solution.py
+++ b/solution.py
@@ -88,9 +88,10 @@
     return mixed
 
 
-def prepare_kernel(tile, taps, proj_t, mid, extra, direct, proj_out):
+def prepare_kernel(tile, small, mid, extra, direct, proj_out):
     frames, rows, part, columns = tile.shape
-    latents = proj_t.shape[0]
+    latents = direct.shape[1]
+    proj_t, taps = small[:latents], small[latents:][:3, :part]
     chan = lax.axis_index("chan")
     proj_back = pick(proj_t, chan, part)
     line = lax.broadcasted_iota(jnp.int32, (part, part), 0)
@@ -129,10 +130,11 @@
         taps_out[tap * part : (tap + 1) * part] = chosen
 
 
-def mix_kernel(low, high, taps, mid, extra, direct, sent, own):
+def mix_kernel(low, high, small, mid, extra, direct, sent, own):
     frames, rows, part, columns = mid.shape
     chips = sent.shape[0]
     latents = direct.shape[1]
+    taps = small[latents:][:3, :part]
     weights, _ = mix_weights(taps)
     before = mix_rows([low[frame, rows - 1].astype(F32) for frame in range(frames)], weights)
     after = mix_rows([high[frame, 0].astype(F32) for frame in range(frames)], weights)
@@ -470,6 +472,8 @@
 
     above, below = both_ways(tile, tile, "slab")
     proj_t = proj[0].T
+    wide_taps = jnp.pad(taps[0], ((0, latents - 3), (0, channels - part)))
+    small = jnp.concatenate([proj_t, wide_taps], axis=0)
     height = (frames * (rows + 2) + 1) * part
     middle, extra, direct, proj_out = call(
         prepare_kernel,
@@ -479,8 +483,8 @@
             shape((frames * rows, latents, columns), BF16),
             shape((part, latents), BF16),
         ),
-        [VMEM] * 3,
-    )(tile, taps[0], proj_t)
+        [VMEM] * 2,
+    )(tile, small)
     sent, own = call(
         mix_kernel,
         (
@@ -488,7 +492,7 @@
             shape((frames, rows + 2, part, columns), BF16),
         ),
         [VMEM] * 6,
-    )(above, below, taps[0], middle, extra, direct)
+    )(above, below, small, middle, extra, direct)
     groups = [[2 * chip + core for chip in range(peers // 2)] for core in range(2)]
     mine = lax.all_to_all(sent, "chan", 0, 0, axis_index_groups=groups)
     theirs = lax.ppermute(mine, "chan", [(i, i ^ 1) for i in range(peers)])

time: 138 us -> 137 us (level)
  local copies, waits for them, and re-layouts: 2.27 us -> 0.87 us
    unnamed x12 -> x8, local copies, waits for them, and re-layouts: 2.21 us -> 0.81 us
  transfers between devices with their start and end apart: 5 -> 5, of which waited for: 3 -> 3; matrix products, arithmetic and copies ran while one was open for 0% -> 1% of each run, Pallas kernels for 2% -> 2%
where the time goes in v8:
time: 137 us; the launch traced here: 136 us
  blocking collectives  98.1 us (72%)
  waiting for transfers between devices  15.2 us (11%)
  starting transfers between devices  13.9 us (10%)
  Pallas kernels  6.88 us (5%)
    all_to_all x1, blocking collectives, on_device(): pieces = lax.all_to_all(partial, 'slab', 0, 0, axis_index_groups=groups)  50.3 us
    all_to_all x2, blocking collectives, on_device(): arrived = lax.all_to_all(sent, ('chan', 'pipe'), 0, 0)  22.4 us
    ppermute x2, waiting for transfers between devices, both_ways(): lax.ppermute(high_side, axis, forward)  14.5 us
    all_to_all x1, blocking collectives, on_device(): mine = lax.all_to_all(sent, 'chan', 0, 0, axis_index_groups=groups)  14.5 us
    all_to_all x1, blocking collectives, on_device(): pieces = lax.all_to_all(sent, 'slab', 0, 0, axis_index_groups=groups)  11 us
    ppermute x2, starting transfers between devices, both_ways(): lax.ppermute(low_side, axis, backward)  6.19 us
    ppermute x2, starting transfers between devices, both_ways(): lax.ppermute(high_side, axis, forward)  5.75 us
  transfers between devices with their start and end apart: 5, of which 3 were waited for; matrix products, arithmetic and copies ran while one was open for 1% of the time, Pallas kernels for 2%

profile of v8, /device:TPU:64, one launch (start us, length us, event | category | flops | bytes accessed | tf_op | source)
XLA Modules:
  0.0 136.4 jit_solution(2300786524809217850)
XLA Ops:
  0.6 0.0 copy-start
  0.6 2.3 %collective-permute-start.1 = (bf16[3,2,32,128]{3,2,1,0:T(8,128)(2,1)}, bf16[3,2,32,128]{3,2,1,0:T(8,128)(2,1)S(1)}, u32[]{:S(2)}, u32[]{:S(2)}) collective-permute-start(bf16[3,2,32,128]{3,2,1,0:T(8,128)(2,1)} %bitcast.22), channel_id=1, source_target_pairs={{32,0},{64,32},{96,64},{128,96},{160,128},{192,160},{224,192},{256... | collective-permute-start | bytes 147464 | tf_op jit(solution)/shard_map/ppermute | solution.py:458
  2.9 3.8 %collective-permute-start = (bf16[3,2,32,128]{3,2,1,0:T(8,128)(2,1)}, bf16[3,2,32,128]{3,2,1,0:T(8,128)(2,1)S(1)}, u32[]{:S(2)}, u32[]{:S(2)}) collective-permute-start(bf16[3,2,32,128]{3,2,1,0:T(8,128)(2,1)} %bitcast.23), channel_id=1, source_target_pairs={{0,32},{32,64},{64,96},{96,128},{128,160},{160,192},{192,224},{224... | collective-permute-start | bytes 147464 | tf_op jit(solution)/shard_map/ppermute | solution.py:458
  6.8 0.7 fusion.1.small
  7.5 0.0 copy-start.1
  7.5 0.8 copy-done.1
  8.3 0.0 copy-start.3
  8.3 0.8 shard_map.59
  9.1 0.0 collective-permute-done.1.high
  9.1 10.7 %collective-permute-done.low = bf16[3,2,32,128]{3,2,1,0:T(8,128)(2,1)S(1)} collective-permute-done((bf16[3,2,32,128]{3,2,1,0:T(8,128)(2,1)}, bf16[3,2,32,128]{3,2,1,0:T(8,128)(2,1)S(1)}, u32[]{:S(2)}, u32[]{:S(2)}) %collective-permute-start) | collective-permute-done | bytes 49184 | tf_op jit(solution)/shard_map/ppermute | solution.py:458
  19.9 0.1 shard_map.60
  20.0 14.5 %all_to_all.25.after.mine = bf16[8,416,128]{2,1,0:T(8,128)(2,1)S(1)} all-to-all(bf16[8,416,128]{2,1,0:T(8,128)(2,1)S(1)} %get-tuple-element.19), channel_id=1, replica_groups={{0,4,8,12,16,20,24,28},{2,6,10,14,18,22,26,30},{1,5,9,13,17,21,25,29},{..., dimensions={0} | all-to-all | bytes 1703936 | tf_op jit(solution)/shard_map/all_to_all | solution.py:497
  34.4 1.9 %collective-permute-start.2 = (bf16[8,416,128]{2,1,0:T(8,128)(2,1)S(1)}, bf16[8,416,128]{2,1,0:T(8,128)(2,1)S(1)}, u32[]{:S(2)}, u32[]{:S(2)}) collective-permute-start(bf16[8,416,128]{2,1,0:T(8,128)(2,1)S(1)} %all_to_all.25.after.mine), channel_id=1, source_target_pairs={{0,2},{2,0},{4,6},{6,4},{8,10},{10,8},{12,14},{14,12},{16,18},{18,... | collective-permute-start | bytes 2555912 | tf_op jit(solution)/shard_map/ppermute | solution.py:498
  36.4 1.7 %shard_map.61.taps_out = bf16[288,512]{1,0:T(8,128)(2,1)S(1)} custom-call(bf16[8,416,128]{2,1,0:T(8,128)(2,1)S(1)} %all_to_all.25.after.mine, bf16[9,512,512]{2,1,0:T(8,128)(2,1)} %bitcast.16), custom_call_target="tpu_custom_call" | custom-call | tf_op jit(solution)/shard_map/pallas_call | solution.py:500
  38.0 0.0 copy-start.2
  38.0 0.7 collective-permute-done.2.theirs
  38.7 0.0 copy-done
  38.7 0.0 copy-done.3
  38.7 1.0 shard_map.62
  39.8 10.6 %all_to_all.26 = bf16[32,8,128]{2,1,0:T(8,128)(2,1)S(1)} all-to-all(bf16[32,8,128]{2,1,0:T(8,128)(2,1)S(1)} %get-tuple-element.20), channel_id=1, replica_groups=mesh['slab'=32,'chan'=16,'pipe'=2] {'chan','pipe'}, dimensions={0} | all-to-all | bytes 131072 | tf_op jit(solution)/shard_map/all_to_all | solution.py:521
  50.4 3.9 %collective-permute-start.4 = (bf16[3,2,16,128]{3,2,1,0:T(8,128)(2,1)S(1)}, bf16[3,2,16,128]{3,2,1,0:T(8,128)(2,1)S(1)}, u32[]{:S(2)}, u32[]{:S(2)}) collective-permute-start(bf16[3,2,16,128]{3,2,1,0:T(8,128)(2,1)S(1)} %bitcast.18), channel_id=1, source_target_pairs={{32,0},{64,32},{96,64},{128,96},{160,128},{192,160},{224,192},{256... | collective-permute-start | bytes 73736 | tf_op jit(solution)/shard_map/ppermute | solution.py:458
  54.3 1.9 %collective-permute-start.3 = (bf16[3,2,16,128]{3,2,1,0:T(8,128)(2,1)S(1)}, bf16[3,2,16,128]{3,2,1,0:T(8,128)(2,1)S(1)}, u32[]{:S(2)}, u32[]{:S(2)}) collective-permute-start(bf16[3,2,16,128]{3,2,1,0:T(8,128)(2,1)S(1)} %bitcast.19), channel_id=1, source_target_pairs={{0,32},{32,64},{64,96},{96,128},{128,160},{160,192},{192,224},{224... | collective-permute-start | bytes 73736 | tf_op jit(solution)/shard_map/ppermute | solution.py:458
  56.3 0.0 collective-permute-done.4.high
  56.3 3.8 %collective-permute-done.3.low = bf16[3,2,16,128]{3,2,1,0:T(8,128)(2,1)S(1)} collective-permute-done((bf16[3,2,16,128]{3,2,1,0:T(8,128)(2,1)S(1)}, bf16[3,2,16,128]{3,2,1,0:T(8,128)(2,1)S(1)}, u32[]{:S(2)}, u32[]{:S(2)}) %collective-permute-start.3) | collective-permute-done | bytes 24608 | tf_op jit(solution)/shard_map/ppermute | solution.py:458
  60.1 0.0 copy-done.2
  60.1 1.4 shard_map.63
  61.4 11.7 %all_to_all.27.arrived = bf16[32,8,128]{2,1,0:T(8,128)(2,1)S(1)} all-to-all(bf16[32,8,128]{2,1,0:T(8,128)(2,1)S(1)} %get-tuple-element.27), channel_id=1, replica_groups=mesh['slab'=32,'chan'=16,'pipe'=2] {'chan','pipe'}, dimensions={0} | all-to-all | bytes 131072 | tf_op jit(solution)/shard_map/all_to_all | solution.py:540
  73.1 1.2 shard_map.64
  74.4 11.0 %all_to_all.28 = bf16[4,8,36,128]{3,1,2,0:T(8,128)(2,1)S(1)} all-to-all(bf16[4,8,36,128]{3,1,2,0:T(8,128)(2,1)S(1)} %copy.10), channel_id=1, replica_groups={{0,32,64,96},{128,160,192,224},{256,288,320,352},{384,416,448,480},{512..., dimensions={0} | all-to-all | bytes 589824 | tf_op jit(solution)/shard_map/all_to_all | solution.py:548
  85.5 50.3 %all_to_all.29.pieces = bf16[8,36,128]{2,1,0:T(8,128)(2,1)S(1)} all-to-all(bf16[8,36,128]{2,1,0:T(8,128)(2,1)S(1)} %copy.11), channel_id=1, replica_groups={{0,128,256,384,512,640,768,896},{32,160,288,416,544,672,800,928},{64,19..., dimensions={0} | all-to-all | bytes 147456 | tf_op jit(solution)/shard_map/all_to_all | solution.py:551
  135.7 0.7 shard_map.65
  (4 shorter events, 0.1 us)
Async XLA Ops:
  0.6 38.1 %copy-start = (bf16[1,512,9,512]{3,1,2,0:T(8,128)(2,1)S(1)}, bf16[1,512,9,512]{3,1,2,0:T(8,128)(2,1)}, u32[]{:S(2)}) copy-start(bf16[1,512,9,512]{3,1,2,0:T(8,128)(2,1)} %param.6) | copy-start | bytes 14155780
  0.6 8.5 %collective-permute-start.1 = (bf16[3,2,32,128]{3,2,1,0:T(8,128)(2,1)}, bf16[3,2,32,128]{3,2,1,0:T(8,128)(2,1)S(1)}, u32[]{:S(2)}, u32[]{:S(2)}) collective-permute-start(bf16[3,2,32,128]{3,2,1,0:T(8,128)(2,1)} %bitcast.22), channel_id=1, source_target_pairs={{32,0},{64,32},{96,64},{128,96},{160,128},{192,160},{224,192},{256... | collective-permute-start | bytes 147464 | tf_op jit(solution)/shard_map/ppermute | solution.py:458
  2.9 16.9 %collective-permute-start = (bf16[3,2,32,128]{3,2,1,0:T(8,128)(2,1)}, bf16[3,2,32,128]{3,2,1,0:T(8,128)(2,1)S(1)}, u32[]{:S(2)}, u32[]{:S(2)}) collective-permute-start(bf16[3,2,32,128]{3,2,1,0:T(8,128)(2,1)} %bitcast.23), channel_id=1, source_target_pairs={{0,32},{32,64},{64,96},{96,128},{128,160},{160,192},{192,224},{224... | collective-permute-start | bytes 147464 | tf_op jit(solution)/shard_map/ppermute | solution.py:458
  7.5 0.8 copy-start.1
  8.3 30.4 %copy-start.3 = (bf16[1,512,16]{1,2,0:T(8,128)(2,1)S(1)}, bf16[1,512,16]{1,2,0:T(8,128)(2,1)}, u32[]{:S(2)}) copy-start(bf16[1,512,16]{1,2,0:T(8,128)(2,1)} %param.7) | copy-start | bytes 49156
  34.4 4.3 %collective-permute-start.2 = (bf16[8,416,128]{2,1,0:T(8,128)(2,1)S(1)}, bf16[8,416,128]{2,1,0:T(8,128)(2,1)S(1)}, u32[]{:S(2)}, u32[]{:S(2)}) collective-permute-start(bf16[8,416,128]{2,1,0:T(8,128)(2,1)S(1)} %all_to_all.25.after.mine), channel_id=1, source_target_pairs={{0,2},{2,0},{4,6},{6,4},{8,10},{10,8},{12,14},{14,12},{16,18},{18,... | collective-permute-start | bytes 2555912 | tf_op jit(solution)/shard_map/ppermute | solution.py:498
  38.0 22.0 %copy-start.2 = (bf16[1,3,2,32,128]{4,3,2,1,0:T(8,128)(2,1)S(1)}, bf16[1,3,2,32,128]{4,3,2,1,0:T(8,128)(2,1)}, u32[]{:S(2)}) copy-start(bf16[1,3,2,32,128]{4,3,2,1,0:T(8,128)(2,1)} %param.4) | copy-start | bytes 147460
  50.4 5.9 %collective-permute-start.4 = (bf16[3,2,16,128]{3,2,1,0:T(8,128)(2,1)S(1)}, bf16[3,2,16,128]{3,2,1,0:T(8,128)(2,1)S(1)}, u32[]{:S(2)}, u32[]{:S(2)}) collective-permute-start(bf16[3,2,16,128]{3,2,1,0:T(8,128)(2,1)S(1)} %bitcast.18), channel_id=1, source_target_pairs={{32,0},{64,32},{96,64},{128,96},{160,128},{192,160},{224,192},{256... | collective-permute-start | bytes 73736 | tf_op jit(solution)/shard_map/ppermute | solution.py:458
  54.3 5.7 %collective-permute-start.3 = (bf16[3,2,16,128]{3,2,1,0:T(8,128)(2,1)S(1)}, bf16[3,2,16,128]{3,2,1,0:T(8,128)(2,1)S(1)}, u32[]{:S(2)}, u32[]{:S(2)}) collective-permute-start(bf16[3,2,16,128]{3,2,1,0:T(8,128)(2,1)S(1)} %bitcast.19), channel_id=1, source_target_pairs={{0,32},{32,64},{64,96},{96,128},{128,160},{160,192},{192,224},{224... | collective-permute-start | bytes 73736 | tf_op jit(solution)/shard_map/ppermute | solution.py:458
